TPU v7x, 32 devices: a whole 2x2x4 slice. The times are simulated.
32 devices in a mesh: grp: 2 (over y), dom: 4 (over z), sub: 2 (over x), feat: 2 (over core).
Axes of the slice: x: 2, y: 2, z: 4, core: 2. Of those that a mesh axis runs over, the one named last changes fastest.
Arguments:
- features: bfloat16 [32768, 256], P(('grp', 'dom', 'sub', 'feat')), parts along dimension 0, may hold values from -6 to 6
- labels: int32 [32768], P(('grp', 'dom', 'sub', 'feat')), parts along dimension 0, may hold values from 0 to 127
- local_index: int32 [256, 4], P(('grp', 'dom', 'sub', 'feat')), parts along dimension 0, may hold values from 0 to 7
- local_values: bfloat16 [256, 4, 128, 128], P(('grp', 'dom', 'sub', 'feat')), parts along dimension 0, may hold values from -0.25 to 0.25
- cross_src: int32 [32, 3, 4], P(('grp', 'dom', 'sub', 'feat')), parts along dimension 0, may hold values from 0 to 7, as said below
- cross_dst: int32 [32, 3, 4], P(('grp', 'dom', 'sub', 'feat')), parts along dimension 0, may hold values from 0 to 7
- cross_count: int32 [32, 3], P(('grp', 'dom', 'sub', 'feat')), parts along dimension 0, may hold values from 1 to 4, as said below
- cross_values: bfloat16 [32, 3, 4, 128, 128], P(('grp', 'dom', 'sub', 'feat')), parts along dimension 0, may hold values from -0.25 to 0.25
- w1_self: bfloat16 [256, 256], replicated, may hold values from -0.375 to 0.375
- w1_near: bfloat16 [256, 256], replicated, may hold values from -0.375 to 0.375
- bias_one: float32 [256], replicated, may hold values from -3 to 3
- w2_self: bfloat16 [256, 128], replicated, may hold values from -0.375 to 0.375
- w2_near: bfloat16 [256, 128], replicated, may hold values from -0.375 to 0.375
- bias_two: float32 [128], replicated, may hold values from -3 to 3
Outputs:
- logits: bfloat16 [32768, 128], P(('grp', 'dom', 'sub', 'feat')), parts along dimension 0
- hidden_grad: bfloat16 [32768, 256], P(('grp', 'dom', 'sub', 'feat')), parts along dimension 0
- grad_w1_self: float32 [512, 256], P('grp'), parts along dimension 0
- grad_w1_near: float32 [512, 256], P('grp'), parts along dimension 0
- grad_bias_one: float32 [512], P('grp'), parts along dimension 0
- grad_w2_self: float32 [512, 128], P('grp'), parts along dimension 0
- grad_w2_near: float32 [512, 128], P('grp'), parts along dimension 0
- grad_bias_two: float32 [256], P('grp'), parts along dimension 0
There are 2 independent parts, one for each index of `grp`. A program takes and returns all parts, laid end to end along the dimension named above; an argument that names none is the same for every part. Nothing has to cross between parts.
Inputs may be any that keep to these rules, and one draw needn't show every extreme that they name: `cross_src`: for one partition and one colour round the 4 entries are distinct tiles of the partner. `cross_count`: slots at or beyond the count are unused; the count 4 occurs in every draw.
All inputs are finite; a program needn't handle non-finite values.
Results may differ from a plain program's by a relative error of at most 0.0062.
Values may be sent and summed in bfloat16 or wider, within the bound.
No kernel may reach another device: no remote copies, remote signals or barrier semaphores. Data moves between devices by JAX's collectives and lax.ppermute only.
A program may use at most 64 MiB of HBM per device.

v0:
```python
import jax
import jax.numpy as jnp
from jax import lax
from jax.sharding import PartitionSpec as P


def swapped(value, axis, distance):
    mask = 2**distance
    pairs = [(source, source ^ mask) for source in range(lax.axis_size(axis))]
    return lax.ppermute(value, axis, pairs)


def place_tiles(slot_tiles, slot_targets, tile_count):
    target = (slot_targets[:, None] == jnp.arange(tile_count, dtype=jnp.int32)[None, :]).astype(
        jnp.float32
    )
    return jnp.einsum("bt,biw->tiw", target, slot_tiles, precision=lax.Precision.HIGHEST)


def silu_slope(pre_act):
    sigmoid_pre = jax.nn.sigmoid(pre_act)
    return sigmoid_pre * (1.0 + pre_act * (1.0 - sigmoid_pre))


def shards(
    features,
    labels,
    local_index,
    local_values,
    cross_src,
    cross_dst,
    cross_count,
    cross_values,
    w1_self,
    w1_near,
    bias_one,
    w2_self,
    w2_near,
    bias_two,
):
    row_tiles = local_index.shape[0]
    tile_size = local_values.shape[2]
    rounds_count = cross_src.shape[1]
    slots_count = cross_src.shape[2]
    total_bits = lax.axis_size(("dom", "sub", "feat")).bit_length() - 1
    colour_bits = [total_bits - 1 - colour for colour in range(rounds_count)]
    wanted_src = cross_src[0]
    wanted_dst = cross_dst[0]
    edge_tiles = cross_values[0]
    slot_ids = jnp.arange(slots_count, dtype=jnp.int32)
    active = (slot_ids[None, :] < cross_count[0][:, None]).astype(jnp.float32)
    tile_ids = jnp.arange(row_tiles, dtype=jnp.int32)

    def fetch(blocks, colour):
        partner_blocks = swapped(blocks, ("dom", "sub", "feat"), colour_bits[colour])
        return partner_blocks[wanted_src[colour]]

    def aggregate(blocks):
        near_rows = blocks[local_index]
        summed = jnp.einsum(
            "tkij,tkjw->tiw", local_values, near_rows, preferred_element_type=jnp.float32
        )
        for colour in range(rounds_count):
            arrived = fetch(blocks, colour)
            products = jnp.einsum(
                "bij,bjw->biw", edge_tiles[colour], arrived, preferred_element_type=jnp.float32
            )
            products = products * active[colour][:, None, None]
            summed = summed + place_tiles(products, wanted_dst[colour], row_tiles)
        return summed

    width_in = features.shape[1]
    hidden_width = w1_self.shape[1]
    classes = w2_self.shape[1]
    first_agg = (
        aggregate(features.reshape(row_tiles, tile_size, width_in))
        .reshape(-1, width_in)
        .astype(jnp.bfloat16)
    )
    first_pre = (
        jnp.dot(features, w1_self, preferred_element_type=jnp.float32)
        + jnp.dot(first_agg, w1_near, preferred_element_type=jnp.float32)
        + bias_one
    )
    hidden = jax.nn.silu(first_pre).astype(jnp.bfloat16)
    second_agg = aggregate(hidden.reshape(row_tiles, tile_size, hidden_width)).reshape(
        -1, hidden_width
    )
    second_agg = second_agg.astype(jnp.bfloat16)
    second_pre = (
        jnp.dot(hidden, w2_self, preferred_element_type=jnp.float32)
        + jnp.dot(second_agg, w2_near, preferred_element_type=jnp.float32)
        + bias_two
    )
    logits = second_pre.astype(jnp.bfloat16)
    target = (labels[:, None] == jnp.arange(classes, dtype=jnp.int32)[None, :]).astype(jnp.float32)
    error_rows = (second_pre - target).astype(jnp.bfloat16)
    grad_w2_self = jnp.einsum("nh,nc->hc", hidden, error_rows, preferred_element_type=jnp.float32)
    grad_w2_near = jnp.einsum(
        "nh,nc->hc", second_agg, error_rows, preferred_element_type=jnp.float32
    )
    grad_bias_two = jnp.sum(error_rows.astype(jnp.float32), axis=0)
    agg_grad = jnp.einsum(
        "nc,hc->nh", error_rows, w2_near, preferred_element_type=jnp.float32
    ).astype(jnp.bfloat16)
    self_grad = jnp.einsum("nc,hc->nh", error_rows, w2_self, preferred_element_type=jnp.float32)
    grad_blocks = agg_grad.reshape(row_tiles, tile_size, hidden_width)
    local_terms = jnp.einsum(
        "tkji,tjw->tkiw", local_values, grad_blocks, preferred_element_type=jnp.float32
    )
    owners = (local_index[:, :, None] == tile_ids[None, None, :]).astype(jnp.float32)
    back_sum = jnp.einsum("tks,tkiw->siw", owners, local_terms, precision=lax.Precision.HIGHEST)
    for colour in range(rounds_count):
        rows_back = jnp.einsum(
            "bji,bjw->biw",
            edge_tiles[colour],
            grad_blocks[wanted_dst[colour]],
            preferred_element_type=jnp.float32,
        )
        rows_back = (rows_back * active[colour][:, None, None]).astype(jnp.bfloat16)
        spread = place_tiles(rows_back.astype(jnp.float32), wanted_src[colour], row_tiles).astype(
            jnp.bfloat16
        )
        give_arrived = swapped(spread, ("dom", "sub", "feat"), colour_bits[colour])
        back_sum = back_sum + give_arrived.astype(jnp.float32)
    full_grad = self_grad + back_sum.reshape(-1, hidden_width)
    hidden_grad = full_grad.astype(jnp.bfloat16)
    first_grad = (full_grad * silu_slope(first_pre)).astype(jnp.bfloat16)
    grad_w1_self = jnp.einsum("nf,nh->fh", features, first_grad, preferred_element_type=jnp.float32)
    grad_w1_near = jnp.einsum(
        "nf,nh->fh", first_agg, first_grad, preferred_element_type=jnp.float32
    )
    grad_bias_one = jnp.sum(first_grad.astype(jnp.float32), axis=0)
    summed_all = lax.psum(
        (grad_w1_self, grad_w1_near, grad_bias_one, grad_w2_self, grad_w2_near, grad_bias_two),
        ("dom", "sub", "feat"),
    )
    grad_w1_self, grad_w1_near, grad_bias_one, grad_w2_self, grad_w2_near, grad_bias_two = (
        summed_all
    )
    return (
        logits,
        hidden_grad,
        grad_w1_self,
        grad_w1_near,
        grad_bias_one,
        grad_w2_self,
        grad_w2_near,
        grad_bias_two,
    )


def solution(mesh):
    in_specs = (
        P(("grp", "dom", "sub", "feat"), None),
        P(("grp", "dom", "sub", "feat")),
        P(("grp", "dom", "sub", "feat"), None),
        P(("grp", "dom", "sub", "feat"), None, None, None),
        P(("grp", "dom", "sub", "feat"), None, None),
        P(("grp", "dom", "sub", "feat"), None, None),
        P(("grp", "dom", "sub", "feat"), None),
        P(("grp", "dom", "sub", "feat"), None, None, None, None),
        P(),
        P(),
        P(),
        P(),
        P(),
        P(),
    )
    out_specs = (
        P(("grp", "dom", "sub", "feat"), None),
        P(("grp", "dom", "sub", "feat"), None),
        P("grp", None),
        P("grp", None),
        P("grp"),
        P("grp", None),
        P("grp", None),
        P("grp"),
    )
    return jax.shard_map(shards, mesh=mesh, in_specs=in_specs, out_specs=out_specs, check_vma=False)
```

profile of v0, /device:TPU:0, one launch (start us, length us, event | category | flops | bytes accessed | tf_op | source)
XLA Modules:
  0.0 260.1 jit_solution(5345827762629368313)
XLA Ops:
  7.2 3.0 %collective-permute-start.2 = (bf16[8,128,256]{2,1,0:T(8,128)(2,1)}, bf16[8,128,256]{2,1,0:T(8,128)(2,1)S(1)}, u32[]{:S(2)}, u32[]{:S(2)}) collective-permute-start(bf16[8,128,256]{2,1,0:T(8,128)(2,1)} %bitcast.210), channel_id=1, source_target_pairs={{0,2},{1,3},{2,0},{3,1},{4,6},{5,7},{6,4},{7,5},{8,10},{9,11},{10,... | collective-permute-start | bytes 1572872 | tf_op jit(solution)/shard_map/ppermute | solution.py:10
  10.2 1.6 collective-permute-start.1
  11.8 2.6 collective-permute-start
  17.7 2.4 fusion.114
  22.2 2.0 gather_fusion
  25.3 9.7 %collective-permute-done.1 = bf16[8,128,256]{2,1,0:T(8,128)(2,1)} collective-permute-done((bf16[8,128,256]{2,1,0:T(8,128)(2,1)}, bf16[8,128,256]{2,1,0:T(8,128)(2,1)}, u32[]{:S(2)}, u32[]{:S(2)}) %collective-permute-start.1) | collective-permute-done | bytes 524320 | tf_op jit(solution)/shard_map/ppermute | solution.py:10
  35.1 1.6 gather_fusion.2
  37.4 2.4 gather_fusion.1
  42.1 1.6 fusion.21
  43.7 1.5 fusion.23
  47.4 1.4 multiply_convert_fusion.1
  51.5 2.6 collective-permute-start.3
  54.1 2.0 gather_fusion.4
  57.3 3.7 %collective-permute-done.5 = bf16[8,128,256]{2,1,0:T(8,128)(2,1)S(1)} collective-permute-done((bf16[8,128,256]{2,1,0:T(8,128)(2,1)S(1)}, bf16[8,128,256]{2,1,0:T(8,128)(2,1)S(1)}, u32[]{:S(2)}, u32[]{:S(2)}) %collective-permute-start.5) | collective-permute-done | bytes 524320 | tf_op jit(solution)/shard_map/ppermute | solution.py:10
  61.0 1.4 gather_fusion.7
  64.7 8.5 %collective-permute-done.4 = bf16[8,128,256]{2,1,0:T(8,128)(2,1)} collective-permute-done((bf16[8,128,256]{2,1,0:T(8,128)(2,1)S(1)}, bf16[8,128,256]{2,1,0:T(8,128)(2,1)}, u32[]{:S(2)}, u32[]{:S(2)}) %collective-permute-start.4) | collective-permute-done | bytes 524320 | tf_op jit(solution)/shard_map/ppermute | solution.py:10
  73.2 2.4 gather_fusion.6
  77.8 2.9 %fusion.15 = f32[8,128,256]{2,0,1:T(8,128)} fusion(f32[4,256,128]{1,0,2:T(4,128)} %copy.47, f32[4]{0:T(128)S(1)} %get-tuple-element.37, s32[4]{0:T(128)S(1)} %copy-done.17), kind=kOutput, calls=%fused_computation.39 | convolution fusion | flops 12714016 | bytes 1572896 | tf_op jit(solution)/shard_map/bt,biw->tiw/dot_general | solution.py:17
  80.7 2.9 %fusion.17 = f32[8,128,256]{2,0,1:T(8,128)} fusion(f32[4,256,128]{1,0,2:T(4,128)} %copy.46, f32[4]{0:T(128)S(1)} %get-tuple-element.38, s32[4]{0:T(128)} %get-tuple-element.47), kind=kOutput, calls=%fused_computation.41 | convolution fusion | flops 12714016 | bytes 1572896 | tf_op jit(solution)/shard_map/bt,biw->tiw/dot_general | solution.py:17
  83.6 2.4 gather_fusion.5
  88.3 2.0 fusion.19
  90.3 3.0 %fusion.12 = bf16[8,128,256]{2,1,0:T(8,128)(2,1)S(1)} fusion(bf16[8,4,128,128]{3,2,1,0:T(8,128)(2,1)S(1)} %copy-done, bf16[8,4,128,256]{3,2,1,0:T(8,128)(2,1)} %bitcast.218, f32[8,128,256]{2,0,1:T(8,128)} %fusion.15, f32[8,128,256]{2,0,1:T(8,128)S(1)} %copy-done.3, f32[8,128,256]{2,0,1:T(8,128)S(1)} %fusion.19), kind=kOutput, calls=%fused_computation.24 | convolution fusion | flops 269484032 | bytes 6815744 | tf_op jit(solution)/shard_map/tkij,tkjw->tiw/dot_general | solution.py:60
  93.3 1.5 convert_reduce_fusion.1
  95.2 1.4 gather_fusion.9
  96.5 2.1 fusion.55
  98.6 2.2 copy.52
  100.8 2.3 convolution_convert_fusion.1
  103.1 1.4 gather_fusion.10
  104.5 2.1 fusion.49
  106.5 2.0 copy.53
  108.5 2.2 convolution_convert_fusion
  110.8 1.3 collective-permute-start.8
  112.1 1.4 gather_fusion.8
  113.5 2.0 fusion.61
  115.5 2.1 copy.51
  117.6 2.3 convolution_convert_fusion.2
  119.8 2.4 collective-permute-start.6
  122.2 2.8 %fusion.116 = f32[8,256,4,128]{3,1,2,0:T(8,128)} fusion(bf16[8,128,256,1]{2,1,3,0:T(8,128)(2,1)S(1)} %bitcast.223, bf16[8,4,128,128]{3,2,1,0:T(8,128)(2,1)S(1)} %copy-done), kind=kOutput, calls=%fused_computation.160 | convolution fusion | flops 268435456 | bytes 5767168 | tf_op jit(solution)/shard_map/tkji,tjw->tkiw/dot_general | solution.py:108
  125.0 5.5 %copy.49 = f32[8,256,4,128]{1,0,2,3:T(8,128)} copy(f32[8,256,4,128]{3,1,2,0:T(8,128)} %fusion.116) | data formatting | bytes 8388608 | tf_op jit(solution)/shard_map/tkji,tjw->tkiw/dot_general | solution.py:108
  132.5 11.4 %collective-permute-done.6 = bf16[8,128,256]{2,0,1:T(8,128)(2,1)} collective-permute-done((bf16[8,128,256]{2,0,1:T(8,128)(2,1)}, bf16[8,128,256]{2,0,1:T(8,128)(2,1)}, u32[]{:S(2)}, u32[]{:S(2)}) %collective-permute-start.6) | collective-permute-done | bytes 524320 | tf_op jit(solution)/shard_map/ppermute | solution.py:10
  143.9 6.3 %convert_add_fusion = f32[8,128,256]{2,0,1:T(8,128)S(1)} fusion(bf16[8,128,256]{2,0,1:T(8,128)(2,1)} %collective-permute-done.8, bf16[8,128,256]{2,0,1:T(8,128)(2,1)} %collective-permute-done.7, bf16[8,128,256]{2,0,1:T(8,128)(2,1)} %collective-permute-done.6, f32[8,256,4,128]{1,0,2,3:T(8,128)} %copy.49, s32[8,4]{0,1:T(4,128)S(1)} %copy-done.11), kind=kOutput, calls=%fused_computation.36 | convolution fusion | flops 102236416 | bytes 6815872 | tf_op jit(solution)/shard_map/tks,tkiw->siw/dot_general | solution.py:112
  151.5 1.3 convert_reduce_fusion
  154.9 30.8 %all-reduce = (f32[256]{0:T(256)}, f32[128]{0:T(128)}) all-reduce(f32[256]{0:T(256)S(1)} %get-tuple-element.32, f32[128]{0:T(128)S(1)} %copy-done.26), channel_id=1, replica_groups=mesh['grp'=2,'dom'=4,'sub'=2,'feat'=2] {'dom','sub','feat'}, use_global_device_ids=true, to_apply=%region_3.4 | all-reduce | flops 384 | bytes 3072 | tf_op jit(solution)/shard_map/psum | solution.py:134
  185.7 60.9 %all-reduce.4.cloned.1.call-done = (f32[256,256]{0,1:T(8,128)}, f32[256,256]{1,0:T(8,128)}, f32[256,128]{1,0:T(8,128)}, f32[256,128]{1,0:T(8,128)}) async-done(((f32[256,256]{0,1:T(8,128)}, f32[256,256]{1,0:T(8,128)}, f32[256,128]{1,0:T(8,128)}, f32[256,128]{1,0:T(8,128)}), (f32[256,256]{0,1:T(8,128)}, f32[256,256]{1,0:T(8,128)}, f32[256,128]{1,0:T(8,128)}, ...) | async-done | bytes 786448 | tf_op jit(solution)/shard_map/psum | solution.py:134
  246.6 1.8 copy.39
  248.4 1.7 copy.64
  250.1 1.6 copy.65
  251.7 1.6 copy.66
  (107 shorter events, 27.8 us)
Async XLA Ops:
  7.2 38.9 %copy-start = (bf16[8,4,128,128]{3,2,1,0:T(8,128)(2,1)S(1)}, bf16[8,4,128,128]{3,2,1,0:T(8,128)(2,1)}, u32[]{:S(2)}) copy-start(bf16[8,4,128,128]{3,2,1,0:T(8,128)(2,1)} %param.17) | copy-start | bytes 3145732
  7.2 15.0 %copy-start.1 = (bf16[1024,256]{1,0:T(8,128)(2,1)S(1)}, bf16[1024,256]{1,0:T(8,128)(2,1)}, u32[]{:S(2)}) copy-start(bf16[1024,256]{1,0:T(8,128)(2,1)} %param.14) | copy-start | bytes 1572868
  7.2 239.4 %all-reduce.4.cloned.1.call-start = ((), (), s32[]{:S(2)}) async-start(), calls=%async_computation | async-start | bytes 1572864 | tf_op jit(solution)/shard_map/psum | solution.py:134
  7.2 17.0 %collective-permute-start.2 = (bf16[8,128,256]{2,1,0:T(8,128)(2,1)}, bf16[8,128,256]{2,1,0:T(8,128)(2,1)S(1)}, u32[]{:S(2)}, u32[]{:S(2)}) collective-permute-start(bf16[8,128,256]{2,1,0:T(8,128)(2,1)} %bitcast.210), channel_id=1, source_target_pairs={{0,2},{1,3},{2,0},{3,1},{4,6},{5,7},{6,4},{7,5},{8,10},{9,11},{10,... | collective-permute-start | bytes 1572872 | tf_op jit(solution)/shard_map/ppermute | solution.py:10
  10.2 24.8 %collective-permute-start.1 = (bf16[8,128,256]{2,1,0:T(8,128)(2,1)}, bf16[8,128,256]{2,1,0:T(8,128)(2,1)}, u32[]{:S(2)}, u32[]{:S(2)}) collective-permute-start(bf16[8,128,256]{2,1,0:T(8,128)(2,1)} %bitcast.211), channel_id=1, source_target_pairs={{0,4},{1,5},{2,6},{3,7},{4,0},{5,1},{6,2},{7,3},{8,12},{9,13},{10,... | collective-permute-start | bytes 1572872 | tf_op jit(solution)/shard_map/ppermute | solution.py:10
  11.8 25.6 %collective-permute-start = (bf16[8,128,256]{2,1,0:T(8,128)(2,1)}, bf16[8,128,256]{2,1,0:T(8,128)(2,1)}, u32[]{:S(2)}, u32[]{:S(2)}) collective-permute-start(bf16[8,128,256]{2,1,0:T(8,128)(2,1)} %bitcast.212), channel_id=1, source_target_pairs={{0,8},{1,9},{2,10},{3,11},{4,12},{5,13},{6,14},{7,15},{8,0},{9,1},... | collective-permute-start | bytes 1572872 | tf_op jit(solution)/shard_map/ppermute | solution.py:10
  15.1 9.1 %copy-start.12 = (s32[1024]{0:T(1024)}, s32[1024]{0:T(1024)S(1)}, u32[]{:S(2)}) copy-start(s32[1024]{0:T(1024)S(1)} %pad_clamp_fusion.3) | copy-start | bytes 12292
  21.4 13.7 %copy-start.13 = (s32[1024]{0:T(1024)}, s32[1024]{0:T(1024)S(1)}, u32[]{:S(2)}) copy-start(s32[1024]{0:T(1024)S(1)} %pad_clamp_fusion.4) | copy-start | bytes 12292
  22.2 2.6 %copy-start.4 = (bf16[1,3,4,128,128]{4,3,2,1,0:T(8,128)(2,1)S(1)}, bf16[1,3,4,128,128]{4,3,2,1,0:T(8,128)(2,1)}, u32[]{:S(2)}) copy-start(bf16[1,3,4,128,128]{4,3,2,1,0:T(8,128)(2,1)} %param.21) | copy-start | bytes 1179652
  42.1 3.1 %copy-start.5 = (f32[4,256,128]{1,0,2:T(4,128)S(1)}, f32[4,256,128]{1,0,2:T(4,128)}, u32[]{:S(2)}) copy-start(f32[4,256,128]{1,0,2:T(4,128)} %copy.41) | copy-start | bytes 1572868
  42.1 3.1 %copy-start.15 = (s32[4]{0:T(128)S(1)}, s32[4]{0:T(128)}, u32[]{:S(2)}) copy-start(s32[4]{0:T(128)} %get-tuple-element.45) | copy-start | bytes 52
  42.1 4.0 %copy-start.2 = (bf16[32,128,256]{2,1,0:T(8,128)(2,1)S(1)}, bf16[32,128,256]{2,1,0:T(8,128)(2,1)}, u32[]{:S(2)}) copy-start(bf16[32,128,256]{2,1,0:T(8,128)(2,1)} %gather_fusion) | copy-start | bytes 6291460
  46.1 1.2 copy-start.8
  46.1 1.2 copy-start.27
  46.1 1.2 copy-start.28
  47.3 1.5 copy-start.6
  47.4 2.0 copy-start.14
  47.4 2.5 copy-start.23
  47.4 2.5 copy-start.24
  47.4 3.5 %copy-start.22 = (s32[4]{0:T(128)S(1)}, s32[4]{0:T(128)}, u32[]{:S(2)}) copy-start(s32[4]{0:T(128)} %get-tuple-element.42) | copy-start | bytes 52
  48.8 12.2 %collective-permute-start.5 = (bf16[8,128,256]{2,1,0:T(8,128)(2,1)S(1)}, bf16[8,128,256]{2,1,0:T(8,128)(2,1)S(1)}, u32[]{:S(2)}, u32[]{:S(2)}) collective-permute-start(bf16[8,128,256]{2,1,0:T(8,128)(2,1)S(1)} %bitcast.214), channel_id=1, source_target_pairs={{0,2},{1,3},{2,0},{3,1},{4,6},{5,7},{6,4},{7,5},{8,10},{9,11},{10,... | collective-permute-start | bytes 1572872 | tf_op jit(solution)/shard_map/ppermute | solution.py:10
  50.5 22.7 %collective-permute-start.4 = (bf16[8,128,256]{2,1,0:T(8,128)(2,1)S(1)}, bf16[8,128,256]{2,1,0:T(8,128)(2,1)}, u32[]{:S(2)}, u32[]{:S(2)}) collective-permute-start(bf16[8,128,256]{2,1,0:T(8,128)(2,1)S(1)} %bitcast.215), channel_id=1, source_target_pairs={{0,4},{1,5},{2,6},{3,7},{4,0},{5,1},{6,2},{7,3},{8,12},{9,13},{10,... | collective-permute-start | bytes 1572872 | tf_op jit(solution)/shard_map/ppermute | solution.py:10
  51.5 32.1 %collective-permute-start.3 = (bf16[8,128,256]{2,1,0:T(8,128)(2,1)S(1)}, bf16[8,128,256]{2,1,0:T(8,128)(2,1)}, u32[]{:S(2)}, u32[]{:S(2)}) collective-permute-start(bf16[8,128,256]{2,1,0:T(8,128)(2,1)S(1)} %bitcast.216), channel_id=1, source_target_pairs={{0,8},{1,9},{2,10},{3,11},{4,12},{5,13},{6,14},{7,15},{8,0},{9,1},... | collective-permute-start | bytes 1572872 | tf_op jit(solution)/shard_map/ppermute | solution.py:10
  62.4 15.4 %copy-start.17 = (s32[4]{0:T(128)S(1)}, s32[4]{0:T(128)}, u32[]{:S(2)}) copy-start(s32[4]{0:T(128)} %get-tuple-element.46) | copy-start | bytes 52
  80.7 7.5 %copy-start.16 = (s32[4]{0:T(128)S(1)}, s32[4]{0:T(128)}, u32[]{:S(2)}) copy-start(s32[4]{0:T(128)} %get-tuple-element.45) | copy-start | bytes 52
  88.3 2.0 copy-start.3
  90.2 3.1 %copy-start.9 = (bf16[256,128]{1,0:T(8,128)(2,1)S(1)}, bf16[256,128]{1,0:T(8,128)(2,1)}, u32[]{:S(2)}) copy-start(bf16[256,128]{1,0:T(8,128)(2,1)} %param.26) | copy-start | bytes 196612
  90.2 3.1 %copy-start.18 = (s32[1024]{0:T(1024)S(1)}, s32[1024]{0:T(1024)}, u32[]{:S(2)}) copy-start(s32[1024]{0:T(1024)} %param.15) | copy-start | bytes 12292
  90.3 3.1 %copy-start.25 = (f32[128]{0:T(128)S(1)}, f32[128]{0:T(128)}, u32[]{:S(2)}) copy-start(f32[128]{0:T(128)} %param.27) | copy-start | bytes 1540
  94.9 5.9 %copy-start.21 = (s32[4]{0:T(128)S(1)}, s32[4]{0:T(128)}, u32[]{:S(2)}) copy-start(s32[4]{0:T(128)} %get-tuple-element.40) | copy-start | bytes 52
  98.6 9.9 %copy-start.20 = (s32[4]{0:T(128)S(1)}, s32[4]{0:T(128)}, u32[]{:S(2)}) copy-start(s32[4]{0:T(128)} %get-tuple-element.41) | copy-start | bytes 52
  103.1 29.4 %collective-permute-start.7 = (bf16[8,128,256]{2,0,1:T(8,128)(2,1)}, bf16[8,128,256]{2,0,1:T(8,128)(2,1)}, u32[]{:S(2)}, u32[]{:S(2)}) collective-permute-start(bf16[8,128,256]{2,0,1:T(8,128)(2,1)} %convolution_convert_fusion.1), channel_id=1, source_target_pairs={{0,4},{1,5},{2,6},{3,7},{4,0},{5,1},{6,2},{7,3},{8,12},{9,13},{10,... | collective-permute-start | bytes 1572872 | tf_op jit(solution)/shard_map/ppermute | solution.py:10
  106.5 11.1 %copy-start.19 = (s32[4]{0:T(128)S(1)}, s32[4]{0:T(128)}, u32[]{:S(2)}) copy-start(s32[4]{0:T(128)} %get-tuple-element.39) | copy-start | bytes 52
  110.8 21.7 %collective-permute-start.8 = (bf16[8,128,256]{2,0,1:T(8,128)(2,1)}, bf16[8,128,256]{2,0,1:T(8,128)(2,1)}, u32[]{:S(2)}, u32[]{:S(2)}) collective-permute-start(bf16[8,128,256]{2,0,1:T(8,128)(2,1)} %convolution_convert_fusion), channel_id=1, source_target_pairs={{0,2},{1,3},{2,0},{3,1},{4,6},{5,7},{6,4},{7,5},{8,10},{9,11},{10,... | collective-permute-start | bytes 1572872 | tf_op jit(solution)/shard_map/ppermute | solution.py:10
  119.8 24.1 %collective-permute-start.6 = (bf16[8,128,256]{2,0,1:T(8,128)(2,1)}, bf16[8,128,256]{2,0,1:T(8,128)(2,1)}, u32[]{:S(2)}, u32[]{:S(2)}) collective-permute-start(bf16[8,128,256]{2,0,1:T(8,128)(2,1)} %convolution_convert_fusion.2), channel_id=1, source_target_pairs={{0,8},{1,9},{2,10},{3,11},{4,12},{5,13},{6,14},{7,15},{8,0},{9,1},... | collective-permute-start | bytes 1572872 | tf_op jit(solution)/shard_map/ppermute | solution.py:10
  125.0 18.9 %copy-start.11 = (s32[8,4]{0,1:T(4,128)S(1)}, s32[8,4]{0,1:T(4,128)}, u32[]{:S(2)}) copy-start(s32[8,4]{0,1:T(4,128)} %param.16) | copy-start | bytes 388
  150.2 0.8 copy-start.10
  150.2 1.3 copy-start.29
  151.5 1.3 copy-start.7
  152.8 2.1 copy-start.26
Sparse Core Ops, SparseCore 0:
  155.0 91.5 all-reduce.3
where the time goes:
time: 261 us; the launch traced here: 260 us
  waiting for transfers between devices  94.6 us (36%)
  matrix products  55.4 us (21%)
  local copies, waits for them, and re-layouts  45.2 us (17%)
  blocking collectives  30.8 us (12%)
  between operations  14.5 us (6%)
  starting transfers between devices  14.4 us (6%)
  other arithmetic  5.2 us (2%)
    psum x1, waiting for transfers between devices, shards(): lax.psum((grad_w1_self, grad_w1_near, grad_bias_one, grad_w2_self, grad_w...  60.9 us
    ppermute x9, waiting for transfers between devices, swapped(): return lax.ppermute(value, axis, pairs)  33.6 us
    psum x1, blocking collectives, shards(): lax.psum((grad_w1_self, grad_w1_near, grad_bias_one, grad_w2_self, grad_w...  30.8 us
    dot_general x9, matrix products, place_tiles(): jnp.einsum('bt,biw->tiw', target, slot_tiles, precision=lax.Precision.HIG...  18.4 us
    ppermute x9, starting transfers between devices, swapped(): return lax.ppermute(value, axis, pairs)  14.4 us
    gather x6, local copies, waits for them, and re-layouts, fetch(): return partner_blocks[wanted_src[colour]]  10.8 us
    unnamed x64, local copies, waits for them, and re-layouts  7.63 us
    dot_general x1, matrix products, shards(): jnp.einsum('tks,tkiw->siw', owners, local_terms, precision=lax.Precision....  6.34 us
  transfers between devices with their start and end apart: 10, of which 6 were waited for; matrix products, arithmetic and copies ran while one was open for 22% of the time, Pallas kernels for 0%

commit v1 on v0

v1 whole, which is shorter than its diff:
```python
import functools

import jax
import jax.numpy as jnp
from jax import lax
from jax.experimental import pallas as pl
from jax.experimental.pallas import tpu as pltpu
from jax.sharding import PartitionSpec as P

AXES = ("dom", "sub", "feat")
CHIPS = ("dom", "sub")
SMEM = pl.BlockSpec(memory_space=pltpu.SMEM)
VMEM = pl.BlockSpec(memory_space=pltpu.VMEM)
ANY = pl.BlockSpec(memory_space=pl.ANY)
VMEM_LIMIT = 40 * 2**20
F32 = jnp.float32
BF16 = jnp.bfloat16


def struct(shape, dtype):
    return jax.ShapeDtypeStruct(shape, dtype)


def swapped(value, mask):
    pairs = [(source, source ^ mask) for source in range(lax.axis_size(AXES))]
    return lax.ppermute(value, AXES, pairs)


def dot(a, b):
    return jnp.dot(a, b, preferred_element_type=F32)


def dot_bt(a, b):
    return lax.dot_general(a, b, (((1,), (1,)), ((), ())), preferred_element_type=F32)


def run(body, in_specs, out_specs, out_shape, scratch, args, flops=0, moved=0):
    return pl.pallas_call(
        body,
        in_specs=in_specs,
        out_specs=out_specs,
        out_shape=out_shape,
        scratch_shapes=scratch,
        compiler_params=pltpu.CompilerParams(vmem_limit_bytes=VMEM_LIMIT),
        cost_estimate=pl.CostEstimate(flops=flops, bytes_accessed=moved, transcendentals=0),
    )(*args)


def pick_body(picked, *refs):
    indices = refs[: len(picked)]
    blocks = refs[len(picked)]
    outs = refs[len(picked) + 1 : -1]
    sems = refs[-1]
    copies = []
    for n, colour in enumerate(picked):
        for slot in range(outs[n].shape[0]):
            copies.append(
                pltpu.make_async_copy(
                    blocks.at[indices[n][0, colour, slot]], outs[n].at[slot], sems.at[len(copies)]
                )
            )
    for copy in copies:
        copy.start()
    for copy in copies:
        copy.wait()


def first_local_body(
    index, count, features, values, edges, w1_self, bias, near, own, features_t, values_t, edges_t
):
    tiles, fan = values.shape[0], values.shape[1]
    for t in range(tiles):
        left = jnp.concatenate([values[t, k] for k in range(fan)], axis=1)
        right = jnp.concatenate([features[index[t, k]] for k in range(fan)], axis=0)
        near[t] = dot(left, right)
        own[t] = dot(features[t], w1_self[...]) + bias[...]
        features_t[:, t * 128 : (t + 1) * 128] = features[t].T
        for k in range(fan):
            values_t[t, k] = values[t, k].T
    rounds, slots = edges.shape[0], edges.shape[1]
    for r in range(rounds):
        for s in range(slots):
            live = s < count[0, r]
            edges_t[r, s] = jnp.where(live, edges[r, s].T, jnp.zeros_like(edges[r, s]))


def add_boundary(total, whole_round, src, dst, count, edges, arrived):
    rounds, slots = edges.shape[0], edges.shape[1]
    spare = total.shape[0] - 1
    for r in range(rounds):
        for s in range(slots):
            where = jnp.where(s < count[0, r], dst[0, r, s], spare)
            tile = arrived[r][src[0, r, s]] if r == whole_round else arrived[r][s]
            total[where] = total[where] + dot(edges[r, s], tile)


def first_body(
    rounds, src, dst, count, *refs
):
    partner_src = refs[:rounds]
    arrived = refs[rounds : 2 * rounds]
    edges, near, own, w1_near, w2_near, first_agg, hidden, message = refs[2 * rounds : 2 * rounds + 8]
    sends = refs[2 * rounds + 8 : 3 * rounds + 8]
    total = refs[-1]
    tiles = near.shape[0]
    total[0:tiles] = near[...]
    add_boundary(total, rounds - 1, src, dst, count, edges, arrived)
    for t in range(tiles):
        agg = total[t].astype(BF16)
        first_agg[t] = agg
        pre = own[t] + dot(agg, w1_near[...])
        act = (pre * jax.nn.sigmoid(pre)).astype(BF16)
        hidden[t] = act
        message[t] = dot(act, w2_near[...]).astype(BF16)
    for r in range(rounds):
        for s in range(sends[r].shape[0]):
            sends[r][s] = message[partner_src[r][0, r, s]]


def second_local_body(
    index, labels, values, first_agg, own, hidden, message, w1_near, w2_self, bias,
    slope, near, target, first_agg_t, hidden_t,
):
    tiles, fan = values.shape[0], values.shape[1]
    classes = w2_self.shape[1]
    class_ids = lax.broadcasted_iota(jnp.int32, (classes, 128), 0)
    for t in range(tiles):
        left = jnp.concatenate([values[t, k] for k in range(fan)], axis=1)
        right = jnp.concatenate([message[index[t, k]] for k in range(fan)], axis=0)
        near[t] = dot(left, right) + dot(hidden[t], w2_self[...]) + bias[...]
        hot = (labels[t : t + 1, :] == class_ids).astype(F32)
        target[t] = hot.T
        pre = own[t] + dot(first_agg[t], w1_near[...])
        sig = jax.nn.sigmoid(pre)
        slope[t] = sig * (1.0 + pre * (1.0 - sig))
        first_agg_t[:, t * 128 : (t + 1) * 128] = first_agg[t].T
        hidden_t[:, t * 128 : (t + 1) * 128] = hidden[t].T


def second_body(rounds, src, dst, count, *refs):
    arrived = refs[:rounds]
    edges, edges_t, near, target, logits, error = refs[rounds : rounds + 6]
    sends = refs[rounds + 6 : 2 * rounds + 6]
    total = refs[-1]
    tiles = near.shape[0]
    total[0:tiles] = near[...]
    add_boundary(total, None, src, dst, count, edges, arrived)
    for t in range(tiles):
        pre = total[t]
        logits[t] = pre.astype(BF16)
        error[t] = (pre - target[t]).astype(BF16)
    for r in range(rounds):
        for s in range(sends[r].shape[0]):
            sends[r][s] = dot(edges_t[r, s], error[dst[0, r, s]]).astype(BF16)


def back_local_body(
    index, values_t, error, hidden_t, w2_self, back, self_grad, grad_w2_self, grad_bias_two
):
    tiles, fan = values_t.shape[0], values_t.shape[1]
    back[...] = jnp.zeros_like(back)
    bias = jnp.zeros((1, error.shape[2]), F32)
    for t in range(tiles):
        rows = error[t]
        for k in range(fan):
            where = index[t, k]
            back[where] = back[where] + dot(values_t[t, k], rows)
        self_grad[t] = dot_bt(rows, w2_self[...])
        bias = bias + jnp.sum(rows.astype(F32), axis=0, keepdims=True)
    grad_bias_two[...] = bias
    flat = error[...].reshape(tiles * error.shape[1], error.shape[2])
    grad_w2_self[...] = dot(hidden_t[...], flat)


def back_body(rounds, feat, *refs):
    partner_src = refs[:rounds]
    arrived = refs[rounds : 2 * rounds]
    (back, self_grad, slope, w2_near, features_t, first_agg_t, hidden_t, grad_w2_self, grad_bias_two,
     hidden_grad, send, keep, total, back_16, first_grad, packed) = refs[2 * rounds :]
    tiles, size, classes = back.shape
    width = self_grad.shape[2]
    total[...] = back[...]
    for r in range(rounds):
        for s in range(arrived[r].shape[0]):
            where = partner_src[r][0, r, s]
            total[where] = total[where] + arrived[r][s].astype(F32)
    bias = jnp.zeros((1, width), F32)
    for t in range(tiles):
        here = slice(t * size, (t + 1) * size)
        rows = total[t].astype(BF16)
        back_16[here, :] = rows
        full = self_grad[t] + dot_bt(rows, w2_near[...])
        hidden_grad[t] = full.astype(BF16)
        grad = (full * slope[t]).astype(BF16)
        first_grad[here, :] = grad
        bias = bias + jnp.sum(grad.astype(F32), axis=0, keepdims=True)
    deep = features_t.shape[0]
    at = 0
    for left in (features_t, first_agg_t):
        product = dot(left[...], first_grad[...])
        for c in range(width // 128):
            packed[at : at + deep, :] = product[:, c * 128 : (c + 1) * 128]
            at += deep
    packed[at : at + width, :] = grad_w2_self[...]
    at += width
    packed[at : at + width, :] = dot(hidden_t[...], back_16[...])
    at += width
    packed[at:, :] = jnp.zeros_like(packed[at:, :])
    for c in range(width // 128):
        packed[at + c : at + c + 1, :] = bias[:, c * 128 : (c + 1) * 128]
    at += width // 128
    packed[at : at + 1, :] = grad_bias_two[...]
    half = keep.shape[0]
    mine = feat[0]
    keep[...] = packed[pl.ds(pl.multiple_of(mine * half, 16), half), :]
    send[...] = packed[pl.ds(pl.multiple_of((1 - mine) * half, 16), half), :].astype(BF16)


def pair_body(keep, arrived, out):
    out[...] = (keep[...] + arrived[...].astype(F32)).astype(BF16)


def chips_body(arrived, out):
    chips = arrived.shape[0]
    total = arrived[0].astype(F32)
    for c in range(1, chips):
        total = total + arrived[c].astype(F32)
    total = total.astype(BF16)
    for c in range(chips):
        out[c] = total


def unpack_body(feat, mine, other, g1_self, g1_near, g1_bias, g2_self, g2_near, g2_bias, packed):
    half = mine.shape[0]
    packed[pl.ds(pl.multiple_of(feat[0] * half, 16), half), :] = mine[...].astype(F32)
    packed[pl.ds(pl.multiple_of((1 - feat[0]) * half, 16), half), :] = other[...].astype(F32)
    deep, width = g1_self.shape
    at = 0
    for out in (g1_self, g1_near):
        for c in range(width // 128):
            out[:, c * 128 : (c + 1) * 128] = packed[at : at + deep, :]
            at += deep
    for out in (g2_self, g2_near):
        out[...] = packed[at : at + width, :]
        at += width
    for c in range(width // 128):
        g1_bias[:, c * 128 : (c + 1) * 128] = packed[at : at + 1, :]
        at += 1
    g2_bias[...] = packed[at : at + 1, :]


def shards(
    features,
    labels,
    local_index,
    local_values,
    cross_src,
    cross_dst,
    cross_count,
    cross_values,
    w1_self,
    w1_near,
    bias_one,
    w2_self,
    w2_near,
    bias_two,
):
    tiles, fan, size, _ = local_values.shape
    rounds, slots = cross_src.shape[1], cross_src.shape[2]
    width_in = features.shape[1]
    hidden_width = w1_self.shape[1]
    classes = w2_self.shape[1]
    nodes = tiles * size
    total_bits = lax.axis_size(AXES).bit_length() - 1
    masks = [1 << (total_bits - 1 - colour) for colour in range(rounds)]
    chips = lax.axis_size(CHIPS)
    blocks = features.reshape(tiles, size, width_in)
    edges = cross_values[0]
    feat = lax.axis_index("feat").astype(jnp.int32).reshape(1)
    bias_one_row = bias_one.reshape(1, hidden_width)
    bias_two_row = bias_two.reshape(1, classes)
    label_rows = labels.reshape(tiles, size)

    whole = swapped(blocks, masks[-1])
    partner_src = [swapped(cross_src, mask) for mask in masks]
    picked = list(range(rounds - 1))
    picks = run(
        functools.partial(pick_body, picked),
        [SMEM] * len(picked) + [ANY],
        [ANY] * len(picked),
        [struct((slots, size, width_in), BF16)] * len(picked),
        [pltpu.SemaphoreType.DMA((len(picked) * slots,))],
        [partner_src[r] for r in picked] + [blocks],
        moved=2 * len(picked) * slots * size * width_in * 2,
    )
    arrived = [swapped(tile, masks[r]) for r, tile in zip(picked, picks)] + [whole]

    near, own, features_t, values_t, edges_t = run(
        first_local_body,
        [SMEM, SMEM] + [VMEM] * 5,
        [VMEM] * 5,
        [
            struct((tiles, size, width_in), F32),
            struct((tiles, size, hidden_width), F32),
            struct((width_in, nodes), BF16),
            struct(local_values.shape, BF16),
            struct(edges.shape, BF16),
        ],
        [],
        [local_index, cross_count, blocks, local_values, edges, w1_self, bias_one_row],
        flops=2 * nodes * width_in * (fan * size + hidden_width),
        moved=8 * 2**20,
    )

    first_agg, hidden, message, *sends = run(
        functools.partial(first_body, rounds),
        [SMEM] * (3 + rounds) + [VMEM] * (rounds + 5),
        [VMEM] * (3 + rounds),
        [
            struct((tiles, size, width_in), BF16),
            struct((tiles, size, hidden_width), BF16),
            struct((tiles, size, classes), BF16),
        ]
        + [struct((slots, size, classes), BF16)] * rounds,
        [pltpu.VMEM((tiles + 1, size, width_in), F32)],
        [cross_src, cross_dst, cross_count, *partner_src, *arrived, edges, near, own, w1_near, w2_near],
        flops=2 * nodes * width_in * (rounds * slots * size // tiles + hidden_width + classes),
        moved=8 * 2**20,
    )
    arrived = [swapped(tile, mask) for tile, mask in zip(sends, masks)]

    slope, near, target, first_agg_t, hidden_t = run(
        second_local_body,
        [SMEM] + [VMEM] * 9,
        [VMEM] * 5,
        [
            struct((tiles, size, hidden_width), F32),
            struct((tiles, size, classes), F32),
            struct((tiles, size, classes), F32),
            struct((width_in, nodes), BF16),
            struct((hidden_width, nodes), BF16),
        ],
        [],
        [local_index, label_rows, local_values, first_agg, own, hidden, message, w1_near, w2_self, bias_two_row],
        flops=2 * nodes * classes * (fan * size + 3 * hidden_width),
        moved=6 * 2**20,
    )

    logits, error, *sends = run(
        functools.partial(second_body, rounds),
        [SMEM] * 3 + [VMEM] * (rounds + 4),
        [VMEM] * (2 + rounds),
        [struct((tiles, size, classes), BF16), struct((tiles, size, classes), BF16)]
        + [struct((slots, size, classes), BF16)] * rounds,
        [pltpu.VMEM((tiles + 1, size, classes), F32)],
        [cross_src, cross_dst, cross_count, *arrived, edges, edges_t, near, target],
        flops=4 * rounds * slots * size * size * classes,
        moved=3 * 2**20,
    )
    arrived = [swapped(tile, mask) for tile, mask in zip(sends, masks)]

    back, self_grad, grad_w2_self, grad_bias_two = run(
        back_local_body,
        [SMEM] + [VMEM] * 4,
        [VMEM] * 4,
        [
            struct((tiles, size, classes), F32),
            struct((tiles, size, hidden_width), F32),
            struct((hidden_width, classes), F32),
            struct((1, classes), F32),
        ],
        [],
        [local_index, values_t, error, hidden_t, w2_self],
        flops=2 * nodes * classes * (fan * size + 2 * hidden_width),
        moved=4 * 2**20,
    )

    rows = (2 * width_in * hidden_width + 2 * hidden_width * classes + hidden_width + classes) // 128
    piece = -(-rows // (2 * chips * 16)) * 16
    half = piece * chips
    hidden_grad, send, keep = run(
        functools.partial(back_body, rounds),
        [SMEM] * (1 + rounds) + [VMEM] * (rounds + 9),
        [VMEM] * 3,
        [
            struct((tiles, size, hidden_width), BF16),
            struct((half, 128), BF16),
            struct((half, 128), F32),
        ],
        [
            pltpu.VMEM((tiles, size, classes), F32),
            pltpu.VMEM((nodes, classes), BF16),
            pltpu.VMEM((nodes, hidden_width), BF16),
            pltpu.VMEM((2 * half, 128), F32),
        ],
        [
            feat, *partner_src, *arrived, back, self_grad, slope, w2_near, features_t, first_agg_t,
            hidden_t, grad_w2_self, grad_bias_two,
        ],
        flops=2 * nodes * hidden_width * (2 * width_in + 2 * classes),
        moved=6 * 2**20,
    )

    pair = run(
        pair_body, [VMEM] * 2, VMEM, struct((half, 128), BF16), [],
        [keep, swapped(send, 1)], flops=half * 128, moved=half * 128 * 8,
    )
    pieces = lax.all_to_all(pair.reshape(chips, piece, 128), CHIPS, 0, 0)
    copies = run(
        chips_body, [VMEM], VMEM, struct((chips, piece, 128), BF16), [],
        [pieces], flops=half * 128, moved=half * 128 * 4,
    )
    mine = lax.all_to_all(copies, CHIPS, 0, 0).reshape(half, 128)
    other = swapped(mine, 1)
    g1_self, g1_near, g1_bias, g2_self, g2_near, g2_bias = run(
        unpack_body,
        [SMEM] + [VMEM] * 2,
        [VMEM] * 6,
        [
            struct((width_in, hidden_width), F32),
            struct((width_in, hidden_width), F32),
            struct((1, hidden_width), F32),
            struct((hidden_width, classes), F32),
            struct((hidden_width, classes), F32),
            struct((1, classes), F32),
        ],
        [pltpu.VMEM((2 * half, 128), F32)],
        [feat, mine, other],
        moved=half * 128 * 12,
    )
    return (
        logits.reshape(nodes, classes),
        hidden_grad.reshape(nodes, hidden_width),
        g1_self,
        g1_near,
        g1_bias.reshape(hidden_width),
        g2_self,
        g2_near,
        g2_bias.reshape(classes),
    )


def solution(mesh):
    in_specs = (
        P(("grp", "dom", "sub", "feat"), None),
        P(("grp", "dom", "sub", "feat")),
        P(("grp", "dom", "sub", "feat"), None),
        P(("grp", "dom", "sub", "feat"), None, None, None),
        P(("grp", "dom", "sub", "feat"), None, None),
        P(("grp", "dom", "sub", "feat"), None, None),
        P(("grp", "dom", "sub", "feat"), None),
        P(("grp", "dom", "sub", "feat"), None, None, None, None),
        P(),
        P(),
        P(),
        P(),
        P(),
        P(),
    )
    out_specs = (
        P(("grp", "dom", "sub", "feat"), None),
        P(("grp", "dom", "sub", "feat"), None),
        P("grp", None),
        P("grp", None),
        P("grp"),
        P("grp", None),
        P("grp", None),
        P("grp"),
    )
    return jax.shard_map(shards, mesh=mesh, in_specs=in_specs, out_specs=out_specs, check_vma=False)
```

time: 261 us -> 78.3 us (0.30)
  waiting for transfers between devices: 94.6 us -> 14.8 us
  matrix products: 55.4 us -> 0 us
  local copies, waits for them, and re-layouts: 45.2 us -> 10.1 us
  between operations: 14.5 us -> 0.82 us
  Pallas kernels: 0 us -> 12.5 us
  blocking collectives: 30.8 us -> 23.1 us
  other arithmetic: 5.2 us -> 0 us
    psum x1 -> x0, waiting for transfers between devices: 60.9 us -> none  [shards(): lax.psum((grad_w1_self, grad_w1_near, grad_bias_one, grad_w2_self, grad_w...]
    dot_general x32 -> x0, matrix products: 55.4 us -> none  [the longest x9 18.4 us: place_tiles(): jnp.einsum('bt,biw->tiw', target, slot_tiles, precision=lax.Precision.HIG...]
    psum x1 -> x0, blocking collectives: 30.8 us -> none  [shards(): lax.psum((grad_w1_self, grad_w1_near, grad_bias_one, grad_w2_self, grad_w...]
    all_to_all x0 -> x2, blocking collectives: none -> 23.1 us  [the longest x1 11.8 us: shards(): pieces = lax.all_to_all(pair.reshape(chips, piece, 128), CHIPS, 0, 0)]
    gather x11 -> x0, local copies, waits for them, and re-layouts: 19.1 us -> none  [the longest x6 10.8 us: fetch(): return partner_blocks[wanted_src[colour]]]
    ppermute x9 -> x14, waiting for transfers between devices: 33.6 us -> 14.8 us  [swapped(): return lax.ppermute(value, AXES, pairs)]
    dot_general x10 -> x0, local copies, waits for them, and re-layouts: 16.3 us -> none  [the longest x3 6.27 us: shards(): jnp.einsum('bji,bjw->biw', edge_tiles[colour], grad_blocks[wanted_dst[col...]
    pallas_call x0 -> x10, Pallas kernels: none -> 12.5 us  [run(): pl.pallas_call(body, in_specs=in_specs, out_specs=out_specs, out_shape=ou...]
  transfers between devices with their start and end apart: 10 -> 14, of which waited for: 6 -> 9; matrix products, arithmetic and copies ran while one was open for 22% -> 1% of each run, Pallas kernels for 0% -> 7%
where the time goes in v1:
time: 78.3 us; the launch traced here: 77.8 us
  blocking collectives  23.1 us (30%)
  starting transfers between devices  16.4 us (21%)
  waiting for transfers between devices  14.8 us (19%)
  Pallas kernels  12.5 us (16%)
  local copies, waits for them, and re-layouts  10.1 us (13%)
  between operations  0.82 us (1%)
    ppermute x14, starting transfers between devices, swapped(): return lax.ppermute(value, AXES, pairs)  16.4 us
    ppermute x14, waiting for transfers between devices, swapped(): return lax.ppermute(value, AXES, pairs)  14.8 us
    pallas_call x10, Pallas kernels, run(): pl.pallas_call(body, in_specs=in_specs, out_specs=out_specs, out_shape=ou...  12.5 us
    all_to_all x1, blocking collectives, shards(): pieces = lax.all_to_all(pair.reshape(chips, piece, 128), CHIPS, 0, 0)  11.8 us
    all_to_all x1, blocking collectives, shards(): mine = lax.all_to_all(copies, CHIPS, 0, 0).reshape(half, 128)  11.3 us
    unnamed x53, local copies, waits for them, and re-layouts  10.1 us
  transfers between devices with their start and end apart: 14, of which 9 were waited for; matrix products, arithmetic and copies ran while one was open for 1% of the time, Pallas kernels for 7%

profile of v1, /device:TPU:0, one launch (start us, length us, event | category | flops | bytes accessed | tf_op | source)
XLA Modules:
  0.0 77.8 jit_solution(150432330752285322)
XLA Ops:
  0.6 3.0 %collective-permute-start.5 = (bf16[8,128,256]{2,1,0:T(8,128)(2,1)}, bf16[8,128,256]{2,1,0:T(8,128)(2,1)S(1)}, u32[]{:S(2)}, u32[]{:S(2)}) collective-permute-start(bf16[8,128,256]{2,1,0:T(8,128)(2,1)} %bitcast.15), channel_id=1, source_target_pairs={{0,2},{1,3},{2,0},{3,1},{4,6},{5,7},{6,4},{7,5},{8,10},{9,11},{10,... | collective-permute-start | bytes 1572872 | tf_op jit(solution)/shard_map/ppermute | solution.py:26
  3.6 0.7 copy.29.src
  4.3 2.6 %collective-permute-start = (s32[1,3,4]{2,1,0:T(4,128)S(1)}, s32[1,3,4]{2,1,0:T(4,128)S(1)}, u32[]{:S(2)}, u32[]{:S(2)}) collective-permute-start(s32[1,3,4]{2,1,0:T(4,128)S(1)} %copy.29.src), channel_id=1, source_target_pairs={{0,8},{1,9},{2,10},{3,11},{4,12},{5,13},{6,14},{7,15},{8,0},{9,1},... | collective-permute-start | bytes 152 | tf_op jit(solution)/shard_map/ppermute | solution.py:26
  6.9 1.6 %collective-permute-start.1 = (s32[1,3,4]{2,1,0:T(4,128)S(1)}, s32[1,3,4]{2,1,0:T(4,128)S(1)}, u32[]{:S(2)}, u32[]{:S(2)}) collective-permute-start(s32[1,3,4]{2,1,0:T(4,128)S(1)} %copy.29.src), channel_id=1, source_target_pairs={{0,4},{1,5},{2,6},{3,7},{4,0},{5,1},{6,2},{7,3},{8,12},{9,13},{10,... | collective-permute-start | bytes 152 | tf_op jit(solution)/shard_map/ppermute | solution.py:26
  8.5 0.3 collective-permute-done.refs_0_
  8.8 1.7 %collective-permute-done.1.refs_1_ = s32[1,3,4]{2,1,0:T(4,128)S(1)} collective-permute-done((s32[1,3,4]{2,1,0:T(4,128)S(1)}, s32[1,3,4]{2,1,0:T(4,128)S(1)}, u32[]{:S(2)}, u32[]{:S(2)}) %collective-permute-start.1) | collective-permute-done | bytes 80 | tf_op jit(solution)/shard_map/ppermute | solution.py:26
  10.5 1.0 %copy-done.3 = bf16[1024,256]{1,0:T(8,128)(2,1)S(1)} copy-done((bf16[1024,256]{1,0:T(8,128)(2,1)S(1)}, bf16[1024,256]{1,0:T(8,128)(2,1)}, u32[]{:S(2)}) %copy-start.3) | copy-done | bytes 524312
  11.5 1.4 %shard_map.197 = (bf16[4,128,256]{2,1,0:T(8,128)(2,1)}, bf16[4,128,256]{2,1,0:T(8,128)(2,1)S(1)}) custom-call(s32[1,3,4]{2,1,0:T(4,128)S(1)} %collective-permute-done.refs_0_, s32[1,3,4]{2,1,0:T(4,128)S(1)} %collective-permute-done.1.refs_1_, bf16[8,128,256]{2,1,0:T(8,128)(2,1)S(1)} %bitcast.16), custom_call_target="tpu_custom_call" | custom-call | bytes 1048576 | tf_op jit(solution)/shard_map/pallas_call | solution.py:38
  12.9 1.0 %collective-permute-start.3 = (bf16[4,128,256]{2,1,0:T(8,128)(2,1)}, bf16[4,128,256]{2,1,0:T(8,128)(2,1)S(1)}, u32[]{:S(2)}, u32[]{:S(2)}) collective-permute-start(bf16[4,128,256]{2,1,0:T(8,128)(2,1)} %get-tuple-element.44), channel_id=1, source_target_pairs={{0,8},{1,9},{2,10},{3,11},{4,12},{5,13},{6,14},{7,15},{8,0},{9,1},... | collective-permute-start | bytes 786440 | tf_op jit(solution)/shard_map/ppermute | solution.py:26
  13.9 1.6 %collective-permute-start.4 = (bf16[4,128,256]{2,1,0:T(8,128)(2,1)S(1)}, bf16[4,128,256]{2,1,0:T(8,128)(2,1)S(1)}, u32[]{:S(2)}, u32[]{:S(2)}) collective-permute-start(bf16[4,128,256]{2,1,0:T(8,128)(2,1)S(1)} %get-tuple-element.45), channel_id=1, source_target_pairs={{0,4},{1,5},{2,6},{3,7},{4,0},{5,1},{6,2},{7,3},{8,12},{9,13},{10,... | collective-permute-start | bytes 786440 | tf_op jit(solution)/shard_map/ppermute | solution.py:26
  15.5 0.5 collective-permute-start.2
  16.0 0.1 copy.25.index
  16.1 0.6 copy-done.19
  16.8 0.0 copy-done.21
  16.8 1.2 %copy-done = bf16[8,4,128,128]{3,2,1,0:T(8,128)(2,1)S(1)} copy-done((bf16[8,4,128,128]{3,2,1,0:T(8,128)(2,1)S(1)}, bf16[8,4,128,128]{3,2,1,0:T(8,128)(2,1)}, u32[]{:S(2)}) %copy-start) | copy-done | bytes 1048600
  18.0 1.0 %copy-done.4 = bf16[1024,256]{1,0:T(8,128)(2,1)S(1)} copy-done((bf16[1024,256]{1,0:T(8,128)(2,1)S(1)}, bf16[1024,256]{1,0:T(8,128)(2,1)}, u32[]{:S(2)}) %copy-start.4) | copy-done | bytes 524312
  19.1 1.4 %shard_map.198 = (f32[8,128,256]{2,1,0:T(8,128)S(1)}, f32[8,128,256]{2,1,0:T(8,128)S(1)}, bf16[256,1024]{1,0:T(8,128)(2,1)S(1)}, bf16[8,4,128,128]{3,2,1,0:T(8,128)(2,1)S(1)}, bf16[3,4,128,128]{3,2,1,0:T(8,128)(2,1)S(1)}) custom-call(s32[8,4]{1,0:T(8,128)S(1)} %copy.25.index, s32[1,3]{1,0:T(1,128)S(1)} %copy-done.19, bf16[8,128,256]{2,1,0:T(8,128)(2,1)S(1)} %bitcast.17, ...), custom_call_target="tpu_custom_call" | custom-call | flops 402653184 | bytes 8388608 | tf_op jit(solution)/shard_map/pallas_call | solution.py:38
  20.5 5.9 %collective-permute-done.3.refs_3_ = bf16[4,128,256]{2,1,0:T(8,128)(2,1)S(1)} collective-permute-done((bf16[4,128,256]{2,1,0:T(8,128)(2,1)}, bf16[4,128,256]{2,1,0:T(8,128)(2,1)S(1)}, u32[]{:S(2)}, u32[]{:S(2)}) %collective-permute-start.3) | collective-permute-done | bytes 262176 | tf_op jit(solution)/shard_map/ppermute | solution.py:26
  26.4 0.0 copy-start.1
  26.4 0.0 copy-start.10
  26.5 1.7 %shard_map.199 = (bf16[8,128,256]{2,1,0:T(8,128)(2,1)S(1)}, bf16[8,128,256]{2,1,0:T(8,128)(2,1)S(1)}, bf16[8,128,128]{2,1,0:T(8,128)(2,1)S(1)}, bf16[4,128,128]{...) custom-call(s32[1,3,4]{2,1,0:T(4,128)S(1)} %copy.29.src, ...), custom_call_target="tpu_custom_call" | custom-call | flops 301989888 | bytes 8388608 | tf_op jit(solution)/shard_map/pallas_call | solution.py:38
  28.2 1.6 %collective-permute-start.6 = (bf16[4,128,128]{2,1,0:T(8,128)(2,1)S(1)}, bf16[4,128,128]{2,1,0:T(8,128)(2,1)S(1)}, u32[]{:S(2)}, u32[]{:S(2)}) collective-permute-start(bf16[4,128,128]{2,1,0:T(8,128)(2,1)S(1)} %get-tuple-element.48), channel_id=1, source_target_pairs={{0,8},{1,9},{2,10},{3,11},{4,12},{5,13},{6,14},{7,15},{8,0},{9,1},... | collective-permute-start | bytes 393224 | tf_op jit(solution)/shard_map/ppermute | solution.py:26
  29.8 1.4 %collective-permute-start.7 = (bf16[4,128,128]{2,1,0:T(8,128)(2,1)S(1)}, bf16[4,128,128]{2,1,0:T(8,128)(2,1)S(1)}, u32[]{:S(2)}, u32[]{:S(2)}) collective-permute-start(bf16[4,128,128]{2,1,0:T(8,128)(2,1)S(1)} %get-tuple-element.49), channel_id=1, source_target_pairs={{0,4},{1,5},{2,6},{3,7},{4,0},{5,1},{6,2},{7,3},{8,12},{9,13},{10,... | collective-permute-start | bytes 393224 | tf_op jit(solution)/shard_map/ppermute | solution.py:26
  31.2 0.5 collective-permute-start.8
  31.8 0.7 copy-done.20
  32.5 1.5 %shard_map.200 = (f32[8,128,256]{2,1,0:T(8,128)S(1)}, f32[8,128,128]{2,1,0:T(8,128)S(1)}, f32[8,128,128]{2,1,0:T(8,128)S(1)}, bf16[256,1024]{1,0:T(8,128)(2,1)S(1)}, bf16[256,1024]{1,0:T(8,128)(2,1)S(1)}) custom-call(s32[8,4]{1,0:T(8,128)S(1)} %copy.25.index, s32[8,128]{1,0:T(8,128)S(1)} %bitcast.21, bf16[8,4,128,128]{3,2,1,0:T(8,128)(2,1)S(1)} %copy-done.1, ...), custom_call_target="tpu_custom_call" | custom-call | flops 335544320 | bytes 6291456 | tf_op jit(solution)/shard_map/pallas_call | solution.py:38
  34.0 0.8 %copy-done.6 = bf16[256,1024]{1,0:T(8,128)(2,1)} copy-done((bf16[256,1024]{1,0:T(8,128)(2,1)}, bf16[256,1024]{1,0:T(8,128)(2,1)S(1)}, u32[]{:S(2)}) %copy-start.6) | copy-done | bytes 524312
  34.8 1.7 %collective-permute-done.6.refs_0_ = bf16[4,128,128]{2,1,0:T(8,128)(2,1)S(1)} collective-permute-done((bf16[4,128,128]{2,1,0:T(8,128)(2,1)S(1)}, bf16[4,128,128]{2,1,0:T(8,128)(2,1)S(1)}, u32[]{:S(2)}, u32[]{:S(2)}) %collective-permute-start.6) | collective-permute-done | bytes 131104 | tf_op jit(solution)/shard_map/ppermute | solution.py:26
  36.4 0.4 collective-permute-done.7.refs_1_
  36.9 0.7 copy-done.16
  37.6 1.9 %shard_map.201 = (bf16[8,128,128]{2,1,0:T(8,128)(2,1)}, bf16[8,128,128]{2,1,0:T(8,128)(2,1)S(1)}, bf16[4,128,128]{2,1,0:T(8,128)(2,1)}, bf16[4,128,128]{2,1,0:T(8,128)(2,1)}, bf16[4,128,128]{2,1,0:T(8,128)(2,1)}) custom-call(s32[1,3,4]{2,1,0:T(4,128)S(1)} %copy.29.src, s32[1,3,4]{2,1,0:T(4,128)S(1)} %copy-done.16, s32[1,3]{1,0:T(1,128)S(1)} %copy-done.19, ...), custom_call_target="tpu_custom_call" | custom-call | flops 100663296 | bytes 3145728 | tf_op jit(solution)/shard_map/pallas_call | solution.py:38
  39.4 0.7 copy-done.12
  40.1 0.2 collective-permute-start.9
  40.4 1.8 %collective-permute-start.10 = (bf16[4,128,128]{2,1,0:T(8,128)(2,1)}, bf16[4,128,128]{2,1,0:T(8,128)(2,1)S(1)}, u32[]{:S(2)}, u32[]{:S(2)}) collective-permute-start(bf16[4,128,128]{2,1,0:T(8,128)(2,1)} %get-tuple-element.59), channel_id=1, source_target_pairs={{0,4},{1,5},{2,6},{3,7},{4,0},{5,1},{6,2},{7,3},{8,12},{9,13},{10,... | collective-permute-start | bytes 393224 | tf_op jit(solution)/shard_map/ppermute | solution.py:26
  42.1 0.5 collective-permute-start.11
  42.7 0.8 %copy-done.11 = bf16[256,128]{1,0:T(8,128)(2,1)S(1)} copy-done((bf16[256,128]{1,0:T(8,128)(2,1)S(1)}, bf16[256,128]{1,0:T(8,128)(2,1)}, u32[]{:S(2)}) %copy-start.11) | copy-done | bytes 65560
  43.5 0.9 %copy-done.13 = bf16[8,128,128]{2,1,0:T(8,128)(2,1)S(1)} copy-done((bf16[8,128,128]{2,1,0:T(8,128)(2,1)S(1)}, bf16[8,128,128]{2,1,0:T(8,128)(2,1)}, u32[]{:S(2)}) %copy-start.13) | copy-done | bytes 262168
  44.5 1.5 %shard_map.202 = (f32[8,128,128]{2,1,0:T(8,128)S(1)}, f32[8,128,256]{2,1,0:T(8,128)S(1)}, f32[256,128]{1,0:T(8,128)S(1)}, f32[1,128]{1,0:T(1,128)S(1)}) custom-call(s32[8,4]{1,0:T(8,128)S(1)} %copy.25.index, bf16[8,4,128,128]{3,2,1,0:T(8,128)(2,1)S(1)} %get-tuple-element.61.values_t, bf16[8,128,128]{2,1,0:T(8,128)(2,1)S(1)} %copy-done.13, ...), custom_call_target="tpu_custom_call" | custom-call | flops 268435456 | bytes 4194304 | tf_op jit(solution)/shard_map/pallas_call | solution.py:38
  45.9 1.6 %collective-permute-done.9.refs_3_ = bf16[4,128,128]{2,1,0:T(8,128)(2,1)S(1)} collective-permute-done((bf16[4,128,128]{2,1,0:T(8,128)(2,1)}, bf16[4,128,128]{2,1,0:T(8,128)(2,1)S(1)}, u32[]{:S(2)}, u32[]{:S(2)}) %collective-permute-start.9) | collective-permute-done | bytes 131104 | tf_op jit(solution)/shard_map/ppermute | solution.py:26
  47.6 0.1 collective-permute-done.10.refs_4_
  47.7 0.7 copy-done.18
  48.4 2.3 %shard_map.203 = (bf16[8,128,256]{2,1,0:T(8,128)(2,1)}, bf16[896,128]{1,0:T(8,128)(2,1)S(1)}, f32[896,128]{1,0:T(8,128)S(1)}) custom-call(s32[1]{0:T(128)} %bitcast.6.feat, s32[1,3,4]{2,1,0:T(4,128)S(1)} %collective-permute-done.refs_0_, s32[1,3,4]{2,1,0:T(4,128)S(1)} %collective-permute-done.1.refs_1_, s32[1,3,4]{2,1,0:T(4,128)S(1)} %copy-done.18, ...), custom_call_target="tpu_custom_call" | custom-call | flops 402653184 | bytes 6291456 | tf_op jit(solution)/shard_map/pallas_call | solution.py:38
  50.6 1.5 %collective-permute-done.12.arrived = bf16[896,128]{1,0:T(8,128)(2,1)S(1)} collective-permute-done((bf16[896,128]{1,0:T(8,128)(2,1)S(1)}, bf16[896,128]{1,0:T(8,128)(2,1)S(1)}, u32[]{:S(2)}, u32[]{:S(2)}) %collective-permute-start.12) | collective-permute-done | bytes 229408 | tf_op jit(solution)/shard_map/ppermute | solution.py:26
  52.1 0.1 shard_map.204
  52.2 11.8 %all_to_all.10.arrived = bf16[8,112,128]{2,1,0:T(8,128)(2,1)S(1)} all-to-all(bf16[8,112,128]{2,1,0:T(8,128)(2,1)S(1)} %bitcast.18), channel_id=1, replica_groups=mesh['grp'=2,'dom'=4,'sub'=2,'feat'=2] {'dom','sub'}, dimensions={0} | all-to-all | bytes 458752 | tf_op jit(solution)/shard_map/all_to_all | solution.py:408
  64.0 11.3 %all_to_all.11 = bf16[8,112,128]{2,1,0:T(8,128)(2,1)S(1)} all-to-all(bf16[8,112,128]{2,1,0:T(8,128)(2,1)S(1)} %shard_map.205), channel_id=1, replica_groups=mesh['grp'=2,'dom'=4,'sub'=2,'feat'=2] {'dom','sub'}, dimensions={0} | all-to-all | bytes 458752 | tf_op jit(solution)/shard_map/all_to_all | solution.py:413
  75.3 1.5 %collective-permute-done.13.other = bf16[896,128]{1,0:T(8,128)(2,1)S(1)} collective-permute-done((bf16[896,128]{1,0:T(8,128)(2,1)S(1)}, bf16[896,128]{1,0:T(8,128)(2,1)S(1)}, u32[]{:S(2)}, u32[]{:S(2)}) %collective-permute-start.13) | collective-permute-done | bytes 229408 | tf_op jit(solution)/shard_map/ppermute | solution.py:26
  76.8 1.0 %shard_map.206 = (f32[256,256]{1,0:T(8,128)}, f32[256,256]{1,0:T(8,128)}, f32[1,256]{1,0:T(1,128)}, f32[256,128]{1,0:T(8,128)}, f32[256,128]{1,0:T(8,128)}, /*index=5*/f32[1,128]{1,0:T(1,128)}) custom-call(s32[1]{0:T(128)} %bitcast.6.feat, bf16[896,128]{1,0:T(8,128)(2,1)S(1)} %bitcast.20, bf16[896,128]{1,0:T(8,128)(2,1)S(1)} %collective-permute-done.13.other), custom_call_target="tpu_custom_call" | custom-call | bytes 1376256 | tf_op jit(solution)/shard_map/pallas_call | solution.py:38
  (45 shorter events, 0.1 us)
Async XLA Ops:
  0.6 15.5 %copy-start.2 = (bf16[1,3,4,128,128]{4,3,2,1,0:T(8,128)(2,1)S(1)}, bf16[1,3,4,128,128]{4,3,2,1,0:T(8,128)(2,1)}, u32[]{:S(2)}) copy-start(bf16[1,3,4,128,128]{4,3,2,1,0:T(8,128)(2,1)} %param.21) | copy-start | bytes 1179652
  0.6 25.8 %collective-permute-start.5 = (bf16[8,128,256]{2,1,0:T(8,128)(2,1)}, bf16[8,128,256]{2,1,0:T(8,128)(2,1)S(1)}, u32[]{:S(2)}, u32[]{:S(2)}) collective-permute-start(bf16[8,128,256]{2,1,0:T(8,128)(2,1)} %bitcast.15), channel_id=1, source_target_pairs={{0,2},{1,3},{2,0},{3,1},{4,6},{5,7},{6,4},{7,5},{8,10},{9,11},{10,... | collective-permute-start | bytes 1572872 | tf_op jit(solution)/shard_map/ppermute | solution.py:26
  4.3 4.5 %collective-permute-start = (s32[1,3,4]{2,1,0:T(4,128)S(1)}, s32[1,3,4]{2,1,0:T(4,128)S(1)}, u32[]{:S(2)}, u32[]{:S(2)}) collective-permute-start(s32[1,3,4]{2,1,0:T(4,128)S(1)} %copy.29.src), channel_id=1, source_target_pairs={{0,8},{1,9},{2,10},{3,11},{4,12},{5,13},{6,14},{7,15},{8,0},{9,1},... | collective-permute-start | bytes 152 | tf_op jit(solution)/shard_map/ppermute | solution.py:26
  6.9 3.6 %collective-permute-start.1 = (s32[1,3,4]{2,1,0:T(4,128)S(1)}, s32[1,3,4]{2,1,0:T(4,128)S(1)}, u32[]{:S(2)}, u32[]{:S(2)}) collective-permute-start(s32[1,3,4]{2,1,0:T(4,128)S(1)} %copy.29.src), channel_id=1, source_target_pairs={{0,4},{1,5},{2,6},{3,7},{4,0},{5,1},{6,2},{7,3},{8,12},{9,13},{10,... | collective-permute-start | bytes 152 | tf_op jit(solution)/shard_map/ppermute | solution.py:26
  10.5 1.0 %copy-start.3 = (bf16[1024,256]{1,0:T(8,128)(2,1)S(1)}, bf16[1024,256]{1,0:T(8,128)(2,1)}, u32[]{:S(2)}) copy-start(bf16[1024,256]{1,0:T(8,128)(2,1)} %param.14) | copy-start | bytes 1572868
  11.5 4.6 %copy-start.14 = (bf16[256,256]{1,0:T(8,128)(2,1)S(1)}, bf16[256,256]{1,0:T(8,128)(2,1)}, u32[]{:S(2)}) copy-start(bf16[256,256]{1,0:T(8,128)(2,1)} %w1_self.1) | copy-start | bytes 393220
  12.9 3.1 %copy-start.24 = (s32[1,3,4]{2,0,1:T(1,128)S(1)}, s32[1,3,4]{2,0,1:T(1,128)}, u32[]{:S(2)}) copy-start(s32[1,3,4]{2,0,1:T(1,128)} %param.19) | copy-start | bytes 148
  12.9 13.5 %collective-permute-start.3 = (bf16[4,128,256]{2,1,0:T(8,128)(2,1)}, bf16[4,128,256]{2,1,0:T(8,128)(2,1)S(1)}, u32[]{:S(2)}, u32[]{:S(2)}) collective-permute-start(bf16[4,128,256]{2,1,0:T(8,128)(2,1)} %get-tuple-element.44), channel_id=1, source_target_pairs={{0,8},{1,9},{2,10},{3,11},{4,12},{5,13},{6,14},{7,15},{8,0},{9,1},... | collective-permute-start | bytes 786440 | tf_op jit(solution)/shard_map/ppermute | solution.py:26
  13.9 2.1 %copy-start.23 = (s32[8,4]{0,1:T(4,128)S(1)}, s32[8,4]{0,1:T(4,128)}, u32[]{:S(2)}) copy-start(s32[8,4]{0,1:T(4,128)} %param.16) | copy-start | bytes 388
  13.9 12.5 %collective-permute-start.4 = (bf16[4,128,256]{2,1,0:T(8,128)(2,1)S(1)}, bf16[4,128,256]{2,1,0:T(8,128)(2,1)S(1)}, u32[]{:S(2)}, u32[]{:S(2)}) collective-permute-start(bf16[4,128,256]{2,1,0:T(8,128)(2,1)S(1)} %get-tuple-element.45), channel_id=1, source_target_pairs={{0,4},{1,5},{2,6},{3,7},{4,0},{5,1},{6,2},{7,3},{8,12},{9,13},{10,... | collective-permute-start | bytes 786440 | tf_op jit(solution)/shard_map/ppermute | solution.py:26
  15.5 5.0 %collective-permute-start.2 = (s32[1,3,4]{2,1,0:T(4,128)S(1)}, s32[1,3,4]{2,1,0:T(4,128)S(1)}, u32[]{:S(2)}, u32[]{:S(2)}) collective-permute-start(s32[1,3,4]{2,1,0:T(4,128)S(1)} %copy.29.src), channel_id=1, source_target_pairs={{0,2},{1,3},{2,0},{3,1},{4,6},{5,7},{6,4},{7,5},{8,10},{9,11},{10,... | collective-permute-start | bytes 152 | tf_op jit(solution)/shard_map/ppermute | solution.py:26
  16.0 10.4 %copy-start.15 = (s32[1,3,4]{2,1,0:T(4,128)}, s32[1,3,4]{2,1,0:T(4,128)S(1)}, u32[]{:S(2)}) copy-start(s32[1,3,4]{2,1,0:T(4,128)S(1)} %copy.30.dst) | copy-start | bytes 148
  16.1 0.7 copy-start.19
  16.1 0.7 copy-start.21
  16.8 1.2 %copy-start = (bf16[8,4,128,128]{3,2,1,0:T(8,128)(2,1)S(1)}, bf16[8,4,128,128]{3,2,1,0:T(8,128)(2,1)}, u32[]{:S(2)}) copy-start(bf16[8,4,128,128]{3,2,1,0:T(8,128)(2,1)} %values.3) | copy-start | bytes 3145732
  18.0 1.0 %copy-start.4 = (bf16[1024,256]{1,0:T(8,128)(2,1)S(1)}, bf16[1024,256]{1,0:T(8,128)(2,1)}, u32[]{:S(2)}) copy-start(bf16[1024,256]{1,0:T(8,128)(2,1)} %param.14) | copy-start | bytes 1572868
  19.1 7.3 %copy-start.5 = (bf16[256,256]{1,0:T(8,128)(2,1)S(1)}, bf16[256,256]{1,0:T(8,128)(2,1)}, u32[]{:S(2)}) copy-start(bf16[256,256]{1,0:T(8,128)(2,1)} %w1_near.1) | copy-start | bytes 393220
  19.1 7.4 %copy-start.8 = (bf16[256,128]{1,0:T(8,128)(2,1)S(1)}, bf16[256,128]{1,0:T(8,128)(2,1)}, u32[]{:S(2)}) copy-start(bf16[256,128]{1,0:T(8,128)(2,1)} %refs_9_.3) | copy-start | bytes 196612
  20.5 7.7 %copy-start.17 = (s32[1,3,4]{2,1,0:T(4,128)}, s32[1,3,4]{2,1,0:T(4,128)S(1)}, u32[]{:S(2)}) copy-start(s32[1,3,4]{2,1,0:T(4,128)S(1)} %collective-permute-done.2.refs_2_) | copy-start | bytes 148
  26.4 5.3 %copy-start.1 = (bf16[8,4,128,128]{3,2,1,0:T(8,128)(2,1)S(1)}, bf16[8,4,128,128]{3,2,1,0:T(8,128)(2,1)}, u32[]{:S(2)}) copy-start(bf16[8,4,128,128]{3,2,1,0:T(8,128)(2,1)} %values.3) | copy-start | bytes 3145732
  26.4 5.3 %copy-start.10 = (bf16[256,128]{1,0:T(8,128)(2,1)S(1)}, bf16[256,128]{1,0:T(8,128)(2,1)}, u32[]{:S(2)}) copy-start(bf16[256,128]{1,0:T(8,128)(2,1)} %w2_self.3) | copy-start | bytes 196612
  28.2 8.3 %collective-permute-start.6 = (bf16[4,128,128]{2,1,0:T(8,128)(2,1)S(1)}, bf16[4,128,128]{2,1,0:T(8,128)(2,1)S(1)}, u32[]{:S(2)}, u32[]{:S(2)}) collective-permute-start(bf16[4,128,128]{2,1,0:T(8,128)(2,1)S(1)} %get-tuple-element.48), channel_id=1, source_target_pairs={{0,8},{1,9},{2,10},{3,11},{4,12},{5,13},{6,14},{7,15},{8,0},{9,1},... | collective-permute-start | bytes 393224 | tf_op jit(solution)/shard_map/ppermute | solution.py:26
  29.8 7.1 %collective-permute-start.7 = (bf16[4,128,128]{2,1,0:T(8,128)(2,1)S(1)}, bf16[4,128,128]{2,1,0:T(8,128)(2,1)S(1)}, u32[]{:S(2)}, u32[]{:S(2)}) collective-permute-start(bf16[4,128,128]{2,1,0:T(8,128)(2,1)S(1)} %get-tuple-element.49), channel_id=1, source_target_pairs={{0,4},{1,5},{2,6},{3,7},{4,0},{5,1},{6,2},{7,3},{8,12},{9,13},{10,... | collective-permute-start | bytes 393224 | tf_op jit(solution)/shard_map/ppermute | solution.py:26
  31.2 5.7 %collective-permute-start.8 = (bf16[4,128,128]{2,1,0:T(8,128)(2,1)S(1)}, bf16[4,128,128]{2,1,0:T(8,128)(2,1)S(1)}, u32[]{:S(2)}, u32[]{:S(2)}) collective-permute-start(bf16[4,128,128]{2,1,0:T(8,128)(2,1)S(1)} %get-tuple-element.50), channel_id=1, source_target_pairs={{0,2},{1,3},{2,0},{3,1},{4,6},{5,7},{6,4},{7,5},{8,10},{9,11},{10,... | collective-permute-start | bytes 393224 | tf_op jit(solution)/shard_map/ppermute | solution.py:26
  31.8 0.7 copy-start.20
  31.8 0.7 copy-start.22
  34.0 0.8 %copy-start.6 = (bf16[256,1024]{1,0:T(8,128)(2,1)}, bf16[256,1024]{1,0:T(8,128)(2,1)S(1)}, u32[]{:S(2)}) copy-start(bf16[256,1024]{1,0:T(8,128)(2,1)S(1)} %get-tuple-element.68.refs_11_) | copy-start | bytes 1572868
  36.9 0.7 copy-start.16
  39.4 0.7 copy-start.12
  40.1 7.4 %collective-permute-start.9 = (bf16[4,128,128]{2,1,0:T(8,128)(2,1)}, bf16[4,128,128]{2,1,0:T(8,128)(2,1)S(1)}, u32[]{:S(2)}, u32[]{:S(2)}) collective-permute-start(bf16[4,128,128]{2,1,0:T(8,128)(2,1)} %get-tuple-element.58), channel_id=1, source_target_pairs={{0,8},{1,9},{2,10},{3,11},{4,12},{5,13},{6,14},{7,15},{8,0},{9,1},... | collective-permute-start | bytes 393224 | tf_op jit(solution)/shard_map/ppermute | solution.py:26
  40.4 7.3 %collective-permute-start.10 = (bf16[4,128,128]{2,1,0:T(8,128)(2,1)}, bf16[4,128,128]{2,1,0:T(8,128)(2,1)S(1)}, u32[]{:S(2)}, u32[]{:S(2)}) collective-permute-start(bf16[4,128,128]{2,1,0:T(8,128)(2,1)} %get-tuple-element.59), channel_id=1, source_target_pairs={{0,4},{1,5},{2,6},{3,7},{4,0},{5,1},{6,2},{7,3},{8,12},{9,13},{10,... | collective-permute-start | bytes 393224 | tf_op jit(solution)/shard_map/ppermute | solution.py:26
  42.1 5.6 %collective-permute-start.11 = (bf16[4,128,128]{2,1,0:T(8,128)(2,1)}, bf16[4,128,128]{2,1,0:T(8,128)(2,1)S(1)}, u32[]{:S(2)}, u32[]{:S(2)}) collective-permute-start(bf16[4,128,128]{2,1,0:T(8,128)(2,1)} %get-tuple-element.60), channel_id=1, source_target_pairs={{0,2},{1,3},{2,0},{3,1},{4,6},{5,7},{6,4},{7,5},{8,10},{9,11},{10,... | collective-permute-start | bytes 393224 | tf_op jit(solution)/shard_map/ppermute | solution.py:26
  42.7 0.8 %copy-start.11 = (bf16[256,128]{1,0:T(8,128)(2,1)S(1)}, bf16[256,128]{1,0:T(8,128)(2,1)}, u32[]{:S(2)}) copy-start(bf16[256,128]{1,0:T(8,128)(2,1)} %w2_self.3) | copy-start | bytes 196612
  43.5 0.9 %copy-start.13 = (bf16[8,128,128]{2,1,0:T(8,128)(2,1)S(1)}, bf16[8,128,128]{2,1,0:T(8,128)(2,1)}, u32[]{:S(2)}) copy-start(bf16[8,128,128]{2,1,0:T(8,128)(2,1)} %copy-done.12) | copy-start | bytes 786436
  44.5 3.2 %copy-start.7 = (bf16[256,1024]{1,0:T(8,128)(2,1)S(1)}, bf16[256,1024]{1,0:T(8,128)(2,1)}, u32[]{:S(2)}) copy-start(bf16[256,1024]{1,0:T(8,128)(2,1)} %copy-done.6) | copy-start | bytes 1572868
  44.5 3.2 %copy-start.9 = (bf16[256,128]{1,0:T(8,128)(2,1)S(1)}, bf16[256,128]{1,0:T(8,128)(2,1)}, u32[]{:S(2)}) copy-start(bf16[256,128]{1,0:T(8,128)(2,1)} %refs_9_.3) | copy-start | bytes 196612
  47.7 0.7 copy-start.18
  50.6 1.5 %collective-permute-start.12 = (bf16[896,128]{1,0:T(8,128)(2,1)S(1)}, bf16[896,128]{1,0:T(8,128)(2,1)S(1)}, u32[]{:S(2)}, u32[]{:S(2)}) collective-permute-start(bf16[896,128]{1,0:T(8,128)(2,1)S(1)} %get-tuple-element.73), channel_id=1, source_target_pairs={{0,1},{1,0},{2,3},{3,2},{4,5},{5,4},{6,7},{7,6},{8,9},{9,8},{10,11... | collective-permute-start | bytes 688136 | tf_op jit(solution)/shard_map/ppermute | solution.py:26
  75.3 1.5 %collective-permute-start.13 = (bf16[896,128]{1,0:T(8,128)(2,1)S(1)}, bf16[896,128]{1,0:T(8,128)(2,1)S(1)}, u32[]{:S(2)}, u32[]{:S(2)}) collective-permute-start(bf16[896,128]{1,0:T(8,128)(2,1)S(1)} %bitcast.19), channel_id=1, source_target_pairs={{0,1},{1,0},{2,3},{3,2},{4,5},{5,4},{6,7},{7,6},{8,9},{9,8},{10,11... | collective-permute-start | bytes 688136 | tf_op jit(solution)/shard_map/ppermute | solution.py:26

commit v2 on v1

v2 whole, which is shorter than its diff:
```python
import functools

import jax
import jax.numpy as jnp
from jax import lax
from jax.experimental import pallas as pl
from jax.experimental.pallas import tpu as pltpu
from jax.sharding import PartitionSpec as P

AXES = ("dom", "sub", "feat")
CHIPS = ("dom", "sub")
SMEM = pl.BlockSpec(memory_space=pltpu.SMEM)
VMEM = pl.BlockSpec(memory_space=pltpu.VMEM)
VMEM_LIMIT = 8 * 2**20
F32 = jnp.float32
BF16 = jnp.bfloat16


def struct(shape, dtype):
    return jax.ShapeDtypeStruct(shape, dtype)


def swapped(value, mask):
    pairs = [(source, source ^ mask) for source in range(lax.axis_size(AXES))]
    return lax.ppermute(value, AXES, pairs)


def dot(a, b):
    return jnp.dot(a, b, preferred_element_type=F32)


def dot_bt(a, b):
    return lax.dot_general(a, b, (((1,), (1,)), ((), ())), preferred_element_type=F32)


def run(body, in_specs, out_specs, out_shape, scratch, args, flops=0, moved=0):
    return pl.pallas_call(
        body,
        in_specs=in_specs,
        out_specs=out_specs,
        out_shape=out_shape,
        scratch_shapes=scratch,
        compiler_params=pltpu.CompilerParams(vmem_limit_bytes=VMEM_LIMIT),
        cost_estimate=pl.CostEstimate(flops=flops, bytes_accessed=moved, transcendentals=0),
    )(*args)


class Table:
    def __init__(self, tiles, fan, rounds, slots):
        self.fan, self.slots = fan, slots
        self.where = tiles * fan
        self.dst = self.where + rounds * slots
        self.give = self.dst + rounds * slots
        self.feat = self.give + rounds * slots
        self.size = self.feat + 1

    def near_at(self, t, k):
        return t * self.fan + k

    def where_at(self, r, s):
        return self.where + r * self.slots + s

    def dst_at(self, r, s):
        return self.dst + r * self.slots + s

    def give_at(self, r, s):
        return self.give + r * self.slots + s


def stage_body(features, blocks, arrival):
    copy = pltpu.make_async_copy(features, blocks, arrival)
    copy.start()
    copy.wait()


def pick_body(rounds, *refs):
    partner_src = refs[:rounds]
    blocks = refs[rounds]
    outs = refs[rounds + 1 :]
    for r in range(rounds):
        for s in range(outs[r].shape[0]):
            outs[r][s] = blocks[partner_src[r][r, 0, s]]


def first_local_body(
    at, rounds, index, dst, count, feat, *refs
):
    partner_src = refs[:rounds]
    (features, values, edges, w1_self, bias, table, near, own, features_t, values_t,
     edges_t) = refs[rounds:]
    tiles, fan, size = values.shape[:3]
    slots = edges.shape[1]
    for t in range(tiles):
        for k in range(fan):
            table[at.near_at(t, k)] = index[k, t]
    for r in range(rounds):
        for s in range(slots):
            table[at.dst_at(r, s)] = dst[r, 0, s]
            table[at.where_at(r, s)] = jnp.where(s < count[0, r], dst[r, 0, s], tiles)
            table[at.give_at(r, s)] = partner_src[r][r, 0, s]
    table[at.feat] = feat[0]
    for t in range(tiles):
        left = jnp.concatenate([values[t, k] for k in range(fan)], axis=1)
        right = jnp.concatenate([features[index[k, t]] for k in range(fan)], axis=0)
        near[t] = dot(left, right)
        own[t] = dot(features[t], w1_self[...]) + bias[...]
        features_t[:, t * size : (t + 1) * size] = features[t].T
        for k in range(fan):
            values_t[t, k] = values[t, k].T
    for r in range(rounds):
        for s in range(slots):
            live = s < count[0, r]
            edges_t[r, s] = jnp.where(live, edges[r, s].T, jnp.zeros_like(edges[r, s]))


def add_boundary(at, total, table, edges, arrived):
    rounds, slots = edges.shape[0], edges.shape[1]
    for r in range(rounds):
        for s in range(slots):
            where = table[at.where_at(r, s)]
            total[where] = total[where] + dot(edges[r, s], arrived[r][s])


def first_body(at, rounds, table, *refs):
    arrived = refs[:rounds]
    edges, near, own, w1_near, w2_near, first_agg, hidden, message = refs[rounds : rounds + 8]
    sends = refs[rounds + 8 : 2 * rounds + 8]
    total = refs[-1]
    tiles = near.shape[0]
    total[0:tiles] = near[...]
    add_boundary(at, total, table, edges, arrived)
    for t in range(tiles):
        agg = total[t].astype(BF16)
        first_agg[t] = agg
        pre = own[t] + dot(agg, w1_near[...])
        act = (pre * jax.nn.sigmoid(pre)).astype(BF16)
        hidden[t] = act
        message[t] = dot(act, w2_near[...]).astype(BF16)
    for r in range(rounds):
        for s in range(sends[r].shape[0]):
            sends[r][s] = message[table[at.give_at(r, s)]]


def second_local_body(
    at, table, labels, values, first_agg, own, hidden, message, w1_near, w2_self, bias,
    slope, near, target, first_agg_t, hidden_t,
):
    tiles, fan = values.shape[0], values.shape[1]
    classes = w2_self.shape[1]
    class_ids = lax.broadcasted_iota(jnp.int32, (classes, 128), 0)
    for t in range(tiles):
        left = jnp.concatenate([values[t, k] for k in range(fan)], axis=1)
        right = jnp.concatenate([message[table[at.near_at(t, k)]] for k in range(fan)], axis=0)
        near[t] = dot(left, right) + dot(hidden[t], w2_self[...]) + bias[...]
        hot = (labels[t : t + 1, :] == class_ids).astype(F32)
        target[t] = hot.T
        pre = own[t] + dot(first_agg[t], w1_near[...])
        sig = jax.nn.sigmoid(pre)
        slope[t] = sig * (1.0 + pre * (1.0 - sig))
        first_agg_t[:, t * 128 : (t + 1) * 128] = first_agg[t].T
        hidden_t[:, t * 128 : (t + 1) * 128] = hidden[t].T


def second_body(at, rounds, table, *refs):
    arrived = refs[:rounds]
    edges, edges_t, near, target, logits, error = refs[rounds : rounds + 6]
    sends = refs[rounds + 6 : 2 * rounds + 6]
    total = refs[-1]
    tiles = near.shape[0]
    total[0:tiles] = near[...]
    add_boundary(at, total, table, edges, arrived)
    for t in range(tiles):
        pre = total[t]
        logits[t] = pre.astype(BF16)
        error[t] = (pre - target[t]).astype(BF16)
    for r in range(rounds):
        for s in range(sends[r].shape[0]):
            sends[r][s] = dot(edges_t[r, s], error[table[at.dst_at(r, s)]]).astype(BF16)


def back_local_body(
    at, table, values_t, error, hidden_t, w2_self, back, self_grad, grad_w2_self, grad_bias_two
):
    tiles, fan = values_t.shape[0], values_t.shape[1]
    back[...] = jnp.zeros_like(back)
    bias = jnp.zeros((1, error.shape[2]), F32)
    for t in range(tiles):
        rows = error[t]
        for k in range(fan):
            where = table[at.near_at(t, k)]
            back[where] = back[where] + dot(values_t[t, k], rows)
        self_grad[t] = dot_bt(rows, w2_self[...])
        bias = bias + jnp.sum(rows.astype(F32), axis=0, keepdims=True)
    grad_bias_two[...] = bias
    flat = error[...].reshape(tiles * error.shape[1], error.shape[2])
    grad_w2_self[...] = dot(hidden_t[...], flat)


def back_body(at, rounds, table, *refs):
    arrived = refs[:rounds]
    (back, self_grad, slope, w2_near, features_t, first_agg_t, hidden_t, grad_w2_self, grad_bias_two,
     hidden_grad, send, keep, total, back_16, first_grad, packed) = refs[rounds:]
    tiles, size, classes = back.shape
    width = self_grad.shape[2]
    total[...] = back[...]
    for r in range(rounds):
        for s in range(arrived[r].shape[0]):
            where = table[at.give_at(r, s)]
            total[where] = total[where] + arrived[r][s].astype(F32)
    bias = jnp.zeros((1, width), F32)
    for t in range(tiles):
        here = slice(t * size, (t + 1) * size)
        rows = total[t].astype(BF16)
        back_16[here, :] = rows
        full = self_grad[t] + dot_bt(rows, w2_near[...])
        hidden_grad[t] = full.astype(BF16)
        grad = (full * slope[t]).astype(BF16)
        first_grad[here, :] = grad
        bias = bias + jnp.sum(grad.astype(F32), axis=0, keepdims=True)
    deep = features_t.shape[0]
    row = 0
    for left in (features_t, first_agg_t):
        product = dot(left[...], first_grad[...])
        for c in range(width // 128):
            packed[row : row + deep, :] = product[:, c * 128 : (c + 1) * 128]
            row += deep
    packed[row : row + width, :] = grad_w2_self[...]
    row += width
    packed[row : row + width, :] = dot(hidden_t[...], back_16[...])
    row += width
    packed[row:, :] = jnp.zeros_like(packed[row:, :])
    for c in range(width // 128):
        packed[row + c : row + c + 1, :] = bias[:, c * 128 : (c + 1) * 128]
    row += width // 128
    packed[row : row + 1, :] = grad_bias_two[...]
    half = keep.shape[0]
    mine = table[at.feat]
    keep[...] = packed[pl.ds(pl.multiple_of(mine * half, 16), half), :]
    send[...] = packed[pl.ds(pl.multiple_of((1 - mine) * half, 16), half), :].astype(BF16)


def pair_body(keep, arrived, out):
    out[...] = (keep[...] + arrived[...].astype(F32)).astype(BF16)


def chips_body(arrived, out):
    chips = arrived.shape[0]
    total = arrived[0].astype(F32)
    for c in range(1, chips):
        total = total + arrived[c].astype(F32)
    total = total.astype(BF16)
    for c in range(chips):
        out[c] = total


def unpack_body(at, table, mine, other, g1_self, g1_near, g1_bias, g2_self, g2_near, g2_bias, packed):
    half = mine.shape[0]
    packed[pl.ds(pl.multiple_of(table[at.feat] * half, 16), half), :] = mine[...].astype(F32)
    packed[pl.ds(pl.multiple_of((1 - table[at.feat]) * half, 16), half), :] = other[...].astype(F32)
    deep, width = g1_self.shape
    row = 0
    for out in (g1_self, g1_near):
        for c in range(width // 128):
            out[:, c * 128 : (c + 1) * 128] = packed[row : row + deep, :]
            row += deep
    for out in (g2_self, g2_near):
        out[...] = packed[row : row + width, :]
        row += width
    for c in range(width // 128):
        g1_bias[:, c * 128 : (c + 1) * 128] = packed[row : row + 1, :]
        row += 1
    g2_bias[...] = packed[row : row + 1, :]


def shards(
    features,
    labels,
    local_index,
    local_values,
    cross_src,
    cross_dst,
    cross_count,
    cross_values,
    w1_self,
    w1_near,
    bias_one,
    w2_self,
    w2_near,
    bias_two,
):
    tiles, fan, size, _ = local_values.shape
    rounds, slots = cross_src.shape[1], cross_src.shape[2]
    width_in = features.shape[1]
    hidden_width = w1_self.shape[1]
    classes = w2_self.shape[1]
    nodes = tiles * size
    total_bits = lax.axis_size(AXES).bit_length() - 1
    masks = [1 << (total_bits - 1 - colour) for colour in range(rounds)]
    chips = lax.axis_size(CHIPS)
    blocks = features.reshape(tiles, size, width_in)
    edges = cross_values[0]
    feat = lax.axis_index("feat").astype(jnp.int32).reshape(1)
    bias_one_row = bias_one.reshape(1, hidden_width)
    bias_two_row = bias_two.reshape(1, classes)
    label_rows = labels.reshape(tiles, size)

    at = Table(tiles, fan, rounds, slots)

    reads = cross_src.transpose(1, 0, 2)
    partner_src = [swapped(reads, mask) for mask in masks]
    blocks = run(
        stage_body,
        [pl.BlockSpec(memory_space=pltpu.HBM)],
        VMEM,
        struct(blocks.shape, BF16),
        [pltpu.SemaphoreType.DMA],
        [blocks],
        moved=2 * nodes * width_in * 2,
    )
    picks = run(
        functools.partial(pick_body, rounds),
        [SMEM] * rounds + [VMEM],
        [VMEM] * rounds,
        [struct((slots, size, width_in), BF16)] * rounds,
        [],
        [*partner_src, blocks],
        moved=2 * rounds * slots * size * width_in * 2,
    )
    arrived = [swapped(tile, mask) for tile, mask in zip(picks, masks)]

    table, near, own, features_t, values_t, edges_t = run(
        functools.partial(first_local_body, at, rounds),
        [SMEM] * (4 + rounds) + [VMEM] * 5,
        [SMEM] + [VMEM] * 5,
        [
            struct((at.size,), jnp.int32),
            struct((tiles, size, width_in), F32),
            struct((tiles, size, hidden_width), F32),
            struct((width_in, nodes), BF16),
            struct(local_values.shape, BF16),
            struct(edges.shape, BF16),
        ],
        [],
        [
            local_index.T, cross_dst.transpose(1, 0, 2), cross_count, feat, *partner_src,
            blocks, local_values, edges, w1_self, bias_one_row,
        ],
        flops=2 * nodes * width_in * (fan * size + hidden_width),
        moved=8 * 2**20,
    )

    first_agg, hidden, message, *sends = run(
        functools.partial(first_body, at, rounds),
        [SMEM] + [VMEM] * (rounds + 5),
        [VMEM] * (3 + rounds),
        [
            struct((tiles, size, width_in), BF16),
            struct((tiles, size, hidden_width), BF16),
            struct((tiles, size, classes), BF16),
        ]
        + [struct((slots, size, classes), BF16)] * rounds,
        [pltpu.VMEM((tiles + 1, size, width_in), F32)],
        [table, *arrived, edges, near, own, w1_near, w2_near],
        flops=2 * nodes * width_in * (rounds * slots * size // tiles + hidden_width + classes),
        moved=8 * 2**20,
    )
    arrived = [swapped(tile, mask) for tile, mask in zip(sends, masks)]

    slope, near, target, first_agg_t, hidden_t = run(
        functools.partial(second_local_body, at),
        [SMEM] + [VMEM] * 9,
        [VMEM] * 5,
        [
            struct((tiles, size, hidden_width), F32),
            struct((tiles, size, classes), F32),
            struct((tiles, size, classes), F32),
            struct((width_in, nodes), BF16),
            struct((hidden_width, nodes), BF16),
        ],
        [],
        [table, label_rows, local_values, first_agg, own, hidden, message, w1_near, w2_self, bias_two_row],
        flops=2 * nodes * classes * (fan * size + 3 * hidden_width),
        moved=6 * 2**20,
    )

    logits, error, *sends = run(
        functools.partial(second_body, at, rounds),
        [SMEM] + [VMEM] * (rounds + 4),
        [VMEM] * (2 + rounds),
        [struct((tiles, size, classes), BF16), struct((tiles, size, classes), BF16)]
        + [struct((slots, size, classes), BF16)] * rounds,
        [pltpu.VMEM((tiles + 1, size, classes), F32)],
        [table, *arrived, edges, edges_t, near, target],
        flops=4 * rounds * slots * size * size * classes,
        moved=3 * 2**20,
    )
    arrived = [swapped(tile, mask) for tile, mask in zip(sends, masks)]

    back, self_grad, grad_w2_self, grad_bias_two = run(
        functools.partial(back_local_body, at),
        [SMEM] + [VMEM] * 4,
        [VMEM] * 4,
        [
            struct((tiles, size, classes), F32),
            struct((tiles, size, hidden_width), F32),
            struct((hidden_width, classes), F32),
            struct((1, classes), F32),
        ],
        [],
        [table, values_t, error, hidden_t, w2_self],
        flops=2 * nodes * classes * (fan * size + 2 * hidden_width),
        moved=4 * 2**20,
    )

    rows = (2 * width_in * hidden_width + 2 * hidden_width * classes + hidden_width + classes) // 128
    piece = -(-rows // (2 * chips * 16)) * 16
    half = piece * chips
    hidden_grad, send, keep = run(
        functools.partial(back_body, at, rounds),
        [SMEM] + [VMEM] * (rounds + 9),
        [VMEM] * 3,
        [
            struct((tiles, size, hidden_width), BF16),
            struct((half, 128), BF16),
            struct((half, 128), F32),
        ],
        [
            pltpu.VMEM((tiles, size, classes), F32),
            pltpu.VMEM((nodes, classes), BF16),
            pltpu.VMEM((nodes, hidden_width), BF16),
            pltpu.VMEM((2 * half, 128), F32),
        ],
        [
            table, *arrived, back, self_grad, slope, w2_near, features_t, first_agg_t,
            hidden_t, grad_w2_self, grad_bias_two,
        ],
        flops=2 * nodes * hidden_width * (2 * width_in + 2 * classes),
        moved=6 * 2**20,
    )

    pair = run(
        pair_body, [VMEM] * 2, VMEM, struct((half, 128), BF16), [],
        [keep, swapped(send, 1)], flops=half * 128, moved=half * 128 * 8,
    )
    pieces = lax.all_to_all(pair.reshape(chips, piece, 128), CHIPS, 0, 0)
    copies = run(
        chips_body, [VMEM], VMEM, struct((chips, piece, 128), BF16), [],
        [pieces], flops=half * 128, moved=half * 128 * 4,
    )
    mine = lax.all_to_all(copies, CHIPS, 0, 0).reshape(half, 128)
    other = swapped(mine, 1)
    g1_self, g1_near, g1_bias, g2_self, g2_near, g2_bias = run(
        functools.partial(unpack_body, at),
        [SMEM] + [VMEM] * 2,
        [VMEM] * 6,
        [
            struct((width_in, hidden_width), F32),
            struct((width_in, hidden_width), F32),
            struct((1, hidden_width), F32),
            struct((hidden_width, classes), F32),
            struct((hidden_width, classes), F32),
            struct((1, classes), F32),
        ],
        [pltpu.VMEM((2 * half, 128), F32)],
        [table, mine, other],
        moved=half * 128 * 12,
    )
    return (
        logits.reshape(nodes, classes),
        hidden_grad.reshape(nodes, hidden_width),
        g1_self,
        g1_near,
        g1_bias.reshape(hidden_width),
        g2_self,
        g2_near,
        g2_bias.reshape(classes),
    )


def solution(mesh):
    in_specs = (
        P(("grp", "dom", "sub", "feat"), None),
        P(("grp", "dom", "sub", "feat")),
        P(("grp", "dom", "sub", "feat"), None),
        P(("grp", "dom", "sub", "feat"), None, None, None),
        P(("grp", "dom", "sub", "feat"), None, None),
        P(("grp", "dom", "sub", "feat"), None, None),
        P(("grp", "dom", "sub", "feat"), None),
        P(("grp", "dom", "sub", "feat"), None, None, None, None),
        P(),
        P(),
        P(),
        P(),
        P(),
        P(),
    )
    out_specs = (
        P(("grp", "dom", "sub", "feat"), None),
        P(("grp", "dom", "sub", "feat"), None),
        P("grp", None),
        P("grp", None),
        P("grp"),
        P("grp", None),
        P("grp", None),
        P("grp"),
    )
    return jax.shard_map(shards, mesh=mesh, in_specs=in_specs, out_specs=out_specs, check_vma=False)
```

time: 78.3 us -> 73.7 us (0.941)
  local copies, waits for them, and re-layouts: 10.1 us -> 2.42 us
  waiting for transfers between devices: 14.8 us -> 17.5 us
    unnamed x53 -> x26, local copies, waits for them, and re-layouts: 10.1 us -> 2.42 us
    ppermute x14, waiting for transfers between devices: 14.8 us -> 17.5 us  [swapped(): return lax.ppermute(value, AXES, pairs)]
    pallas_call x10 -> x11, Pallas kernels: 12.5 us -> 13.1 us  [run(): pl.pallas_call(body, in_specs=in_specs, out_specs=out_specs, out_shape=ou...]
  transfers between devices with their start and end apart: 14 -> 14, of which waited for: 9 -> 9; matrix products, arithmetic and copies ran while one was open for 1% -> 0% of each run, Pallas kernels for 7% -> 7%
where the time goes in v2:
time: 73.7 us; the launch traced here: 73.4 us
  blocking collectives  22.7 us (31%)
  waiting for transfers between devices  17.5 us (24%)
  starting transfers between devices  16.9 us (23%)
  Pallas kernels  13.1 us (18%)
  local copies, waits for them, and re-layouts  2.42 us (3%)
  between operations  0.79 us (1%)
    ppermute x14, waiting for transfers between devices, swapped(): return lax.ppermute(value, AXES, pairs)  17.5 us
    ppermute x14, starting transfers between devices, swapped(): return lax.ppermute(value, AXES, pairs)  16.9 us
    pallas_call x11, Pallas kernels, run(): pl.pallas_call(body, in_specs=in_specs, out_specs=out_specs, out_shape=ou...  13.1 us
    all_to_all x1, blocking collectives, shards(): pieces = lax.all_to_all(pair.reshape(chips, piece, 128), CHIPS, 0, 0)  11.4 us
    all_to_all x1, blocking collectives, shards(): mine = lax.all_to_all(copies, CHIPS, 0, 0).reshape(half, 128)  11.3 us
    unnamed x26, local copies, waits for them, and re-layouts  2.42 us
  transfers between devices with their start and end apart: 14, of which 9 were waited for; matrix products, arithmetic and copies ran while one was open for 0% of the time, Pallas kernels for 7%

profile of v2, /device:TPU:0, one launch (start us, length us, event | category | flops | bytes accessed | tf_op | source)
XLA Modules:
  0.0 73.4 jit_solution(10278389000268380758)
XLA Ops:
  0.6 3.0 %collective-permute-start.2 = (s32[3,1,4]{2,1,0:T(1,128)}, s32[3,1,4]{2,1,0:T(1,128)S(1)}, u32[]{:S(2)}, u32[]{:S(2)}) collective-permute-start(s32[3,1,4]{2,1,0:T(1,128)} %bitcast.29), channel_id=1, source_target_pairs={{0,2},{1,3},{2,0},{3,1},{4,6},{5,7},{6,4},{7,5},{8,10},{9,11},{10,... | collective-permute-start | bytes 152 | tf_op jit(solution)/shard_map/ppermute | solution.py:25
  3.6 1.6 %collective-permute-start.1 = (s32[3,1,4]{2,1,0:T(1,128)}, s32[3,1,4]{2,1,0:T(1,128)S(1)}, u32[]{:S(2)}, u32[]{:S(2)}) collective-permute-start(s32[3,1,4]{2,1,0:T(1,128)} %bitcast.30), channel_id=1, source_target_pairs={{0,4},{1,5},{2,6},{3,7},{4,0},{5,1},{6,2},{7,3},{8,12},{9,13},{10,... | collective-permute-start | bytes 152 | tf_op jit(solution)/shard_map/ppermute | solution.py:25
  5.2 2.6 %collective-permute-start = (s32[3,1,4]{2,1,0:T(1,128)}, s32[3,1,4]{2,1,0:T(1,128)S(1)}, u32[]{:S(2)}, u32[]{:S(2)}) collective-permute-start(s32[3,1,4]{2,1,0:T(1,128)} %bitcast.31), channel_id=1, source_target_pairs={{0,8},{1,9},{2,10},{3,11},{4,12},{5,13},{6,14},{7,15},{8,0},{9,1},... | collective-permute-start | bytes 152 | tf_op jit(solution)/shard_map/ppermute | solution.py:25
  7.8 1.0 %copy-done.3 = bf16[1024,256]{1,0:T(8,128)(2,1)S(1)} copy-done((bf16[1024,256]{1,0:T(8,128)(2,1)S(1)}, bf16[1024,256]{1,0:T(8,128)(2,1)}, u32[]{:S(2)}) %copy-start.3) | copy-done | bytes 524312
  8.9 0.0 copy-start.1
  8.9 0.0 copy-start.6
  8.9 0.0 collective-permute-done.2.refs_2_
  8.9 0.0 collective-permute-done.1.refs_1_
  9.0 1.0 %collective-permute-done.refs_0_ = s32[3,1,4]{2,1,0:T(1,128)S(1)} collective-permute-done((s32[3,1,4]{2,1,0:T(1,128)}, s32[3,1,4]{2,1,0:T(1,128)S(1)}, u32[]{:S(2)}, u32[]{:S(2)}) %collective-permute-start) | collective-permute-done | bytes 80 | tf_op jit(solution)/shard_map/ppermute | solution.py:25
  9.9 1.4 %shard_map.199 = (bf16[4,128,256]{2,1,0:T(8,128)(2,1)}, bf16[4,128,256]{2,1,0:T(8,128)(2,1)S(1)}, bf16[4,128,256]{2,1,0:T(8,128)(2,1)S(1)}) custom-call(s32[3,1,4]{2,1,0:T(1,128)S(1)} %collective-permute-done.refs_0_, s32[3,1,4]{2,1,0:T(1,128)S(1)} %collective-permute-done.1.refs_1_, s32[3,1,4]{2,1,0:T(1,128)S(1)} %collective-permute-done.2.refs_2_, ...), custom_call_target="tpu_custom_call" | custom-call | bytes 1572864 | tf_op jit(solution)/shard_map/pallas_call | solution.py:37
  11.3 2.6 %collective-permute-start.3 = (bf16[4,128,256]{2,1,0:T(8,128)(2,1)}, bf16[4,128,256]{2,1,0:T(8,128)(2,1)S(1)}, u32[]{:S(2)}, u32[]{:S(2)}) collective-permute-start(bf16[4,128,256]{2,1,0:T(8,128)(2,1)} %get-tuple-element.47), channel_id=1, source_target_pairs={{0,8},{1,9},{2,10},{3,11},{4,12},{5,13},{6,14},{7,15},{8,0},{9,1},... | collective-permute-start | bytes 786440 | tf_op jit(solution)/shard_map/ppermute | solution.py:25
  13.9 0.4 collective-permute-start.4
  14.3 0.5 collective-permute-start.5
  14.9 0.0 copy-done.1
  14.9 0.6 copy-done.8
  15.5 0.0 copy-done.9
  15.6 1.9 %shard_map.198 = (s32[69]{0:T(128)S(1)}, f32[8,128,256]{2,1,0:T(8,128)S(1)}, f32[8,128,256]{2,1,0:T(8,128)S(1)}, bf16[256,1024]{1,0:T(8,128)(2,1)S(1)}, bf16[8,4...) custom-call(s32[4,8]{1,0:T(4,128)S(1)} %bitcast.23, s32[3,1,4]{2,1,0:T(1,128)S(1)} %bitcast.24, ...), custom_call_target="tpu_custom_call" | custom-call | flops 402653184 | bytes 8388608 | tf_op jit(solution)/shard_map/pallas_call | solution.py:37
  17.5 6.8 %collective-permute-done.3.refs_0_ = bf16[4,128,256]{2,1,0:T(8,128)(2,1)S(1)} collective-permute-done((bf16[4,128,256]{2,1,0:T(8,128)(2,1)}, bf16[4,128,256]{2,1,0:T(8,128)(2,1)S(1)}, u32[]{:S(2)}, u32[]{:S(2)}) %collective-permute-start.3) | collective-permute-done | bytes 262176 | tf_op jit(solution)/shard_map/ppermute | solution.py:25
  24.3 1.1 %collective-permute-done.4.refs_1_ = bf16[4,128,256]{2,1,0:T(8,128)(2,1)S(1)} collective-permute-done((bf16[4,128,256]{2,1,0:T(8,128)(2,1)S(1)}, bf16[4,128,256]{2,1,0:T(8,128)(2,1)S(1)}, u32[]{:S(2)}, u32[]{:S(2)}) %collective-permute-start.4) | collective-permute-done | bytes 262176 | tf_op jit(solution)/shard_map/ppermute | solution.py:25
  25.4 0.0 collective-permute-done.5.refs_2_
  25.4 0.0 copy-done.2
  25.5 0.0 copy-start.4
  25.5 1.5 %shard_map.200 = (bf16[8,128,256]{2,1,0:T(8,128)(2,1)S(1)}, bf16[8,128,256]{2,1,0:T(8,128)(2,1)S(1)}, bf16[8,128,128]{2,1,0:T(8,128)(2,1)S(1)}, bf16[4,128,128]{...) custom-call(s32[69]{0:T(128)S(1)} %get-tuple-element.46.table, ...), custom_call_target="tpu_custom_call" | custom-call | flops 301989888 | bytes 8388608 | tf_op jit(solution)/shard_map/pallas_call | solution.py:37
  27.0 0.1 collective-permute-start.6
  27.1 2.0 %collective-permute-start.7 = (bf16[4,128,128]{2,1,0:T(8,128)(2,1)S(1)}, bf16[4,128,128]{2,1,0:T(8,128)(2,1)S(1)}, u32[]{:S(2)}, u32[]{:S(2)}) collective-permute-start(bf16[4,128,128]{2,1,0:T(8,128)(2,1)S(1)} %get-tuple-element.53), channel_id=1, source_target_pairs={{0,4},{1,5},{2,6},{3,7},{4,0},{5,1},{6,2},{7,3},{8,12},{9,13},{10,... | collective-permute-start | bytes 393224 | tf_op jit(solution)/shard_map/ppermute | solution.py:25
  29.0 0.5 collective-permute-start.8
  29.6 0.7 copy-done.7
  30.3 1.5 %shard_map.201 = (f32[8,128,256]{2,1,0:T(8,128)S(1)}, f32[8,128,128]{2,1,0:T(8,128)S(1)}, f32[8,128,128]{2,1,0:T(8,128)S(1)}, bf16[256,1024]{1,0:T(8,128)(2,1)S(1)}, bf16[256,1024]{1,0:T(8,128)(2,1)S(1)}) custom-call(s32[69]{0:T(128)S(1)} %get-tuple-element.46.table, s32[8,128]{1,0:T(8,128)S(1)} %bitcast.22, bf16[8,4,128,128]{3,2,1,0:T(8,128)(2,1)S(1)} %copy-done, ...), custom_call_target="tpu_custom_call" | custom-call | flops 335544320 | bytes 6291456 | tf_op jit(solution)/shard_map/pallas_call | solution.py:37
  31.7 2.6 %collective-permute-done.6.refs_0_ = bf16[4,128,128]{2,1,0:T(8,128)(2,1)S(1)} collective-permute-done((bf16[4,128,128]{2,1,0:T(8,128)(2,1)S(1)}, bf16[4,128,128]{2,1,0:T(8,128)(2,1)S(1)}, u32[]{:S(2)}, u32[]{:S(2)}) %collective-permute-start.6) | collective-permute-done | bytes 131104 | tf_op jit(solution)/shard_map/ppermute | solution.py:25
  34.3 0.0 collective-permute-done.7.refs_1_
  34.3 0.0 collective-permute-done.8.refs_2_
  34.3 1.6 %shard_map.202 = (bf16[8,128,128]{2,1,0:T(8,128)(2,1)}, bf16[8,128,128]{2,1,0:T(8,128)(2,1)S(1)}, bf16[4,128,128]{2,1,0:T(8,128)(2,1)S(1)}, bf16[4,128,128]{2,1,0:T(8,128)(2,1)S(1)}, bf16[4,128,128]{2,1,0:T(8,128)(2,1)S(1)}) custom-call(s32[69]{0:T(128)S(1)} %get-tuple-element.46.table, bf16[4,128,128]{2,1,0:T(8,128)(2,1)S(1)} %collective-permute-done.6.refs_0_, ...), custom_call_target="tpu_custom_call" | custom-call | flops 100663296 | bytes 3145728 | tf_op jit(solution)/shard_map/pallas_call | solution.py:37
  36.0 1.2 %collective-permute-start.9 = (bf16[4,128,128]{2,1,0:T(8,128)(2,1)S(1)}, bf16[4,128,128]{2,1,0:T(8,128)(2,1)S(1)}, u32[]{:S(2)}, u32[]{:S(2)}) collective-permute-start(bf16[4,128,128]{2,1,0:T(8,128)(2,1)S(1)} %get-tuple-element.62), channel_id=1, source_target_pairs={{0,8},{1,9},{2,10},{3,11},{4,12},{5,13},{6,14},{7,15},{8,0},{9,1},... | collective-permute-start | bytes 393224 | tf_op jit(solution)/shard_map/ppermute | solution.py:25
  37.2 1.8 %collective-permute-start.10 = (bf16[4,128,128]{2,1,0:T(8,128)(2,1)S(1)}, bf16[4,128,128]{2,1,0:T(8,128)(2,1)S(1)}, u32[]{:S(2)}, u32[]{:S(2)}) collective-permute-start(bf16[4,128,128]{2,1,0:T(8,128)(2,1)S(1)} %get-tuple-element.63), channel_id=1, source_target_pairs={{0,4},{1,5},{2,6},{3,7},{4,0},{5,1},{6,2},{7,3},{8,12},{9,13},{10,... | collective-permute-start | bytes 393224 | tf_op jit(solution)/shard_map/ppermute | solution.py:25
  39.0 0.5 collective-permute-start.11
  39.5 1.4 %shard_map.203 = (f32[8,128,128]{2,1,0:T(8,128)S(1)}, f32[8,128,256]{2,1,0:T(8,128)S(1)}, f32[256,128]{1,0:T(8,128)S(1)}, f32[1,128]{1,0:T(1,128)S(1)}) custom-call(s32[69]{0:T(128)S(1)} %get-tuple-element.46.table, bf16[8,4,128,128]{3,2,1,0:T(8,128)(2,1)S(1)} %get-tuple-element.65.values_t, bf16[8,128,128]{2,1,0:T(8,128)(2,1)S(1)} %get-tuple-element.66.error, ...), custom_call_target="tpu_custom_call" | custom-call | flops 268435456 | bytes 4194304 | tf_op jit(solution)/shard_map/pallas_call | solution.py:37
  40.9 2.3 %collective-permute-done.9.refs_0_ = bf16[4,128,128]{2,1,0:T(8,128)(2,1)S(1)} collective-permute-done((bf16[4,128,128]{2,1,0:T(8,128)(2,1)S(1)}, bf16[4,128,128]{2,1,0:T(8,128)(2,1)S(1)}, u32[]{:S(2)}, u32[]{:S(2)}) %collective-permute-start.9) | collective-permute-done | bytes 131104 | tf_op jit(solution)/shard_map/ppermute | solution.py:25
  43.2 0.2 collective-permute-done.10.refs_1_
  43.4 0.6 collective-permute-done.11.refs_2_
  44.0 2.2 %shard_map.204 = (bf16[8,128,256]{2,1,0:T(8,128)(2,1)}, bf16[896,128]{1,0:T(8,128)(2,1)S(1)}, f32[896,128]{1,0:T(8,128)S(1)}) custom-call(s32[69]{0:T(128)S(1)} %get-tuple-element.46.table, bf16[4,128,128]{2,1,0:T(8,128)(2,1)S(1)} %collective-permute-done.9.refs_0_, bf16[4,128,128]{2,1,0:T(8,128)(2,1)S(1)} %collective-permute-done.10.refs_1_, ...), custom_call_target="tpu_custom_call" | custom-call | flops 402653184 | bytes 6291456 | tf_op jit(solution)/shard_map/pallas_call | solution.py:37
  46.1 0.0 collective-permute-start.12
  46.1 1.5 %collective-permute-done.12.arrived = bf16[896,128]{1,0:T(8,128)(2,1)S(1)} collective-permute-done((bf16[896,128]{1,0:T(8,128)(2,1)S(1)}, bf16[896,128]{1,0:T(8,128)(2,1)S(1)}, u32[]{:S(2)}, u32[]{:S(2)}) %collective-permute-start.12) | collective-permute-done | bytes 229408 | tf_op jit(solution)/shard_map/ppermute | solution.py:25
  47.6 0.1 shard_map.205
  47.7 11.4 %all_to_all.10.arrived = bf16[8,112,128]{2,1,0:T(8,128)(2,1)S(1)} all-to-all(bf16[8,112,128]{2,1,0:T(8,128)(2,1)S(1)} %bitcast.18), channel_id=1, replica_groups=mesh['grp'=2,'dom'=4,'sub'=2,'feat'=2] {'dom','sub'}, dimensions={0} | all-to-all | bytes 458752 | tf_op jit(solution)/shard_map/all_to_all | solution.py:445
  59.1 11.3 %all_to_all.11 = bf16[8,112,128]{2,1,0:T(8,128)(2,1)S(1)} all-to-all(bf16[8,112,128]{2,1,0:T(8,128)(2,1)S(1)} %shard_map.206), channel_id=1, replica_groups=mesh['grp'=2,'dom'=4,'sub'=2,'feat'=2] {'dom','sub'}, dimensions={0} | all-to-all | bytes 458752 | tf_op jit(solution)/shard_map/all_to_all | solution.py:450
  70.4 0.0 collective-permute-start.13
  70.4 1.5 %collective-permute-done.13.other = bf16[896,128]{1,0:T(8,128)(2,1)S(1)} collective-permute-done((bf16[896,128]{1,0:T(8,128)(2,1)S(1)}, bf16[896,128]{1,0:T(8,128)(2,1)S(1)}, u32[]{:S(2)}, u32[]{:S(2)}) %collective-permute-start.13) | collective-permute-done | bytes 229408 | tf_op jit(solution)/shard_map/ppermute | solution.py:25
  71.9 1.5 %shard_map.207 = (f32[256,256]{1,0:T(8,128)}, f32[256,256]{1,0:T(8,128)}, f32[1,256]{1,0:T(1,128)}, f32[256,128]{1,0:T(8,128)}, f32[256,128]{1,0:T(8,128)}, /*index=5*/f32[1,128]{1,0:T(1,128)}) custom-call(s32[69]{0:T(128)S(1)} %get-tuple-element.46.table, bf16[896,128]{1,0:T(8,128)(2,1)S(1)} %bitcast.20, bf16[896,128]{1,0:T(8,128)(2,1)S(1)} %collective-permute-done.13.other), custom_call_target="tpu_custom_call" | custom-call | bytes 1376256 | tf_op jit(solution)/shard_map/pallas_call | solution.py:37
  (19 shorter events, 0.1 us)
Async XLA Ops:
  0.6 14.2 %copy-start = (bf16[8,4,128,128]{3,2,1,0:T(8,128)(2,1)S(1)}, bf16[8,4,128,128]{3,2,1,0:T(8,128)(2,1)}, u32[]{:S(2)}) copy-start(bf16[8,4,128,128]{3,2,1,0:T(8,128)(2,1)} %values.1) | copy-start | bytes 3145732
  0.6 8.3 %collective-permute-start.2 = (s32[3,1,4]{2,1,0:T(1,128)}, s32[3,1,4]{2,1,0:T(1,128)S(1)}, u32[]{:S(2)}, u32[]{:S(2)}) collective-permute-start(s32[3,1,4]{2,1,0:T(1,128)} %bitcast.29), channel_id=1, source_target_pairs={{0,2},{1,3},{2,0},{3,1},{4,6},{5,7},{6,4},{7,5},{8,10},{9,11},{10,... | collective-permute-start | bytes 152 | tf_op jit(solution)/shard_map/ppermute | solution.py:25
  3.6 5.3 %collective-permute-start.1 = (s32[3,1,4]{2,1,0:T(1,128)}, s32[3,1,4]{2,1,0:T(1,128)S(1)}, u32[]{:S(2)}, u32[]{:S(2)}) collective-permute-start(s32[3,1,4]{2,1,0:T(1,128)} %bitcast.30), channel_id=1, source_target_pairs={{0,4},{1,5},{2,6},{3,7},{4,0},{5,1},{6,2},{7,3},{8,12},{9,13},{10,... | collective-permute-start | bytes 152 | tf_op jit(solution)/shard_map/ppermute | solution.py:25
  5.2 4.7 %collective-permute-start = (s32[3,1,4]{2,1,0:T(1,128)}, s32[3,1,4]{2,1,0:T(1,128)S(1)}, u32[]{:S(2)}, u32[]{:S(2)}) collective-permute-start(s32[3,1,4]{2,1,0:T(1,128)} %bitcast.31), channel_id=1, source_target_pairs={{0,8},{1,9},{2,10},{3,11},{4,12},{5,13},{6,14},{7,15},{8,0},{9,1},... | collective-permute-start | bytes 152 | tf_op jit(solution)/shard_map/ppermute | solution.py:25
  7.8 1.0 %copy-start.3 = (bf16[1024,256]{1,0:T(8,128)(2,1)S(1)}, bf16[1024,256]{1,0:T(8,128)(2,1)}, u32[]{:S(2)}) copy-start(bf16[1024,256]{1,0:T(8,128)(2,1)} %param.14) | copy-start | bytes 1572868
  8.9 6.0 %copy-start.1 = (bf16[1,3,4,128,128]{4,3,2,1,0:T(8,128)(2,1)S(1)}, bf16[1,3,4,128,128]{4,3,2,1,0:T(8,128)(2,1)}, u32[]{:S(2)}) copy-start(bf16[1,3,4,128,128]{4,3,2,1,0:T(8,128)(2,1)} %param.21) | copy-start | bytes 1179652
  8.9 5.9 %copy-start.6 = (bf16[256,256]{1,0:T(8,128)(2,1)S(1)}, bf16[256,256]{1,0:T(8,128)(2,1)}, u32[]{:S(2)}) copy-start(bf16[256,256]{1,0:T(8,128)(2,1)} %refs_6_.3) | copy-start | bytes 393220
  11.3 13.1 %collective-permute-start.3 = (bf16[4,128,256]{2,1,0:T(8,128)(2,1)}, bf16[4,128,256]{2,1,0:T(8,128)(2,1)S(1)}, u32[]{:S(2)}, u32[]{:S(2)}) collective-permute-start(bf16[4,128,256]{2,1,0:T(8,128)(2,1)} %get-tuple-element.47), channel_id=1, source_target_pairs={{0,8},{1,9},{2,10},{3,11},{4,12},{5,13},{6,14},{7,15},{8,0},{9,1},... | collective-permute-start | bytes 786440 | tf_op jit(solution)/shard_map/ppermute | solution.py:25
  13.9 1.0 %copy-start.10 = (f32[256]{0:T(256)S(1)}, f32[256]{0:T(256)}, u32[]{:S(2)}) copy-start(f32[256]{0:T(256)} %param.24) | copy-start | bytes 3076
  13.9 1.0 %copy-start.11 = (s32[1,3]{1,0:T(1,128)S(1)}, s32[1,3]{1,0:T(1,128)}, u32[]{:S(2)}) copy-start(s32[1,3]{1,0:T(1,128)} %count.1) | copy-start | bytes 40
  13.9 11.6 %collective-permute-start.4 = (bf16[4,128,256]{2,1,0:T(8,128)(2,1)S(1)}, bf16[4,128,256]{2,1,0:T(8,128)(2,1)S(1)}, u32[]{:S(2)}, u32[]{:S(2)}) collective-permute-start(bf16[4,128,256]{2,1,0:T(8,128)(2,1)S(1)} %get-tuple-element.48), channel_id=1, source_target_pairs={{0,4},{1,5},{2,6},{3,7},{4,0},{5,1},{6,2},{7,3},{8,12},{9,13},{10,... | collective-permute-start | bytes 786440 | tf_op jit(solution)/shard_map/ppermute | solution.py:25
  14.3 11.1 %collective-permute-start.5 = (bf16[4,128,256]{2,1,0:T(8,128)(2,1)S(1)}, bf16[4,128,256]{2,1,0:T(8,128)(2,1)S(1)}, u32[]{:S(2)}, u32[]{:S(2)}) collective-permute-start(bf16[4,128,256]{2,1,0:T(8,128)(2,1)S(1)} %get-tuple-element.49), channel_id=1, source_target_pairs={{0,2},{1,3},{2,0},{3,1},{4,6},{5,7},{6,4},{7,5},{8,10},{9,11},{10,... | collective-permute-start | bytes 786440 | tf_op jit(solution)/shard_map/ppermute | solution.py:25
  14.9 0.7 copy-start.8
  14.9 0.7 copy-start.9
  15.5 9.9 %copy-start.2 = (bf16[256,256]{1,0:T(8,128)(2,1)S(1)}, bf16[256,256]{1,0:T(8,128)(2,1)}, u32[]{:S(2)}) copy-start(bf16[256,256]{1,0:T(8,128)(2,1)} %w1_near.1) | copy-start | bytes 393220
  15.6 9.9 %copy-start.5 = (bf16[256,128]{1,0:T(8,128)(2,1)S(1)}, bf16[256,128]{1,0:T(8,128)(2,1)}, u32[]{:S(2)}) copy-start(bf16[256,128]{1,0:T(8,128)(2,1)} %refs_6_.5) | copy-start | bytes 196612
  25.5 4.1 %copy-start.4 = (bf16[256,128]{1,0:T(8,128)(2,1)S(1)}, bf16[256,128]{1,0:T(8,128)(2,1)}, u32[]{:S(2)}) copy-start(bf16[256,128]{1,0:T(8,128)(2,1)} %w2_self.3) | copy-start | bytes 196612
  27.0 7.3 %collective-permute-start.6 = (bf16[4,128,128]{2,1,0:T(8,128)(2,1)S(1)}, bf16[4,128,128]{2,1,0:T(8,128)(2,1)S(1)}, u32[]{:S(2)}, u32[]{:S(2)}) collective-permute-start(bf16[4,128,128]{2,1,0:T(8,128)(2,1)S(1)} %get-tuple-element.52), channel_id=1, source_target_pairs={{0,8},{1,9},{2,10},{3,11},{4,12},{5,13},{6,14},{7,15},{8,0},{9,1},... | collective-permute-start | bytes 393224 | tf_op jit(solution)/shard_map/ppermute | solution.py:25
  27.1 7.3 %collective-permute-start.7 = (bf16[4,128,128]{2,1,0:T(8,128)(2,1)S(1)}, bf16[4,128,128]{2,1,0:T(8,128)(2,1)S(1)}, u32[]{:S(2)}, u32[]{:S(2)}) collective-permute-start(bf16[4,128,128]{2,1,0:T(8,128)(2,1)S(1)} %get-tuple-element.53), channel_id=1, source_target_pairs={{0,4},{1,5},{2,6},{3,7},{4,0},{5,1},{6,2},{7,3},{8,12},{9,13},{10,... | collective-permute-start | bytes 393224 | tf_op jit(solution)/shard_map/ppermute | solution.py:25
  29.0 5.3 %collective-permute-start.8 = (bf16[4,128,128]{2,1,0:T(8,128)(2,1)S(1)}, bf16[4,128,128]{2,1,0:T(8,128)(2,1)S(1)}, u32[]{:S(2)}, u32[]{:S(2)}) collective-permute-start(bf16[4,128,128]{2,1,0:T(8,128)(2,1)S(1)} %get-tuple-element.54), channel_id=1, source_target_pairs={{0,2},{1,3},{2,0},{3,1},{4,6},{5,7},{6,4},{7,5},{8,10},{9,11},{10,... | collective-permute-start | bytes 393224 | tf_op jit(solution)/shard_map/ppermute | solution.py:25
  29.6 0.7 copy-start.7
  29.6 0.7 copy-start.12
  36.0 7.2 %collective-permute-start.9 = (bf16[4,128,128]{2,1,0:T(8,128)(2,1)S(1)}, bf16[4,128,128]{2,1,0:T(8,128)(2,1)S(1)}, u32[]{:S(2)}, u32[]{:S(2)}) collective-permute-start(bf16[4,128,128]{2,1,0:T(8,128)(2,1)S(1)} %get-tuple-element.62), channel_id=1, source_target_pairs={{0,8},{1,9},{2,10},{3,11},{4,12},{5,13},{6,14},{7,15},{8,0},{9,1},... | collective-permute-start | bytes 393224 | tf_op jit(solution)/shard_map/ppermute | solution.py:25
  37.2 6.2 %collective-permute-start.10 = (bf16[4,128,128]{2,1,0:T(8,128)(2,1)S(1)}, bf16[4,128,128]{2,1,0:T(8,128)(2,1)S(1)}, u32[]{:S(2)}, u32[]{:S(2)}) collective-permute-start(bf16[4,128,128]{2,1,0:T(8,128)(2,1)S(1)} %get-tuple-element.63), channel_id=1, source_target_pairs={{0,4},{1,5},{2,6},{3,7},{4,0},{5,1},{6,2},{7,3},{8,12},{9,13},{10,... | collective-permute-start | bytes 393224 | tf_op jit(solution)/shard_map/ppermute | solution.py:25
  39.0 5.0 %collective-permute-start.11 = (bf16[4,128,128]{2,1,0:T(8,128)(2,1)S(1)}, bf16[4,128,128]{2,1,0:T(8,128)(2,1)S(1)}, u32[]{:S(2)}, u32[]{:S(2)}) collective-permute-start(bf16[4,128,128]{2,1,0:T(8,128)(2,1)S(1)} %get-tuple-element.64), channel_id=1, source_target_pairs={{0,2},{1,3},{2,0},{3,1},{4,6},{5,7},{6,4},{7,5},{8,10},{9,11},{10,... | collective-permute-start | bytes 393224 | tf_op jit(solution)/shard_map/ppermute | solution.py:25
  46.1 1.5 %collective-permute-start.12 = (bf16[896,128]{1,0:T(8,128)(2,1)S(1)}, bf16[896,128]{1,0:T(8,128)(2,1)S(1)}, u32[]{:S(2)}, u32[]{:S(2)}) collective-permute-start(bf16[896,128]{1,0:T(8,128)(2,1)S(1)} %get-tuple-element.77), channel_id=1, source_target_pairs={{0,1},{1,0},{2,3},{3,2},{4,5},{5,4},{6,7},{7,6},{8,9},{9,8},{10,11... | collective-permute-start | bytes 688136 | tf_op jit(solution)/shard_map/ppermute | solution.py:25
  70.4 1.5 %collective-permute-start.13 = (bf16[896,128]{1,0:T(8,128)(2,1)S(1)}, bf16[896,128]{1,0:T(8,128)(2,1)S(1)}, u32[]{:S(2)}, u32[]{:S(2)}) collective-permute-start(bf16[896,128]{1,0:T(8,128)(2,1)S(1)} %bitcast.19), channel_id=1, source_target_pairs={{0,1},{1,0},{2,3},{3,2},{4,5},{5,4},{6,7},{7,6},{8,9},{9,8},{10,11... | collective-permute-start | bytes 688136 | tf_op jit(solution)/shard_map/ppermute | solution.py:25

commit v3 on v2

--- a/solution.py
+++ b/solution.py
@@ -51,8 +51,7 @@
         self.where = tiles * fan
         self.dst = self.where + rounds * slots
         self.give = self.dst + rounds * slots
-        self.feat = self.give + rounds * slots
-        self.size = self.feat + 1
+        self.size = self.give + rounds * slots
 
     def near_at(self, t, k):
         return t * self.fan + k
@@ -83,7 +82,7 @@
 
 
 def first_local_body(
-    at, rounds, index, dst, count, feat, *refs
+    at, rounds, index, dst, count, *refs
 ):
     partner_src = refs[:rounds]
     (features, values, edges, w1_self, bias, table, near, own, features_t, values_t,
@@ -98,7 +97,6 @@
             table[at.dst_at(r, s)] = dst[r, 0, s]
             table[at.where_at(r, s)] = jnp.where(s < count[0, r], dst[r, 0, s], tiles)
             table[at.give_at(r, s)] = partner_src[r][r, 0, s]
-    table[at.feat] = feat[0]
     for t in range(tiles):
         left = jnp.concatenate([values[t, k] for k in range(fan)], axis=1)
         right = jnp.concatenate([features[index[k, t]] for k in range(fan)], axis=0)
@@ -163,7 +161,7 @@
 
 def second_body(at, rounds, table, *refs):
     arrived = refs[:rounds]
-    edges, edges_t, near, target, logits, error = refs[rounds : rounds + 6]
+    edges, edges_t, near, target, scores, error = refs[rounds : rounds + 6]
     sends = refs[rounds + 6 : 2 * rounds + 6]
     total = refs[-1]
     tiles = near.shape[0]
@@ -171,7 +169,7 @@
     add_boundary(at, total, table, edges, arrived)
     for t in range(tiles):
         pre = total[t]
-        logits[t] = pre.astype(BF16)
+        scores[t] = pre.astype(BF16)
         error[t] = (pre - target[t]).astype(BF16)
     for r in range(rounds):
         for s in range(sends[r].shape[0]):
@@ -179,8 +177,10 @@
 
 
 def back_local_body(
-    at, table, values_t, error, hidden_t, w2_self, back, self_grad, grad_w2_self, grad_bias_two
+    at, table, values_t, scores, error, hidden_t, w2_self,
+    logits, back, self_grad, grad_w2_self, grad_bias_two,
 ):
+    logits[...] = scores[...]
     tiles, fan = values_t.shape[0], values_t.shape[1]
     back[...] = jnp.zeros_like(back)
     bias = jnp.zeros((1, error.shape[2]), F32)
@@ -234,9 +234,13 @@
     row += width // 128
     packed[row : row + 1, :] = grad_bias_two[...]
     half = keep.shape[0]
-    mine = table[at.feat]
+    mine = lax.axis_index("feat")
     keep[...] = packed[pl.ds(pl.multiple_of(mine * half, 16), half), :]
     send[...] = packed[pl.ds(pl.multiple_of((1 - mine) * half, 16), half), :].astype(BF16)
+
+
+def leave_body(value, out):
+    out[...] = value[...]
 
 
 def pair_body(keep, arrived, out):
@@ -253,10 +257,11 @@
         out[c] = total
 
 
-def unpack_body(at, table, mine, other, g1_self, g1_near, g1_bias, g2_self, g2_near, g2_bias, packed):
+def unpack_body(mine, other, g1_self, g1_near, g1_bias, g2_self, g2_near, g2_bias, packed):
     half = mine.shape[0]
-    packed[pl.ds(pl.multiple_of(table[at.feat] * half, 16), half), :] = mine[...].astype(F32)
-    packed[pl.ds(pl.multiple_of((1 - table[at.feat]) * half, 16), half), :] = other[...].astype(F32)
+    feat = lax.axis_index("feat")
+    packed[pl.ds(pl.multiple_of(feat * half, 16), half), :] = mine[...].astype(F32)
+    packed[pl.ds(pl.multiple_of((1 - feat) * half, 16), half), :] = other[...].astype(F32)
     deep, width = g1_self.shape
     row = 0
     for out in (g1_self, g1_near):
@@ -299,7 +304,6 @@
     chips = lax.axis_size(CHIPS)
     blocks = features.reshape(tiles, size, width_in)
     edges = cross_values[0]
-    feat = lax.axis_index("feat").astype(jnp.int32).reshape(1)
     bias_one_row = bias_one.reshape(1, hidden_width)
     bias_two_row = bias_two.reshape(1, classes)
     label_rows = labels.reshape(tiles, size)
@@ -330,7 +334,7 @@
 
     table, near, own, features_t, values_t, edges_t = run(
         functools.partial(first_local_body, at, rounds),
-        [SMEM] * (4 + rounds) + [VMEM] * 5,
+        [SMEM] * (3 + rounds) + [VMEM] * 5,
         [SMEM] + [VMEM] * 5,
         [
             struct((at.size,), jnp.int32),
@@ -342,7 +346,7 @@
         ],
         [],
         [
-            local_index.T, cross_dst.transpose(1, 0, 2), cross_count, feat, *partner_src,
+            local_index.T, cross_dst.transpose(1, 0, 2), cross_count, *partner_src,
             blocks, local_values, edges, w1_self, bias_one_row,
         ],
         flops=2 * nodes * width_in * (fan * size + hidden_width),
@@ -383,7 +387,7 @@
         moved=6 * 2**20,
     )
 
-    logits, error, *sends = run(
+    scores, error, *sends = run(
         functools.partial(second_body, at, rounds),
         [SMEM] + [VMEM] * (rounds + 4),
         [VMEM] * (2 + rounds),
@@ -396,18 +400,19 @@
     )
     arrived = [swapped(tile, mask) for tile, mask in zip(sends, masks)]
 
-    back, self_grad, grad_w2_self, grad_bias_two = run(
+    logits, back, self_grad, grad_w2_self, grad_bias_two = run(
         functools.partial(back_local_body, at),
-        [SMEM] + [VMEM] * 4,
-        [VMEM] * 4,
-        [
+        [SMEM] + [VMEM] * 5,
+        [VMEM] * 5,
+        [
+            struct((tiles, size, classes), BF16),
             struct((tiles, size, classes), F32),
             struct((tiles, size, hidden_width), F32),
             struct((hidden_width, classes), F32),
             struct((1, classes), F32),
         ],
         [],
-        [table, values_t, error, hidden_t, w2_self],
+        [table, values_t, scores, error, hidden_t, w2_self],
         flops=2 * nodes * classes * (fan * size + 2 * hidden_width),
         moved=4 * 2**20,
     )
@@ -438,9 +443,15 @@
         moved=6 * 2**20,
     )
 
+    arrived = swapped(send, 1)
+    hidden_grad = run(
+        leave_body, [VMEM], VMEM, struct(hidden_grad.shape, BF16), [],
+        [hidden_grad], moved=4 * nodes * hidden_width,
+    )
+
     pair = run(
         pair_body, [VMEM] * 2, VMEM, struct((half, 128), BF16), [],
-        [keep, swapped(send, 1)], flops=half * 128, moved=half * 128 * 8,
+        [keep, arrived], flops=half * 128, moved=half * 128 * 8,
     )
     pieces = lax.all_to_all(pair.reshape(chips, piece, 128), CHIPS, 0, 0)
     copies = run(
@@ -450,8 +461,8 @@
     mine = lax.all_to_all(copies, CHIPS, 0, 0).reshape(half, 128)
     other = swapped(mine, 1)
     g1_self, g1_near, g1_bias, g2_self, g2_near, g2_bias = run(
-        functools.partial(unpack_body, at),
-        [SMEM] + [VMEM] * 2,
+        unpack_body,
+        [VMEM] * 2,
         [VMEM] * 6,
         [
             struct((width_in, hidden_width), F32),
@@ -462,7 +473,7 @@
             struct((1, classes), F32),
         ],
         [pltpu.VMEM((2 * half, 128), F32)],
-        [table, mine, other],
+        [mine, other],
         moved=half * 128 * 12,
     )
     return (

time: 73.7 us -> 71.4 us (0.969)
  waiting for transfers between devices: 17.5 us -> 16.1 us
  Pallas kernels: 13.1 us -> 12.3 us
    ppermute x14, waiting for transfers between devices: 17.5 us -> 16.1 us  [swapped(): return lax.ppermute(value, AXES, pairs)]
    pallas_call x11 -> x12, Pallas kernels: 13.1 us -> 12.3 us  [run(): pl.pallas_call(body, in_specs=in_specs, out_specs=out_specs, out_shape=ou...]
  transfers between devices with their start and end apart: 14 -> 14, of which waited for: 9 -> 9; matrix products, arithmetic and copies ran while one was open for 0% -> 0% of each run, Pallas kernels for 7% -> 9%
where the time goes in v3:
time: 71.4 us; the launch traced here: 71.1 us
  blocking collectives  22.7 us (32%)
  starting transfers between devices  16.7 us (23%)
  waiting for transfers between devices  16.1 us (23%)
  Pallas kernels  12.3 us (17%)
  local copies, waits for them, and re-layouts  2.42 us (3%)
  between operations  0.8 us (1%)
    ppermute x14, starting transfers between devices, swapped(): return lax.ppermute(value, AXES, pairs)  16.7 us
    ppermute x14, waiting for transfers between devices, swapped(): return lax.ppermute(value, AXES, pairs)  16.1 us
    pallas_call x12, Pallas kernels, run(): pl.pallas_call(body, in_specs=in_specs, out_specs=out_specs, out_shape=ou...  12.3 us
    all_to_all x1, blocking collectives, shards(): pieces = lax.all_to_all(pair.reshape(chips, piece, 128), CHIPS, 0, 0)  11.4 us
    all_to_all x1, blocking collectives, shards(): mine = lax.all_to_all(copies, CHIPS, 0, 0).reshape(half, 128)  11.3 us
    unnamed x26, local copies, waits for them, and re-layouts  2.42 us
  transfers between devices with their start and end apart: 14, of which 9 were waited for; matrix products, arithmetic and copies ran while one was open for 0% of the time, Pallas kernels for 9%

profile of v3, /device:TPU:0, one launch (start us, length us, event | category | flops | bytes accessed | tf_op | source)
XLA Modules:
  0.0 71.1 jit_solution(7895606626731184881)
XLA Ops:
  0.6 3.0 %collective-permute-start.2 = (s32[3,1,4]{2,1,0:T(1,128)}, s32[3,1,4]{2,1,0:T(1,128)S(1)}, u32[]{:S(2)}, u32[]{:S(2)}) collective-permute-start(s32[3,1,4]{2,1,0:T(1,128)} %bitcast.28), channel_id=1, source_target_pairs={{0,2},{1,3},{2,0},{3,1},{4,6},{5,7},{6,4},{7,5},{8,10},{9,11},{10,... | collective-permute-start | bytes 152 | tf_op jit(solution)/shard_map/ppermute | solution.py:25
  3.6 1.6 %collective-permute-start.1 = (s32[3,1,4]{2,1,0:T(1,128)}, s32[3,1,4]{2,1,0:T(1,128)S(1)}, u32[]{:S(2)}, u32[]{:S(2)}) collective-permute-start(s32[3,1,4]{2,1,0:T(1,128)} %bitcast.29), channel_id=1, source_target_pairs={{0,4},{1,5},{2,6},{3,7},{4,0},{5,1},{6,2},{7,3},{8,12},{9,13},{10,... | collective-permute-start | bytes 152 | tf_op jit(solution)/shard_map/ppermute | solution.py:25
  5.2 2.6 %collective-permute-start = (s32[3,1,4]{2,1,0:T(1,128)}, s32[3,1,4]{2,1,0:T(1,128)S(1)}, u32[]{:S(2)}, u32[]{:S(2)}) collective-permute-start(s32[3,1,4]{2,1,0:T(1,128)} %bitcast.30), channel_id=1, source_target_pairs={{0,8},{1,9},{2,10},{3,11},{4,12},{5,13},{6,14},{7,15},{8,0},{9,1},... | collective-permute-start | bytes 152 | tf_op jit(solution)/shard_map/ppermute | solution.py:25
  7.8 1.0 %copy-done.3 = bf16[1024,256]{1,0:T(8,128)(2,1)S(1)} copy-done((bf16[1024,256]{1,0:T(8,128)(2,1)S(1)}, bf16[1024,256]{1,0:T(8,128)(2,1)}, u32[]{:S(2)}) %copy-start.3) | copy-done | bytes 524312
  8.9 0.0 copy-start.1
  8.9 0.0 copy-start.6
  8.9 0.0 collective-permute-done.2.refs_2_
  8.9 0.0 collective-permute-done.1.refs_1_
  9.0 1.0 %collective-permute-done.refs_0_ = s32[3,1,4]{2,1,0:T(1,128)S(1)} collective-permute-done((s32[3,1,4]{2,1,0:T(1,128)}, s32[3,1,4]{2,1,0:T(1,128)S(1)}, u32[]{:S(2)}, u32[]{:S(2)}) %collective-permute-start) | collective-permute-done | bytes 80 | tf_op jit(solution)/shard_map/ppermute | solution.py:25
  9.9 0.7 shard_map.199
  10.6 2.7 %collective-permute-start.3 = (bf16[4,128,256]{2,1,0:T(8,128)(2,1)S(1)}, bf16[4,128,256]{2,1,0:T(8,128)(2,1)S(1)}, u32[]{:S(2)}, u32[]{:S(2)}) collective-permute-start(bf16[4,128,256]{2,1,0:T(8,128)(2,1)S(1)} %get-tuple-element.49), channel_id=1, source_target_pairs={{0,8},{1,9},{2,10},{3,11},{4,12},{5,13},{6,14},{7,15},{8,0},{9,1},... | collective-permute-start | bytes 786440 | tf_op jit(solution)/shard_map/ppermute | solution.py:25
  13.2 0.4 collective-permute-start.4
  13.7 0.5 collective-permute-start.5
  14.3 0.6 copy-done.8
  14.9 0.0 copy-done.9
  14.9 2.0 %shard_map.198 = (s32[68]{0:T(128)S(1)}, f32[8,128,256]{2,1,0:T(8,128)S(1)}, f32[8,128,256]{2,1,0:T(8,128)S(1)}, bf16[256,1024]{1,0:T(8,128)(2,1)S(1)}, bf16[8,4...) custom-call(s32[4,8]{1,0:T(4,128)S(1)} %bitcast.22, s32[3,1,4]{2,1,0:T(1,128)S(1)} %bitcast.23, ...), custom_call_target="tpu_custom_call" | custom-call | flops 402653184 | bytes 8388608 | tf_op jit(solution)/shard_map/pallas_call | solution.py:37
  16.9 6.6 %collective-permute-done.3.refs_0_ = bf16[4,128,256]{2,1,0:T(8,128)(2,1)S(1)} collective-permute-done((bf16[4,128,256]{2,1,0:T(8,128)(2,1)S(1)}, bf16[4,128,256]{2,1,0:T(8,128)(2,1)S(1)}, u32[]{:S(2)}, u32[]{:S(2)}) %collective-permute-start.3) | collective-permute-done | bytes 262176 | tf_op jit(solution)/shard_map/ppermute | solution.py:25
  23.5 1.3 %collective-permute-done.4.refs_1_ = bf16[4,128,256]{2,1,0:T(8,128)(2,1)S(1)} collective-permute-done((bf16[4,128,256]{2,1,0:T(8,128)(2,1)S(1)}, bf16[4,128,256]{2,1,0:T(8,128)(2,1)S(1)}, u32[]{:S(2)}, u32[]{:S(2)}) %collective-permute-start.4) | collective-permute-done | bytes 262176 | tf_op jit(solution)/shard_map/ppermute | solution.py:25
  24.8 0.0 collective-permute-done.5.refs_2_
  24.8 0.0 copy-done.5
  24.8 0.0 copy-start.4
  24.8 1.5 %shard_map.200 = (bf16[8,128,256]{2,1,0:T(8,128)(2,1)S(1)}, bf16[8,128,256]{2,1,0:T(8,128)(2,1)S(1)}, bf16[8,128,128]{2,1,0:T(8,128)(2,1)S(1)}, bf16[4,128,128]{...) custom-call(s32[68]{0:T(128)S(1)} %get-tuple-element.47.table, ...), custom_call_target="tpu_custom_call" | custom-call | flops 301989888 | bytes 8388608 | tf_op jit(solution)/shard_map/pallas_call | solution.py:37
  26.4 0.1 collective-permute-start.6
  26.4 1.8 %collective-permute-start.7 = (bf16[4,128,128]{2,1,0:T(8,128)(2,1)S(1)}, bf16[4,128,128]{2,1,0:T(8,128)(2,1)S(1)}, u32[]{:S(2)}, u32[]{:S(2)}) collective-permute-start(bf16[4,128,128]{2,1,0:T(8,128)(2,1)S(1)} %get-tuple-element.55), channel_id=1, source_target_pairs={{0,4},{1,5},{2,6},{3,7},{4,0},{5,1},{6,2},{7,3},{8,12},{9,13},{10,... | collective-permute-start | bytes 393224 | tf_op jit(solution)/shard_map/ppermute | solution.py:25
  28.2 0.5 collective-permute-start.8
  28.8 0.7 copy-done.7
  29.4 1.5 %shard_map.201 = (f32[8,128,256]{2,1,0:T(8,128)S(1)}, f32[8,128,128]{2,1,0:T(8,128)S(1)}, f32[8,128,128]{2,1,0:T(8,128)S(1)}, bf16[256,1024]{1,0:T(8,128)(2,1)S(1)}, bf16[256,1024]{1,0:T(8,128)(2,1)S(1)}) custom-call(s32[68]{0:T(128)S(1)} %get-tuple-element.47.table, s32[8,128]{1,0:T(8,128)S(1)} %bitcast.21, bf16[8,4,128,128]{3,2,1,0:T(8,128)(2,1)S(1)} %copy-done, ...), custom_call_target="tpu_custom_call" | custom-call | flops 335544320 | bytes 6291456 | tf_op jit(solution)/shard_map/pallas_call | solution.py:37
  30.9 2.7 %collective-permute-done.6.refs_0_ = bf16[4,128,128]{2,1,0:T(8,128)(2,1)S(1)} collective-permute-done((bf16[4,128,128]{2,1,0:T(8,128)(2,1)S(1)}, bf16[4,128,128]{2,1,0:T(8,128)(2,1)S(1)}, u32[]{:S(2)}, u32[]{:S(2)}) %collective-permute-start.6) | collective-permute-done | bytes 131104 | tf_op jit(solution)/shard_map/ppermute | solution.py:25
  33.6 0.0 collective-permute-done.7.refs_1_
  33.6 0.0 collective-permute-done.8.refs_2_
  33.6 1.1 %shard_map.202 = (bf16[8,128,128]{2,1,0:T(8,128)(2,1)S(1)}, bf16[8,128,128]{2,1,0:T(8,128)(2,1)S(1)}, bf16[4,128,128]{2,1,0:T(8,128)(2,1)S(1)}, bf16[4,128,128]{2,1,0:T(8,128)(2,1)S(1)}, bf16[4,128,128]{2,1,0:T(8,128)(2,1)S(1)}) custom-call(s32[68]{0:T(128)S(1)} %get-tuple-element.47.table, bf16[4,128,128]{2,1,0:T(8,128)(2,1)S(1)} %collective-permute-done.6.refs_0_, ...), custom_call_target="tpu_custom_call" | custom-call | flops 100663296 | bytes 3145728 | tf_op jit(solution)/shard_map/pallas_call | solution.py:37
  34.8 1.2 %collective-permute-start.9 = (bf16[4,128,128]{2,1,0:T(8,128)(2,1)S(1)}, bf16[4,128,128]{2,1,0:T(8,128)(2,1)S(1)}, u32[]{:S(2)}, u32[]{:S(2)}) collective-permute-start(bf16[4,128,128]{2,1,0:T(8,128)(2,1)S(1)} %get-tuple-element.67), channel_id=1, source_target_pairs={{0,8},{1,9},{2,10},{3,11},{4,12},{5,13},{6,14},{7,15},{8,0},{9,1},... | collective-permute-start | bytes 393224 | tf_op jit(solution)/shard_map/ppermute | solution.py:25
  36.0 1.7 %collective-permute-start.10 = (bf16[4,128,128]{2,1,0:T(8,128)(2,1)S(1)}, bf16[4,128,128]{2,1,0:T(8,128)(2,1)S(1)}, u32[]{:S(2)}, u32[]{:S(2)}) collective-permute-start(bf16[4,128,128]{2,1,0:T(8,128)(2,1)S(1)} %get-tuple-element.68), channel_id=1, source_target_pairs={{0,4},{1,5},{2,6},{3,7},{4,0},{5,1},{6,2},{7,3},{8,12},{9,13},{10,... | collective-permute-start | bytes 393224 | tf_op jit(solution)/shard_map/ppermute | solution.py:25
  37.7 0.5 collective-permute-start.11
  38.2 2.0 %shard_map.203 = (bf16[8,128,128]{2,1,0:T(8,128)(2,1)}, f32[8,128,128]{2,1,0:T(8,128)S(1)}, f32[8,128,256]{2,1,0:T(8,128)S(1)}, f32[256,128]{1,0:T(8,128)S(1)}, f32[1,128]{1,0:T(1,128)S(1)}) custom-call(s32[68]{0:T(128)S(1)} %get-tuple-element.47.table, bf16[8,4,128,128]{3,2,1,0:T(8,128)(2,1)S(1)} %get-tuple-element.48.values_t, ...), custom_call_target="tpu_custom_call" | custom-call | flops 268435456 | bytes 4194304 | tf_op jit(solution)/shard_map/pallas_call | solution.py:37
  40.2 1.8 %collective-permute-done.9.refs_0_ = bf16[4,128,128]{2,1,0:T(8,128)(2,1)S(1)} collective-permute-done((bf16[4,128,128]{2,1,0:T(8,128)(2,1)S(1)}, bf16[4,128,128]{2,1,0:T(8,128)(2,1)S(1)}, u32[]{:S(2)}, u32[]{:S(2)}) %collective-permute-start.9) | collective-permute-done | bytes 131104 | tf_op jit(solution)/shard_map/ppermute | solution.py:25
  42.0 0.2 collective-permute-done.10.refs_1_
  42.2 0.4 collective-permute-done.11.refs_2_
  42.7 1.6 %shard_map.204 = (bf16[8,128,256]{2,1,0:T(8,128)(2,1)S(1)}, bf16[896,128]{1,0:T(8,128)(2,1)S(1)}, f32[896,128]{1,0:T(8,128)S(1)}) custom-call(s32[68]{0:T(128)S(1)} %get-tuple-element.47.table, bf16[4,128,128]{2,1,0:T(8,128)(2,1)S(1)} %collective-permute-done.9.refs_0_, bf16[4,128,128]{2,1,0:T(8,128)(2,1)S(1)} %collective-permute-done.10.refs_1_, ...), custom_call_target="tpu_custom_call" | custom-call | flops 402653184 | bytes 6291456 | tf_op jit(solution)/shard_map/pallas_call | solution.py:37
  44.3 0.1 collective-permute-start.12
  44.4 1.5 %collective-permute-done.12.arrived = bf16[896,128]{1,0:T(8,128)(2,1)S(1)} collective-permute-done((bf16[896,128]{1,0:T(8,128)(2,1)S(1)}, bf16[896,128]{1,0:T(8,128)(2,1)S(1)}, u32[]{:S(2)}, u32[]{:S(2)}) %collective-permute-start.12) | collective-permute-done | bytes 229408 | tf_op jit(solution)/shard_map/ppermute | solution.py:25
  45.8 0.1 shard_map.206
  45.9 11.4 %all_to_all.10.arrived = bf16[8,112,128]{2,1,0:T(8,128)(2,1)S(1)} all-to-all(bf16[8,112,128]{2,1,0:T(8,128)(2,1)S(1)} %bitcast.17), channel_id=1, replica_groups=mesh['grp'=2,'dom'=4,'sub'=2,'feat'=2] {'dom','sub'}, dimensions={0} | all-to-all | bytes 458752 | tf_op jit(solution)/shard_map/all_to_all | solution.py:456
  57.4 11.3 %all_to_all.11 = bf16[8,112,128]{2,1,0:T(8,128)(2,1)S(1)} all-to-all(bf16[8,112,128]{2,1,0:T(8,128)(2,1)S(1)} %shard_map.207), channel_id=1, replica_groups=mesh['grp'=2,'dom'=4,'sub'=2,'feat'=2] {'dom','sub'}, dimensions={0} | all-to-all | bytes 458752 | tf_op jit(solution)/shard_map/all_to_all | solution.py:461
  68.7 0.0 collective-permute-start.13
  68.7 0.8 %shard_map.205 = bf16[8,128,256]{2,1,0:T(8,128)(2,1)} custom-call(bf16[8,128,256]{2,1,0:T(8,128)(2,1)S(1)} %get-tuple-element.77.value), custom_call_target="tpu_custom_call" | custom-call | bytes 1048576 | tf_op jit(solution)/shard_map/pallas_call | solution.py:37
  69.5 0.7 collective-permute-done.13.other
  70.2 1.0 %shard_map.208 = (f32[256,256]{1,0:T(8,128)}, f32[256,256]{1,0:T(8,128)}, f32[1,256]{1,0:T(1,128)}, f32[256,128]{1,0:T(8,128)}, f32[256,128]{1,0:T(8,128)}, /*index=5*/f32[1,128]{1,0:T(1,128)}) custom-call(bf16[896,128]{1,0:T(8,128)(2,1)S(1)} %bitcast.19, bf16[896,128]{1,0:T(8,128)(2,1)S(1)} %collective-permute-done.13.other), custom_call_target="tpu_custom_call" | custom-call | bytes 1376256 | tf_op jit(solution)/shard_map/pallas_call | solution.py:37
  (20 shorter events, 0.1 us)
Async XLA Ops:
  0.6 13.6 %copy-start = (bf16[8,4,128,128]{3,2,1,0:T(8,128)(2,1)S(1)}, bf16[8,4,128,128]{3,2,1,0:T(8,128)(2,1)}, u32[]{:S(2)}) copy-start(bf16[8,4,128,128]{3,2,1,0:T(8,128)(2,1)} %values.1) | copy-start | bytes 3145732
  0.6 8.3 %collective-permute-start.2 = (s32[3,1,4]{2,1,0:T(1,128)}, s32[3,1,4]{2,1,0:T(1,128)S(1)}, u32[]{:S(2)}, u32[]{:S(2)}) collective-permute-start(s32[3,1,4]{2,1,0:T(1,128)} %bitcast.28), channel_id=1, source_target_pairs={{0,2},{1,3},{2,0},{3,1},{4,6},{5,7},{6,4},{7,5},{8,10},{9,11},{10,... | collective-permute-start | bytes 152 | tf_op jit(solution)/shard_map/ppermute | solution.py:25
  3.6 5.3 %collective-permute-start.1 = (s32[3,1,4]{2,1,0:T(1,128)}, s32[3,1,4]{2,1,0:T(1,128)S(1)}, u32[]{:S(2)}, u32[]{:S(2)}) collective-permute-start(s32[3,1,4]{2,1,0:T(1,128)} %bitcast.29), channel_id=1, source_target_pairs={{0,4},{1,5},{2,6},{3,7},{4,0},{5,1},{6,2},{7,3},{8,12},{9,13},{10,... | collective-permute-start | bytes 152 | tf_op jit(solution)/shard_map/ppermute | solution.py:25
  5.2 4.7 %collective-permute-start = (s32[3,1,4]{2,1,0:T(1,128)}, s32[3,1,4]{2,1,0:T(1,128)S(1)}, u32[]{:S(2)}, u32[]{:S(2)}) collective-permute-start(s32[3,1,4]{2,1,0:T(1,128)} %bitcast.30), channel_id=1, source_target_pairs={{0,8},{1,9},{2,10},{3,11},{4,12},{5,13},{6,14},{7,15},{8,0},{9,1},... | collective-permute-start | bytes 152 | tf_op jit(solution)/shard_map/ppermute | solution.py:25
  7.8 1.0 %copy-start.3 = (bf16[1024,256]{1,0:T(8,128)(2,1)S(1)}, bf16[1024,256]{1,0:T(8,128)(2,1)}, u32[]{:S(2)}) copy-start(bf16[1024,256]{1,0:T(8,128)(2,1)} %param.14) | copy-start | bytes 1572868
  8.9 5.3 %copy-start.1 = (bf16[1,3,4,128,128]{4,3,2,1,0:T(8,128)(2,1)S(1)}, bf16[1,3,4,128,128]{4,3,2,1,0:T(8,128)(2,1)}, u32[]{:S(2)}) copy-start(bf16[1,3,4,128,128]{4,3,2,1,0:T(8,128)(2,1)} %param.21) | copy-start | bytes 1179652
  8.9 5.3 %copy-start.6 = (bf16[256,256]{1,0:T(8,128)(2,1)S(1)}, bf16[256,256]{1,0:T(8,128)(2,1)}, u32[]{:S(2)}) copy-start(bf16[256,256]{1,0:T(8,128)(2,1)} %refs_6_.3) | copy-start | bytes 393220
  9.9 4.3 %copy-start.10 = (f32[256]{0:T(256)S(1)}, f32[256]{0:T(256)}, u32[]{:S(2)}) copy-start(f32[256]{0:T(256)} %param.24) | copy-start | bytes 3076
  9.9 4.3 %copy-start.11 = (s32[1,3]{1,0:T(1,128)S(1)}, s32[1,3]{1,0:T(1,128)}, u32[]{:S(2)}) copy-start(s32[1,3]{1,0:T(1,128)} %count.1) | copy-start | bytes 40
  10.6 12.9 %collective-permute-start.3 = (bf16[4,128,256]{2,1,0:T(8,128)(2,1)S(1)}, bf16[4,128,256]{2,1,0:T(8,128)(2,1)S(1)}, u32[]{:S(2)}, u32[]{:S(2)}) collective-permute-start(bf16[4,128,256]{2,1,0:T(8,128)(2,1)S(1)} %get-tuple-element.49), channel_id=1, source_target_pairs={{0,8},{1,9},{2,10},{3,11},{4,12},{5,13},{6,14},{7,15},{8,0},{9,1},... | collective-permute-start | bytes 786440 | tf_op jit(solution)/shard_map/ppermute | solution.py:25
  13.2 11.6 %collective-permute-start.4 = (bf16[4,128,256]{2,1,0:T(8,128)(2,1)S(1)}, bf16[4,128,256]{2,1,0:T(8,128)(2,1)S(1)}, u32[]{:S(2)}, u32[]{:S(2)}) collective-permute-start(bf16[4,128,256]{2,1,0:T(8,128)(2,1)S(1)} %get-tuple-element.50), channel_id=1, source_target_pairs={{0,4},{1,5},{2,6},{3,7},{4,0},{5,1},{6,2},{7,3},{8,12},{9,13},{10,... | collective-permute-start | bytes 786440 | tf_op jit(solution)/shard_map/ppermute | solution.py:25
  13.7 11.1 %collective-permute-start.5 = (bf16[4,128,256]{2,1,0:T(8,128)(2,1)S(1)}, bf16[4,128,256]{2,1,0:T(8,128)(2,1)S(1)}, u32[]{:S(2)}, u32[]{:S(2)}) collective-permute-start(bf16[4,128,256]{2,1,0:T(8,128)(2,1)S(1)} %get-tuple-element.51), channel_id=1, source_target_pairs={{0,2},{1,3},{2,0},{3,1},{4,6},{5,7},{6,4},{7,5},{8,10},{9,11},{10,... | collective-permute-start | bytes 786440 | tf_op jit(solution)/shard_map/ppermute | solution.py:25
  14.2 0.7 copy-start.8
  14.2 0.7 copy-start.9
  14.9 9.9 %copy-start.2 = (bf16[256,256]{1,0:T(8,128)(2,1)S(1)}, bf16[256,256]{1,0:T(8,128)(2,1)}, u32[]{:S(2)}) copy-start(bf16[256,256]{1,0:T(8,128)(2,1)} %w1_near.1) | copy-start | bytes 393220
  14.9 9.9 %copy-start.5 = (bf16[256,128]{1,0:T(8,128)(2,1)S(1)}, bf16[256,128]{1,0:T(8,128)(2,1)}, u32[]{:S(2)}) copy-start(bf16[256,128]{1,0:T(8,128)(2,1)} %refs_6_.5) | copy-start | bytes 196612
  24.8 3.9 %copy-start.4 = (bf16[256,128]{1,0:T(8,128)(2,1)S(1)}, bf16[256,128]{1,0:T(8,128)(2,1)}, u32[]{:S(2)}) copy-start(bf16[256,128]{1,0:T(8,128)(2,1)} %w2_self.3) | copy-start | bytes 196612
  26.4 7.3 %collective-permute-start.6 = (bf16[4,128,128]{2,1,0:T(8,128)(2,1)S(1)}, bf16[4,128,128]{2,1,0:T(8,128)(2,1)S(1)}, u32[]{:S(2)}, u32[]{:S(2)}) collective-permute-start(bf16[4,128,128]{2,1,0:T(8,128)(2,1)S(1)} %get-tuple-element.54), channel_id=1, source_target_pairs={{0,8},{1,9},{2,10},{3,11},{4,12},{5,13},{6,14},{7,15},{8,0},{9,1},... | collective-permute-start | bytes 393224 | tf_op jit(solution)/shard_map/ppermute | solution.py:25
  26.4 7.2 %collective-permute-start.7 = (bf16[4,128,128]{2,1,0:T(8,128)(2,1)S(1)}, bf16[4,128,128]{2,1,0:T(8,128)(2,1)S(1)}, u32[]{:S(2)}, u32[]{:S(2)}) collective-permute-start(bf16[4,128,128]{2,1,0:T(8,128)(2,1)S(1)} %get-tuple-element.55), channel_id=1, source_target_pairs={{0,4},{1,5},{2,6},{3,7},{4,0},{5,1},{6,2},{7,3},{8,12},{9,13},{10,... | collective-permute-start | bytes 393224 | tf_op jit(solution)/shard_map/ppermute | solution.py:25
  28.2 5.4 %collective-permute-start.8 = (bf16[4,128,128]{2,1,0:T(8,128)(2,1)S(1)}, bf16[4,128,128]{2,1,0:T(8,128)(2,1)S(1)}, u32[]{:S(2)}, u32[]{:S(2)}) collective-permute-start(bf16[4,128,128]{2,1,0:T(8,128)(2,1)S(1)} %get-tuple-element.56), channel_id=1, source_target_pairs={{0,2},{1,3},{2,0},{3,1},{4,6},{5,7},{6,4},{7,5},{8,10},{9,11},{10,... | collective-permute-start | bytes 393224 | tf_op jit(solution)/shard_map/ppermute | solution.py:25
  28.8 0.7 copy-start.7
  28.8 0.7 copy-start.12
  34.8 7.2 %collective-permute-start.9 = (bf16[4,128,128]{2,1,0:T(8,128)(2,1)S(1)}, bf16[4,128,128]{2,1,0:T(8,128)(2,1)S(1)}, u32[]{:S(2)}, u32[]{:S(2)}) collective-permute-start(bf16[4,128,128]{2,1,0:T(8,128)(2,1)S(1)} %get-tuple-element.67), channel_id=1, source_target_pairs={{0,8},{1,9},{2,10},{3,11},{4,12},{5,13},{6,14},{7,15},{8,0},{9,1},... | collective-permute-start | bytes 393224 | tf_op jit(solution)/shard_map/ppermute | solution.py:25
  36.0 6.3 %collective-permute-start.10 = (bf16[4,128,128]{2,1,0:T(8,128)(2,1)S(1)}, bf16[4,128,128]{2,1,0:T(8,128)(2,1)S(1)}, u32[]{:S(2)}, u32[]{:S(2)}) collective-permute-start(bf16[4,128,128]{2,1,0:T(8,128)(2,1)S(1)} %get-tuple-element.68), channel_id=1, source_target_pairs={{0,4},{1,5},{2,6},{3,7},{4,0},{5,1},{6,2},{7,3},{8,12},{9,13},{10,... | collective-permute-start | bytes 393224 | tf_op jit(solution)/shard_map/ppermute | solution.py:25
  37.7 5.0 %collective-permute-start.11 = (bf16[4,128,128]{2,1,0:T(8,128)(2,1)S(1)}, bf16[4,128,128]{2,1,0:T(8,128)(2,1)S(1)}, u32[]{:S(2)}, u32[]{:S(2)}) collective-permute-start(bf16[4,128,128]{2,1,0:T(8,128)(2,1)S(1)} %get-tuple-element.69), channel_id=1, source_target_pairs={{0,2},{1,3},{2,0},{3,1},{4,6},{5,7},{6,4},{7,5},{8,10},{9,11},{10,... | collective-permute-start | bytes 393224 | tf_op jit(solution)/shard_map/ppermute | solution.py:25
  44.3 1.6 %collective-permute-start.12 = (bf16[896,128]{1,0:T(8,128)(2,1)S(1)}, bf16[896,128]{1,0:T(8,128)(2,1)S(1)}, u32[]{:S(2)}, u32[]{:S(2)}) collective-permute-start(bf16[896,128]{1,0:T(8,128)(2,1)S(1)} %get-tuple-element.79), channel_id=1, source_target_pairs={{0,1},{1,0},{2,3},{3,2},{4,5},{5,4},{6,7},{7,6},{8,9},{9,8},{10,11... | collective-permute-start | bytes 688136 | tf_op jit(solution)/shard_map/ppermute | solution.py:25
  68.7 1.5 %collective-permute-start.13 = (bf16[896,128]{1,0:T(8,128)(2,1)S(1)}, bf16[896,128]{1,0:T(8,128)(2,1)S(1)}, u32[]{:S(2)}, u32[]{:S(2)}) collective-permute-start(bf16[896,128]{1,0:T(8,128)(2,1)S(1)} %bitcast.18), channel_id=1, source_target_pairs={{0,1},{1,0},{2,3},{3,2},{4,5},{5,4},{6,7},{7,6},{8,9},{9,8},{10,11... | collective-permute-start | bytes 688136 | tf_op jit(solution)/shard_map/ppermute | solution.py:25

commit v4 on v3

--- a/solution.py
+++ b/solution.py
@@ -77,8 +77,9 @@
     blocks = refs[rounds]
     outs = refs[rounds + 1 :]
     for r in range(rounds):
+        row = partner_src[r][r]
         for s in range(outs[r].shape[0]):
-            outs[r][s] = blocks[partner_src[r][r, 0, s]]
+            outs[r][s] = blocks[row[0, s]]
 
 
 def first_local_body(
@@ -323,7 +324,7 @@
     )
     picks = run(
         functools.partial(pick_body, rounds),
-        [SMEM] * rounds + [VMEM],
+        [VMEM] * rounds + [VMEM],
         [VMEM] * rounds,
         [struct((slots, size, width_in), BF16)] * rounds,
         [],
@@ -337,7 +338,7 @@
         [SMEM] * (3 + rounds) + [VMEM] * 5,
         [SMEM] + [VMEM] * 5,
         [
-            struct((at.size,), jnp.int32),
+            pltpu.SMEM((at.size,), jnp.int32),
             struct((tiles, size, width_in), F32),
             struct((tiles, size, hidden_width), F32),
             struct((width_in, nodes), BF16),
@@ -418,7 +419,7 @@
     )
 
     rows = (2 * width_in * hidden_width + 2 * hidden_width * classes + hidden_width + classes) // 128
-    piece = -(-rows // (2 * chips * 16)) * 16
+    piece = -(-rows // (2 * chips * 8)) * 8
     half = piece * chips
     hidden_grad, send, keep = run(
         functools.partial(back_body, at, rounds),

time: 71.4 us -> 68.6 us (0.961)
  Pallas kernels: 12.3 us -> 8.62 us
  waiting for transfers between devices: 16.1 us -> 17.7 us
    pallas_call x12, Pallas kernels: 12.3 us -> 8.62 us  [run(): pl.pallas_call(body, in_specs=in_specs, out_specs=out_specs, out_shape=ou...]
    ppermute x14, waiting for transfers between devices: 16.1 us -> 17.7 us  [swapped(): return lax.ppermute(value, AXES, pairs)]
  transfers between devices with their start and end apart: 14 -> 14, of which waited for: 9 -> 9; matrix products, arithmetic and copies ran while one was open for 0% -> 0% of each run, Pallas kernels for 9% -> 7%
where the time goes in v4:
time: 68.6 us; the launch traced here: 68.3 us
  blocking collectives  22.2 us (32%)
  waiting for transfers between devices  17.7 us (26%)
  starting transfers between devices  16.7 us (24%)
  Pallas kernels  8.62 us (13%)
  local copies, waits for them, and re-layouts  2.42 us (4%)
  between operations  0.8 us (1%)
    ppermute x14, waiting for transfers between devices, swapped(): return lax.ppermute(value, AXES, pairs)  17.7 us
    ppermute x14, starting transfers between devices, swapped(): return lax.ppermute(value, AXES, pairs)  16.7 us
    all_to_all x1, blocking collectives, shards(): pieces = lax.all_to_all(pair.reshape(chips, piece, 128), CHIPS, 0, 0)  11.2 us
    all_to_all x1, blocking collectives, shards(): mine = lax.all_to_all(copies, CHIPS, 0, 0).reshape(half, 128)  11 us
    pallas_call x12, Pallas kernels, run(): pl.pallas_call(body, in_specs=in_specs, out_specs=out_specs, out_shape=ou...  8.62 us
    unnamed x26, local copies, waits for them, and re-layouts  2.42 us
  transfers between devices with their start and end apart: 14, of which 9 were waited for; matrix products, arithmetic and copies ran while one was open for 0% of the time, Pallas kernels for 7%

profile of v4, /device:TPU:0, one launch (start us, length us, event | category | flops | bytes accessed | tf_op | source)
XLA Modules:
  0.0 68.3 jit_solution(18423244246090325544)
XLA Ops:
  0.6 0.0 copy-start
  0.6 3.0 %collective-permute-start.2 = (s32[3,1,4]{2,1,0:T(1,128)}, s32[3,1,4]{2,1,0:T(1,128)S(1)}, u32[]{:S(2)}, u32[]{:S(2)}) collective-permute-start(s32[3,1,4]{2,1,0:T(1,128)} %bitcast.28), channel_id=1, source_target_pairs={{0,2},{1,3},{2,0},{3,1},{4,6},{5,7},{6,4},{7,5},{8,10},{9,11},{10,... | collective-permute-start | bytes 152 | tf_op jit(solution)/shard_map/ppermute | solution.py:25
  3.6 1.6 %collective-permute-start.1 = (s32[3,1,4]{2,1,0:T(1,128)}, s32[3,1,4]{2,1,0:T(1,128)S(1)}, u32[]{:S(2)}, u32[]{:S(2)}) collective-permute-start(s32[3,1,4]{2,1,0:T(1,128)} %bitcast.29), channel_id=1, source_target_pairs={{0,4},{1,5},{2,6},{3,7},{4,0},{5,1},{6,2},{7,3},{8,12},{9,13},{10,... | collective-permute-start | bytes 152 | tf_op jit(solution)/shard_map/ppermute | solution.py:25
  5.2 2.6 %collective-permute-start = (s32[3,1,4]{2,1,0:T(1,128)}, s32[3,1,4]{2,1,0:T(1,128)S(1)}, u32[]{:S(2)}, u32[]{:S(2)}) collective-permute-start(s32[3,1,4]{2,1,0:T(1,128)} %bitcast.30), channel_id=1, source_target_pairs={{0,8},{1,9},{2,10},{3,11},{4,12},{5,13},{6,14},{7,15},{8,0},{9,1},... | collective-permute-start | bytes 152 | tf_op jit(solution)/shard_map/ppermute | solution.py:25
  7.8 1.0 %copy-done.3 = bf16[1024,256]{1,0:T(8,128)(2,1)S(1)} copy-done((bf16[1024,256]{1,0:T(8,128)(2,1)S(1)}, bf16[1024,256]{1,0:T(8,128)(2,1)}, u32[]{:S(2)}) %copy-start.3) | copy-done | bytes 524312
  8.9 0.0 copy-start.1
  8.9 0.0 copy-start.6
  8.9 0.0 collective-permute-done.2.refs_2_
  8.9 0.0 collective-permute-done.1.refs_1_
  9.0 1.0 %collective-permute-done.refs_0_ = s32[3,1,4]{2,1,0:T(1,128)S(1)} collective-permute-done((s32[3,1,4]{2,1,0:T(1,128)}, s32[3,1,4]{2,1,0:T(1,128)S(1)}, u32[]{:S(2)}, u32[]{:S(2)}) %collective-permute-start) | collective-permute-done | bytes 80 | tf_op jit(solution)/shard_map/ppermute | solution.py:25
  9.9 0.1 shard_map.199
  10.1 2.7 %collective-permute-start.3 = (bf16[4,128,256]{2,1,0:T(8,128)(2,1)S(1)}, bf16[4,128,256]{2,1,0:T(8,128)(2,1)S(1)}, u32[]{:S(2)}, u32[]{:S(2)}) collective-permute-start(bf16[4,128,256]{2,1,0:T(8,128)(2,1)S(1)} %get-tuple-element.49), channel_id=1, source_target_pairs={{0,8},{1,9},{2,10},{3,11},{4,12},{5,13},{6,14},{7,15},{8,0},{9,1},... | collective-permute-start | bytes 786440 | tf_op jit(solution)/shard_map/ppermute | solution.py:25
  12.7 0.4 collective-permute-start.4
  13.2 0.5 collective-permute-start.5
  13.8 0.6 copy-done.8
  14.4 0.0 copy-done.9
  14.4 1.5 %shard_map.198 = (s32[68]{0:T(128)S(4)}, f32[8,128,256]{2,1,0:T(8,128)S(1)}, f32[8,128,256]{2,1,0:T(8,128)S(1)}, bf16[256,1024]{1,0:T(8,128)(2,1)S(1)}, bf16[8,4...) custom-call(s32[4,8]{1,0:T(4,128)S(1)} %bitcast.22, s32[3,1,4]{2,1,0:T(1,128)S(1)} %bitcast.23, ...), custom_call_target="tpu_custom_call" | custom-call | flops 402653184 | bytes 8388608 | tf_op jit(solution)/shard_map/pallas_call | solution.py:37
  15.9 7.1 %collective-permute-done.3.refs_0_ = bf16[4,128,256]{2,1,0:T(8,128)(2,1)S(1)} collective-permute-done((bf16[4,128,256]{2,1,0:T(8,128)(2,1)S(1)}, bf16[4,128,256]{2,1,0:T(8,128)(2,1)S(1)}, u32[]{:S(2)}, u32[]{:S(2)}) %collective-permute-start.3) | collective-permute-done | bytes 262176 | tf_op jit(solution)/shard_map/ppermute | solution.py:25
  23.0 1.3 %collective-permute-done.4.refs_1_ = bf16[4,128,256]{2,1,0:T(8,128)(2,1)S(1)} collective-permute-done((bf16[4,128,256]{2,1,0:T(8,128)(2,1)S(1)}, bf16[4,128,256]{2,1,0:T(8,128)(2,1)S(1)}, u32[]{:S(2)}, u32[]{:S(2)}) %collective-permute-start.4) | collective-permute-done | bytes 262176 | tf_op jit(solution)/shard_map/ppermute | solution.py:25
  24.3 0.0 collective-permute-done.5.refs_2_
  24.3 0.0 copy-done.5
  24.3 0.0 copy-start.4
  24.3 1.0 %shard_map.200 = (bf16[8,128,256]{2,1,0:T(8,128)(2,1)S(1)}, bf16[8,128,256]{2,1,0:T(8,128)(2,1)S(1)}, bf16[8,128,128]{2,1,0:T(8,128)(2,1)S(1)}, bf16[4,128,128]{...) custom-call(s32[68]{0:T(128)S(4)} %get-tuple-element.47.table, ...), custom_call_target="tpu_custom_call" | custom-call | flops 301989888 | bytes 8388608 | tf_op jit(solution)/shard_map/pallas_call | solution.py:37
  25.3 0.1 collective-permute-start.6
  25.4 1.8 %collective-permute-start.7 = (bf16[4,128,128]{2,1,0:T(8,128)(2,1)S(1)}, bf16[4,128,128]{2,1,0:T(8,128)(2,1)S(1)}, u32[]{:S(2)}, u32[]{:S(2)}) collective-permute-start(bf16[4,128,128]{2,1,0:T(8,128)(2,1)S(1)} %get-tuple-element.55), channel_id=1, source_target_pairs={{0,4},{1,5},{2,6},{3,7},{4,0},{5,1},{6,2},{7,3},{8,12},{9,13},{10,... | collective-permute-start | bytes 393224 | tf_op jit(solution)/shard_map/ppermute | solution.py:25
  27.1 0.5 collective-permute-start.8
  27.7 0.7 copy-done.7
  28.4 1.0 %shard_map.201 = (f32[8,128,256]{2,1,0:T(8,128)S(1)}, f32[8,128,128]{2,1,0:T(8,128)S(1)}, f32[8,128,128]{2,1,0:T(8,128)S(1)}, bf16[256,1024]{1,0:T(8,128)(2,1)S(1)}, bf16[256,1024]{1,0:T(8,128)(2,1)S(1)}) custom-call(s32[68]{0:T(128)S(4)} %get-tuple-element.47.table, s32[8,128]{1,0:T(8,128)S(1)} %bitcast.21, bf16[8,4,128,128]{3,2,1,0:T(8,128)(2,1)S(1)} %copy-done, ...), custom_call_target="tpu_custom_call" | custom-call | flops 335544320 | bytes 6291456 | tf_op jit(solution)/shard_map/pallas_call | solution.py:37
  29.3 3.2 %collective-permute-done.6.refs_0_ = bf16[4,128,128]{2,1,0:T(8,128)(2,1)S(1)} collective-permute-done((bf16[4,128,128]{2,1,0:T(8,128)(2,1)S(1)}, bf16[4,128,128]{2,1,0:T(8,128)(2,1)S(1)}, u32[]{:S(2)}, u32[]{:S(2)}) %collective-permute-start.6) | collective-permute-done | bytes 131104 | tf_op jit(solution)/shard_map/ppermute | solution.py:25
  32.6 0.0 collective-permute-done.7.refs_1_
  32.6 0.0 collective-permute-done.8.refs_2_
  32.6 0.6 shard_map.202
  33.2 1.2 %collective-permute-start.9 = (bf16[4,128,128]{2,1,0:T(8,128)(2,1)S(1)}, bf16[4,128,128]{2,1,0:T(8,128)(2,1)S(1)}, u32[]{:S(2)}, u32[]{:S(2)}) collective-permute-start(bf16[4,128,128]{2,1,0:T(8,128)(2,1)S(1)} %get-tuple-element.67), channel_id=1, source_target_pairs={{0,8},{1,9},{2,10},{3,11},{4,12},{5,13},{6,14},{7,15},{8,0},{9,1},... | collective-permute-start | bytes 393224 | tf_op jit(solution)/shard_map/ppermute | solution.py:25
  34.3 1.7 %collective-permute-start.10 = (bf16[4,128,128]{2,1,0:T(8,128)(2,1)S(1)}, bf16[4,128,128]{2,1,0:T(8,128)(2,1)S(1)}, u32[]{:S(2)}, u32[]{:S(2)}) collective-permute-start(bf16[4,128,128]{2,1,0:T(8,128)(2,1)S(1)} %get-tuple-element.68), channel_id=1, source_target_pairs={{0,4},{1,5},{2,6},{3,7},{4,0},{5,1},{6,2},{7,3},{8,12},{9,13},{10,... | collective-permute-start | bytes 393224 | tf_op jit(solution)/shard_map/ppermute | solution.py:25
  36.1 0.5 collective-permute-start.11
  36.6 1.5 %shard_map.203 = (bf16[8,128,128]{2,1,0:T(8,128)(2,1)}, f32[8,128,128]{2,1,0:T(8,128)S(1)}, f32[8,128,256]{2,1,0:T(8,128)S(1)}, f32[256,128]{1,0:T(8,128)S(1)}, f32[1,128]{1,0:T(1,128)S(1)}) custom-call(s32[68]{0:T(128)S(4)} %get-tuple-element.47.table, bf16[8,4,128,128]{3,2,1,0:T(8,128)(2,1)S(1)} %get-tuple-element.48.values_t, ...), custom_call_target="tpu_custom_call" | custom-call | flops 268435456 | bytes 4194304 | tf_op jit(solution)/shard_map/pallas_call | solution.py:37
  38.1 2.3 %collective-permute-done.9.refs_0_ = bf16[4,128,128]{2,1,0:T(8,128)(2,1)S(1)} collective-permute-done((bf16[4,128,128]{2,1,0:T(8,128)(2,1)S(1)}, bf16[4,128,128]{2,1,0:T(8,128)(2,1)S(1)}, u32[]{:S(2)}, u32[]{:S(2)}) %collective-permute-start.9) | collective-permute-done | bytes 131104 | tf_op jit(solution)/shard_map/ppermute | solution.py:25
  40.4 0.2 collective-permute-done.10.refs_1_
  40.6 0.4 collective-permute-done.11.refs_2_
  41.0 1.1 %shard_map.204 = (bf16[8,128,256]{2,1,0:T(8,128)(2,1)S(1)}, bf16[832,128]{1,0:T(8,128)(2,1)S(1)}, f32[832,128]{1,0:T(8,128)S(1)}) custom-call(s32[68]{0:T(128)S(4)} %get-tuple-element.47.table, bf16[4,128,128]{2,1,0:T(8,128)(2,1)S(1)} %collective-permute-done.9.refs_0_, bf16[4,128,128]{2,1,0:T(8,128)(2,1)S(1)} %collective-permute-done.10.refs_1_, ...), custom_call_target="tpu_custom_call" | custom-call | flops 402653184 | bytes 6291456 | tf_op jit(solution)/shard_map/pallas_call | solution.py:37
  42.1 0.1 collective-permute-start.12
  42.2 1.5 %collective-permute-done.12.arrived = bf16[832,128]{1,0:T(8,128)(2,1)S(1)} collective-permute-done((bf16[832,128]{1,0:T(8,128)(2,1)S(1)}, bf16[832,128]{1,0:T(8,128)(2,1)S(1)}, u32[]{:S(2)}, u32[]{:S(2)}) %collective-permute-start.12) | collective-permute-done | bytes 213024 | tf_op jit(solution)/shard_map/ppermute | solution.py:25
  43.7 11.2 %all_to_all.10.arrived = bf16[8,104,128]{2,1,0:T(8,128)(2,1)S(1)} all-to-all(bf16[8,104,128]{2,1,0:T(8,128)(2,1)S(1)} %bitcast.19), channel_id=1, replica_groups=mesh['grp'=2,'dom'=4,'sub'=2,'feat'=2] {'dom','sub'}, dimensions={0} | all-to-all | bytes 425984 | tf_op jit(solution)/shard_map/all_to_all | solution.py:457
  54.9 11.0 %all_to_all.11 = bf16[8,104,128]{2,1,0:T(8,128)(2,1)S(1)} all-to-all(bf16[8,104,128]{2,1,0:T(8,128)(2,1)S(1)} %shard_map.207), channel_id=1, replica_groups=mesh['grp'=2,'dom'=4,'sub'=2,'feat'=2] {'dom','sub'}, dimensions={0} | all-to-all | bytes 425984 | tf_op jit(solution)/shard_map/all_to_all | solution.py:462
  65.9 0.0 collective-permute-start.13
  65.9 0.8 %shard_map.205 = bf16[8,128,256]{2,1,0:T(8,128)(2,1)} custom-call(bf16[8,128,256]{2,1,0:T(8,128)(2,1)S(1)} %get-tuple-element.77.value), custom_call_target="tpu_custom_call" | custom-call | bytes 1048576 | tf_op jit(solution)/shard_map/pallas_call | solution.py:37
  66.7 0.6 collective-permute-done.13.other
  67.4 1.0 %shard_map.208 = (f32[256,256]{1,0:T(8,128)}, f32[256,256]{1,0:T(8,128)}, f32[1,256]{1,0:T(1,128)}, f32[256,128]{1,0:T(8,128)}, f32[256,128]{1,0:T(8,128)}, /*index=5*/f32[1,128]{1,0:T(1,128)}) custom-call(bf16[832,128]{1,0:T(8,128)(2,1)S(1)} %bitcast.18, bf16[832,128]{1,0:T(8,128)(2,1)S(1)} %collective-permute-done.13.other), custom_call_target="tpu_custom_call" | custom-call | bytes 1277952 | tf_op jit(solution)/shard_map/pallas_call | solution.py:37
  (20 shorter events, 0.2 us)
Async XLA Ops:
  0.6 13.1 %copy-start = (bf16[8,4,128,128]{3,2,1,0:T(8,128)(2,1)S(1)}, bf16[8,4,128,128]{3,2,1,0:T(8,128)(2,1)}, u32[]{:S(2)}) copy-start(bf16[8,4,128,128]{3,2,1,0:T(8,128)(2,1)} %values.1) | copy-start | bytes 3145732
  0.6 8.3 %collective-permute-start.2 = (s32[3,1,4]{2,1,0:T(1,128)}, s32[3,1,4]{2,1,0:T(1,128)S(1)}, u32[]{:S(2)}, u32[]{:S(2)}) collective-permute-start(s32[3,1,4]{2,1,0:T(1,128)} %bitcast.28), channel_id=1, source_target_pairs={{0,2},{1,3},{2,0},{3,1},{4,6},{5,7},{6,4},{7,5},{8,10},{9,11},{10,... | collective-permute-start | bytes 152 | tf_op jit(solution)/shard_map/ppermute | solution.py:25
  3.6 5.3 %collective-permute-start.1 = (s32[3,1,4]{2,1,0:T(1,128)}, s32[3,1,4]{2,1,0:T(1,128)S(1)}, u32[]{:S(2)}, u32[]{:S(2)}) collective-permute-start(s32[3,1,4]{2,1,0:T(1,128)} %bitcast.29), channel_id=1, source_target_pairs={{0,4},{1,5},{2,6},{3,7},{4,0},{5,1},{6,2},{7,3},{8,12},{9,13},{10,... | collective-permute-start | bytes 152 | tf_op jit(solution)/shard_map/ppermute | solution.py:25
  5.2 4.7 %collective-permute-start = (s32[3,1,4]{2,1,0:T(1,128)}, s32[3,1,4]{2,1,0:T(1,128)S(1)}, u32[]{:S(2)}, u32[]{:S(2)}) collective-permute-start(s32[3,1,4]{2,1,0:T(1,128)} %bitcast.30), channel_id=1, source_target_pairs={{0,8},{1,9},{2,10},{3,11},{4,12},{5,13},{6,14},{7,15},{8,0},{9,1},... | collective-permute-start | bytes 152 | tf_op jit(solution)/shard_map/ppermute | solution.py:25
  7.8 1.0 %copy-start.3 = (bf16[1024,256]{1,0:T(8,128)(2,1)S(1)}, bf16[1024,256]{1,0:T(8,128)(2,1)}, u32[]{:S(2)}) copy-start(bf16[1024,256]{1,0:T(8,128)(2,1)} %param.14) | copy-start | bytes 1572868
  8.9 4.8 %copy-start.1 = (bf16[1,3,4,128,128]{4,3,2,1,0:T(8,128)(2,1)S(1)}, bf16[1,3,4,128,128]{4,3,2,1,0:T(8,128)(2,1)}, u32[]{:S(2)}) copy-start(bf16[1,3,4,128,128]{4,3,2,1,0:T(8,128)(2,1)} %param.21) | copy-start | bytes 1179652
  8.9 4.8 %copy-start.6 = (bf16[256,256]{1,0:T(8,128)(2,1)S(1)}, bf16[256,256]{1,0:T(8,128)(2,1)}, u32[]{:S(2)}) copy-start(bf16[256,256]{1,0:T(8,128)(2,1)} %refs_6_.3) | copy-start | bytes 393220
  9.9 3.8 %copy-start.10 = (f32[256]{0:T(256)S(1)}, f32[256]{0:T(256)}, u32[]{:S(2)}) copy-start(f32[256]{0:T(256)} %param.24) | copy-start | bytes 3076
  9.9 3.8 %copy-start.11 = (s32[1,3]{1,0:T(1,128)S(1)}, s32[1,3]{1,0:T(1,128)}, u32[]{:S(2)}) copy-start(s32[1,3]{1,0:T(1,128)} %count.1) | copy-start | bytes 40
  10.1 12.9 %collective-permute-start.3 = (bf16[4,128,256]{2,1,0:T(8,128)(2,1)S(1)}, bf16[4,128,256]{2,1,0:T(8,128)(2,1)S(1)}, u32[]{:S(2)}, u32[]{:S(2)}) collective-permute-start(bf16[4,128,256]{2,1,0:T(8,128)(2,1)S(1)} %get-tuple-element.49), channel_id=1, source_target_pairs={{0,8},{1,9},{2,10},{3,11},{4,12},{5,13},{6,14},{7,15},{8,0},{9,1},... | collective-permute-start | bytes 786440 | tf_op jit(solution)/shard_map/ppermute | solution.py:25
  12.7 11.6 %collective-permute-start.4 = (bf16[4,128,256]{2,1,0:T(8,128)(2,1)S(1)}, bf16[4,128,256]{2,1,0:T(8,128)(2,1)S(1)}, u32[]{:S(2)}, u32[]{:S(2)}) collective-permute-start(bf16[4,128,256]{2,1,0:T(8,128)(2,1)S(1)} %get-tuple-element.50), channel_id=1, source_target_pairs={{0,4},{1,5},{2,6},{3,7},{4,0},{5,1},{6,2},{7,3},{8,12},{9,13},{10,... | collective-permute-start | bytes 786440 | tf_op jit(solution)/shard_map/ppermute | solution.py:25
  13.2 11.1 %collective-permute-start.5 = (bf16[4,128,256]{2,1,0:T(8,128)(2,1)S(1)}, bf16[4,128,256]{2,1,0:T(8,128)(2,1)S(1)}, u32[]{:S(2)}, u32[]{:S(2)}) collective-permute-start(bf16[4,128,256]{2,1,0:T(8,128)(2,1)S(1)} %get-tuple-element.51), channel_id=1, source_target_pairs={{0,2},{1,3},{2,0},{3,1},{4,6},{5,7},{6,4},{7,5},{8,10},{9,11},{10,... | collective-permute-start | bytes 786440 | tf_op jit(solution)/shard_map/ppermute | solution.py:25
  13.7 0.7 copy-start.8
  13.7 0.7 %copy-start.9 = (s32[1,3,4]{2,0,1:T(1,128)S(1)}, s32[1,3,4]{2,0,1:T(1,128)}, u32[]{:S(2)}) copy-start(s32[1,3,4]{2,0,1:T(1,128)} %param.19) | copy-start | bytes 148
  14.4 9.9 %copy-start.2 = (bf16[256,256]{1,0:T(8,128)(2,1)S(1)}, bf16[256,256]{1,0:T(8,128)(2,1)}, u32[]{:S(2)}) copy-start(bf16[256,256]{1,0:T(8,128)(2,1)} %w1_near.1) | copy-start | bytes 393220
  14.4 9.9 %copy-start.5 = (bf16[256,128]{1,0:T(8,128)(2,1)S(1)}, bf16[256,128]{1,0:T(8,128)(2,1)}, u32[]{:S(2)}) copy-start(bf16[256,128]{1,0:T(8,128)(2,1)} %refs_6_.5) | copy-start | bytes 196612
  24.3 3.4 %copy-start.4 = (bf16[256,128]{1,0:T(8,128)(2,1)S(1)}, bf16[256,128]{1,0:T(8,128)(2,1)}, u32[]{:S(2)}) copy-start(bf16[256,128]{1,0:T(8,128)(2,1)} %w2_self.3) | copy-start | bytes 196612
  25.3 7.3 %collective-permute-start.6 = (bf16[4,128,128]{2,1,0:T(8,128)(2,1)S(1)}, bf16[4,128,128]{2,1,0:T(8,128)(2,1)S(1)}, u32[]{:S(2)}, u32[]{:S(2)}) collective-permute-start(bf16[4,128,128]{2,1,0:T(8,128)(2,1)S(1)} %get-tuple-element.54), channel_id=1, source_target_pairs={{0,8},{1,9},{2,10},{3,11},{4,12},{5,13},{6,14},{7,15},{8,0},{9,1},... | collective-permute-start | bytes 393224 | tf_op jit(solution)/shard_map/ppermute | solution.py:25
  25.4 7.2 %collective-permute-start.7 = (bf16[4,128,128]{2,1,0:T(8,128)(2,1)S(1)}, bf16[4,128,128]{2,1,0:T(8,128)(2,1)S(1)}, u32[]{:S(2)}, u32[]{:S(2)}) collective-permute-start(bf16[4,128,128]{2,1,0:T(8,128)(2,1)S(1)} %get-tuple-element.55), channel_id=1, source_target_pairs={{0,4},{1,5},{2,6},{3,7},{4,0},{5,1},{6,2},{7,3},{8,12},{9,13},{10,... | collective-permute-start | bytes 393224 | tf_op jit(solution)/shard_map/ppermute | solution.py:25
  27.1 5.4 %collective-permute-start.8 = (bf16[4,128,128]{2,1,0:T(8,128)(2,1)S(1)}, bf16[4,128,128]{2,1,0:T(8,128)(2,1)S(1)}, u32[]{:S(2)}, u32[]{:S(2)}) collective-permute-start(bf16[4,128,128]{2,1,0:T(8,128)(2,1)S(1)} %get-tuple-element.56), channel_id=1, source_target_pairs={{0,2},{1,3},{2,0},{3,1},{4,6},{5,7},{6,4},{7,5},{8,10},{9,11},{10,... | collective-permute-start | bytes 393224 | tf_op jit(solution)/shard_map/ppermute | solution.py:25
  27.7 0.7 %copy-start.7 = (s32[1024]{0:T(1024)S(1)}, s32[1024]{0:T(1024)}, u32[]{:S(2)}) copy-start(s32[1024]{0:T(1024)} %param.15) | copy-start | bytes 12292
  27.7 0.7 %copy-start.12 = (f32[128]{0:T(128)S(1)}, f32[128]{0:T(128)}, u32[]{:S(2)}) copy-start(f32[128]{0:T(128)} %param.27) | copy-start | bytes 1540
  33.2 7.2 %collective-permute-start.9 = (bf16[4,128,128]{2,1,0:T(8,128)(2,1)S(1)}, bf16[4,128,128]{2,1,0:T(8,128)(2,1)S(1)}, u32[]{:S(2)}, u32[]{:S(2)}) collective-permute-start(bf16[4,128,128]{2,1,0:T(8,128)(2,1)S(1)} %get-tuple-element.67), channel_id=1, source_target_pairs={{0,8},{1,9},{2,10},{3,11},{4,12},{5,13},{6,14},{7,15},{8,0},{9,1},... | collective-permute-start | bytes 393224 | tf_op jit(solution)/shard_map/ppermute | solution.py:25
  34.3 6.3 %collective-permute-start.10 = (bf16[4,128,128]{2,1,0:T(8,128)(2,1)S(1)}, bf16[4,128,128]{2,1,0:T(8,128)(2,1)S(1)}, u32[]{:S(2)}, u32[]{:S(2)}) collective-permute-start(bf16[4,128,128]{2,1,0:T(8,128)(2,1)S(1)} %get-tuple-element.68), channel_id=1, source_target_pairs={{0,4},{1,5},{2,6},{3,7},{4,0},{5,1},{6,2},{7,3},{8,12},{9,13},{10,... | collective-permute-start | bytes 393224 | tf_op jit(solution)/shard_map/ppermute | solution.py:25
  36.1 5.0 %collective-permute-start.11 = (bf16[4,128,128]{2,1,0:T(8,128)(2,1)S(1)}, bf16[4,128,128]{2,1,0:T(8,128)(2,1)S(1)}, u32[]{:S(2)}, u32[]{:S(2)}) collective-permute-start(bf16[4,128,128]{2,1,0:T(8,128)(2,1)S(1)} %get-tuple-element.69), channel_id=1, source_target_pairs={{0,2},{1,3},{2,0},{3,1},{4,6},{5,7},{6,4},{7,5},{8,10},{9,11},{10,... | collective-permute-start | bytes 393224 | tf_op jit(solution)/shard_map/ppermute | solution.py:25
  42.1 1.5 %collective-permute-start.12 = (bf16[832,128]{1,0:T(8,128)(2,1)S(1)}, bf16[832,128]{1,0:T(8,128)(2,1)S(1)}, u32[]{:S(2)}, u32[]{:S(2)}) collective-permute-start(bf16[832,128]{1,0:T(8,128)(2,1)S(1)} %get-tuple-element.79), channel_id=1, source_target_pairs={{0,1},{1,0},{2,3},{3,2},{4,5},{5,4},{6,7},{7,6},{8,9},{9,8},{10,11... | collective-permute-start | bytes 638984 | tf_op jit(solution)/shard_map/ppermute | solution.py:25
  65.9 1.5 %collective-permute-start.13 = (bf16[832,128]{1,0:T(8,128)(2,1)S(1)}, bf16[832,128]{1,0:T(8,128)(2,1)S(1)}, u32[]{:S(2)}, u32[]{:S(2)}) collective-permute-start(bf16[832,128]{1,0:T(8,128)(2,1)S(1)} %bitcast.17), channel_id=1, source_target_pairs={{0,1},{1,0},{2,3},{3,2},{4,5},{5,4},{6,7},{7,6},{8,9},{9,8},{10,11... | collective-permute-start | bytes 638984 | tf_op jit(solution)/shard_map/ppermute | solution.py:25

commit v5 on v4

--- a/solution.py
+++ b/solution.py
@@ -8,7 +8,6 @@
 from jax.sharding import PartitionSpec as P
 
 AXES = ("dom", "sub", "feat")
-CHIPS = ("dom", "sub")
 SMEM = pl.BlockSpec(memory_space=pltpu.SMEM)
 VMEM = pl.BlockSpec(memory_space=pltpu.VMEM)
 VMEM_LIMIT = 8 * 2**20
@@ -244,18 +243,27 @@
     out[...] = value[...]
 
 
-def pair_body(keep, arrived, out):
-    out[...] = (keep[...] + arrived[...].astype(F32)).astype(BF16)
-
-
-def chips_body(arrived, out):
-    chips = arrived.shape[0]
-    total = arrived[0].astype(F32)
-    for c in range(1, chips):
-        total = total + arrived[c].astype(F32)
-    total = total.astype(BF16)
-    for c in range(chips):
-        out[c] = total
+def spread_body(keep, arrived, own, *sends):
+    rows = own.shape[0]
+    for distance, out in enumerate((own, *sends)):
+        owner = jnp.bitwise_xor(lax.axis_index("dom"), distance)
+        here = pl.ds(pl.multiple_of(owner * rows, 16), rows)
+        out[...] = (keep[here, :] + arrived[here, :].astype(F32)).astype(out.dtype)
+
+
+def gather_body(own, *refs):
+    total = own[...].astype(F32)
+    for arrived in refs[:-1]:
+        total = total + arrived[...].astype(F32)
+    refs[-1][...] = total.astype(BF16)
+
+
+def join_body(*refs):
+    out = refs[-1]
+    rows = refs[0].shape[0]
+    for distance, piece in enumerate(refs[:-1]):
+        owner = jnp.bitwise_xor(lax.axis_index("dom"), distance)
+        out[pl.ds(pl.multiple_of(owner * rows, 16), rows), :] = piece[...]
 
 
 def unpack_body(mine, other, g1_self, g1_near, g1_bias, g2_self, g2_near, g2_bias, packed):
@@ -302,7 +310,6 @@
     nodes = tiles * size
     total_bits = lax.axis_size(AXES).bit_length() - 1
     masks = [1 << (total_bits - 1 - colour) for colour in range(rounds)]
-    chips = lax.axis_size(CHIPS)
     blocks = features.reshape(tiles, size, width_in)
     edges = cross_values[0]
     bias_one_row = bias_one.reshape(1, hidden_width)
@@ -418,9 +425,10 @@
         moved=4 * 2**20,
     )
 
+    lines, columns = lax.axis_size("dom"), lax.axis_size("sub")
     rows = (2 * width_in * hidden_width + 2 * hidden_width * classes + hidden_width + classes) // 128
-    piece = -(-rows // (2 * chips * 8)) * 8
-    half = piece * chips
+    piece = -(-rows // (2 * lines * 16)) * 16
+    half = piece * lines
     hidden_grad, send, keep = run(
         functools.partial(back_body, at, rounds),
         [SMEM] + [VMEM] * (rounds + 9),
@@ -450,16 +458,27 @@
         [hidden_grad], moved=4 * nodes * hidden_width,
     )
 
-    pair = run(
-        pair_body, [VMEM] * 2, VMEM, struct((half, 128), BF16), [],
+    along = [distance * 2 * columns for distance in range(1, lines)]
+    piece_struct = struct((piece, 128), BF16)
+    own, *sends = run(
+        spread_body, [VMEM] * 2, [VMEM] * lines,
+        [struct((piece, 128), F32)] + [piece_struct] * (lines - 1), [],
         [keep, arrived], flops=half * 128, moved=half * 128 * 8,
     )
-    pieces = lax.all_to_all(pair.reshape(chips, piece, 128), CHIPS, 0, 0)
-    copies = run(
-        chips_body, [VMEM], VMEM, struct((chips, piece, 128), BF16), [],
-        [pieces], flops=half * 128, moved=half * 128 * 4,
-    )
-    mine = lax.all_to_all(copies, CHIPS, 0, 0).reshape(half, 128)
+    arrived = [swapped(value, mask) for value, mask in zip(sends, along)]
+    total = run(
+        gather_body, [VMEM] * lines, VMEM, piece_struct, [],
+        [own, *arrived], flops=half * 128, moved=half * 128 * 2,
+    )
+    for bit in range(columns.bit_length() - 1):
+        total = run(
+            gather_body, [VMEM] * 2, VMEM, piece_struct, [],
+            [total, swapped(total, 2 << bit)], flops=piece * 128, moved=piece * 128 * 6,
+        )
+    mine = run(
+        join_body, [VMEM] * lines, VMEM, struct((half, 128), BF16), [],
+        [total, *(swapped(total, mask) for mask in along)], moved=half * 128 * 4,
+    )
     other = swapped(mine, 1)
     g1_self, g1_near, g1_bias, g2_self, g2_near, g2_bias = run(
         unpack_body,

time: 68.6 us -> 66.2 us (0.965)
  blocking collectives: 22.2 us -> 0 us
  waiting for transfers between devices: 17.7 us -> 27.8 us
  starting transfers between devices: 16.7 us -> 26.2 us
    all_to_all x2 -> x0, blocking collectives: 22.2 us -> none  [the longest x1 11.2 us: shards(): pieces = lax.all_to_all(pair.reshape(chips, piece, 128), CHIPS, 0, 0)]
    ppermute x14 -> x21, waiting for transfers between devices: 17.7 us -> 27.8 us  [swapped(): return lax.ppermute(value, AXES, pairs)]
    ppermute x14 -> x21, starting transfers between devices: 16.7 us -> 26.2 us  [swapped(): return lax.ppermute(value, AXES, pairs)]
    pallas_call x12 -> x14, Pallas kernels: 8.62 us -> 8.65 us  [run(): pl.pallas_call(body, in_specs=in_specs, out_specs=out_specs, out_shape=ou...]
  transfers between devices with their start and end apart: 14 -> 21, of which waited for: 9 -> 15; matrix products, arithmetic and copies ran while one was open for 0% -> 0% of each run, Pallas kernels for 7% -> 7%
where the time goes in v5:
time: 66.2 us; the launch traced here: 66 us
  waiting for transfers between devices  27.8 us (42%)
  starting transfers between devices  26.2 us (40%)
  Pallas kernels  8.65 us (13%)
  local copies, waits for them, and re-layouts  2.42 us (4%)
  between operations  0.83 us (1%)
    ppermute x21, waiting for transfers between devices, swapped(): return lax.ppermute(value, AXES, pairs)  27.8 us
    ppermute x21, starting transfers between devices, swapped(): return lax.ppermute(value, AXES, pairs)  26.2 us
    pallas_call x14, Pallas kernels, run(): pl.pallas_call(body, in_specs=in_specs, out_specs=out_specs, out_shape=ou...  8.65 us
    unnamed x26, local copies, waits for them, and re-layouts  2.42 us
  transfers between devices with their start and end apart: 21, of which 15 were waited for; matrix products, arithmetic and copies ran while one was open for 0% of the time, Pallas kernels for 7%

profile of v5, /device:TPU:0, one launch (start us, length us, event | category | flops | bytes accessed | tf_op | source)
XLA Modules:
  0.0 66.0 jit_solution(626222959598018184)
XLA Ops:
  0.6 3.0 %collective-permute-start.2 = (s32[3,1,4]{2,1,0:T(1,128)}, s32[3,1,4]{2,1,0:T(1,128)S(1)}, u32[]{:S(2)}, u32[]{:S(2)}) collective-permute-start(s32[3,1,4]{2,1,0:T(1,128)} %bitcast.23), channel_id=1, source_target_pairs={{0,2},{1,3},{2,0},{3,1},{4,6},{5,7},{6,4},{7,5},{8,10},{9,11},{10,... | collective-permute-start | bytes 152 | tf_op jit(solution)/shard_map/ppermute | solution.py:24
  3.6 1.6 %collective-permute-start.1 = (s32[3,1,4]{2,1,0:T(1,128)}, s32[3,1,4]{2,1,0:T(1,128)S(1)}, u32[]{:S(2)}, u32[]{:S(2)}) collective-permute-start(s32[3,1,4]{2,1,0:T(1,128)} %bitcast.24), channel_id=1, source_target_pairs={{0,4},{1,5},{2,6},{3,7},{4,0},{5,1},{6,2},{7,3},{8,12},{9,13},{10,... | collective-permute-start | bytes 152 | tf_op jit(solution)/shard_map/ppermute | solution.py:24
  5.2 2.6 %collective-permute-start = (s32[3,1,4]{2,1,0:T(1,128)}, s32[3,1,4]{2,1,0:T(1,128)S(1)}, u32[]{:S(2)}, u32[]{:S(2)}) collective-permute-start(s32[3,1,4]{2,1,0:T(1,128)} %bitcast.25), channel_id=1, source_target_pairs={{0,8},{1,9},{2,10},{3,11},{4,12},{5,13},{6,14},{7,15},{8,0},{9,1},... | collective-permute-start | bytes 152 | tf_op jit(solution)/shard_map/ppermute | solution.py:24
  7.8 1.0 %copy-done.3 = bf16[1024,256]{1,0:T(8,128)(2,1)S(1)} copy-done((bf16[1024,256]{1,0:T(8,128)(2,1)S(1)}, bf16[1024,256]{1,0:T(8,128)(2,1)}, u32[]{:S(2)}) %copy-start.3) | copy-done | bytes 524312
  9.0 1.0 %collective-permute-done.refs_0_ = s32[3,1,4]{2,1,0:T(1,128)S(1)} collective-permute-done((s32[3,1,4]{2,1,0:T(1,128)}, s32[3,1,4]{2,1,0:T(1,128)S(1)}, u32[]{:S(2)}, u32[]{:S(2)}) %collective-permute-start) | collective-permute-done | bytes 80 | tf_op jit(solution)/shard_map/ppermute | solution.py:24
  9.9 0.1 shard_map.199
  10.1 2.7 %collective-permute-start.3 = (bf16[4,128,256]{2,1,0:T(8,128)(2,1)S(1)}, bf16[4,128,256]{2,1,0:T(8,128)(2,1)S(1)}, u32[]{:S(2)}, u32[]{:S(2)}) collective-permute-start(bf16[4,128,256]{2,1,0:T(8,128)(2,1)S(1)} %get-tuple-element.53), channel_id=1, source_target_pairs={{0,8},{1,9},{2,10},{3,11},{4,12},{5,13},{6,14},{7,15},{8,0},{9,1},... | collective-permute-start | bytes 786440 | tf_op jit(solution)/shard_map/ppermute | solution.py:24
  12.7 0.4 collective-permute-start.4
  13.2 0.5 collective-permute-start.5
  13.8 0.6 copy-done.8
  14.4 0.0 copy-done.9
  14.4 1.5 %shard_map.198 = (s32[68]{0:T(128)S(4)}, f32[8,128,256]{2,1,0:T(8,128)S(1)}, f32[8,128,256]{2,1,0:T(8,128)S(1)}, bf16[256,1024]{1,0:T(8,128)(2,1)S(1)}, bf16[8,4...) custom-call(s32[4,8]{1,0:T(4,128)S(1)} %bitcast.17, s32[3,1,4]{2,1,0:T(1,128)S(1)} %bitcast.18, ...), custom_call_target="tpu_custom_call" | custom-call | flops 402653184 | bytes 8388608 | tf_op jit(solution)/shard_map/pallas_call | solution.py:36
  15.9 7.1 %collective-permute-done.3.refs_0_ = bf16[4,128,256]{2,1,0:T(8,128)(2,1)S(1)} collective-permute-done((bf16[4,128,256]{2,1,0:T(8,128)(2,1)S(1)}, bf16[4,128,256]{2,1,0:T(8,128)(2,1)S(1)}, u32[]{:S(2)}, u32[]{:S(2)}) %collective-permute-start.3) | collective-permute-done | bytes 262176 | tf_op jit(solution)/shard_map/ppermute | solution.py:24
  23.0 1.3 %collective-permute-done.4.refs_1_ = bf16[4,128,256]{2,1,0:T(8,128)(2,1)S(1)} collective-permute-done((bf16[4,128,256]{2,1,0:T(8,128)(2,1)S(1)}, bf16[4,128,256]{2,1,0:T(8,128)(2,1)S(1)}, u32[]{:S(2)}, u32[]{:S(2)}) %collective-permute-start.4) | collective-permute-done | bytes 262176 | tf_op jit(solution)/shard_map/ppermute | solution.py:24
  24.3 1.0 %shard_map.200 = (bf16[8,128,256]{2,1,0:T(8,128)(2,1)S(1)}, bf16[8,128,256]{2,1,0:T(8,128)(2,1)S(1)}, bf16[8,128,128]{2,1,0:T(8,128)(2,1)S(1)}, bf16[4,128,128]{...) custom-call(s32[68]{0:T(128)S(4)} %get-tuple-element.51.table, ...), custom_call_target="tpu_custom_call" | custom-call | flops 301989888 | bytes 8388608 | tf_op jit(solution)/shard_map/pallas_call | solution.py:36
  25.3 0.1 collective-permute-start.6
  25.4 1.8 %collective-permute-start.7 = (bf16[4,128,128]{2,1,0:T(8,128)(2,1)S(1)}, bf16[4,128,128]{2,1,0:T(8,128)(2,1)S(1)}, u32[]{:S(2)}, u32[]{:S(2)}) collective-permute-start(bf16[4,128,128]{2,1,0:T(8,128)(2,1)S(1)} %get-tuple-element.59), channel_id=1, source_target_pairs={{0,4},{1,5},{2,6},{3,7},{4,0},{5,1},{6,2},{7,3},{8,12},{9,13},{10,... | collective-permute-start | bytes 393224 | tf_op jit(solution)/shard_map/ppermute | solution.py:24
  27.1 0.5 collective-permute-start.8
  27.7 0.7 %copy-done.7 = s32[1024]{0:T(1024)S(1)} copy-done((s32[1024]{0:T(1024)S(1)}, s32[1024]{0:T(1024)}, u32[]{:S(2)}) %copy-start.7) | copy-done | bytes 4120
  28.4 0.9 %shard_map.201 = (f32[8,128,256]{2,1,0:T(8,128)S(1)}, f32[8,128,128]{2,1,0:T(8,128)S(1)}, f32[8,128,128]{2,1,0:T(8,128)S(1)}, bf16[256,1024]{1,0:T(8,128)(2,1)S(1)}, bf16[256,1024]{1,0:T(8,128)(2,1)S(1)}) custom-call(s32[68]{0:T(128)S(4)} %get-tuple-element.51.table, s32[8,128]{1,0:T(8,128)S(1)} %bitcast.16, bf16[8,4,128,128]{3,2,1,0:T(8,128)(2,1)S(1)} %copy-done, ...), custom_call_target="tpu_custom_call" | custom-call | flops 335544320 | bytes 6291456 | tf_op jit(solution)/shard_map/pallas_call | solution.py:36
  29.3 3.2 %collective-permute-done.6.refs_0_ = bf16[4,128,128]{2,1,0:T(8,128)(2,1)S(1)} collective-permute-done((bf16[4,128,128]{2,1,0:T(8,128)(2,1)S(1)}, bf16[4,128,128]{2,1,0:T(8,128)(2,1)S(1)}, u32[]{:S(2)}, u32[]{:S(2)}) %collective-permute-start.6) | collective-permute-done | bytes 131104 | tf_op jit(solution)/shard_map/ppermute | solution.py:24
  32.6 0.6 shard_map.202
  33.2 1.2 %collective-permute-start.9 = (bf16[4,128,128]{2,1,0:T(8,128)(2,1)S(1)}, bf16[4,128,128]{2,1,0:T(8,128)(2,1)S(1)}, u32[]{:S(2)}, u32[]{:S(2)}) collective-permute-start(bf16[4,128,128]{2,1,0:T(8,128)(2,1)S(1)} %get-tuple-element.71), channel_id=1, source_target_pairs={{0,8},{1,9},{2,10},{3,11},{4,12},{5,13},{6,14},{7,15},{8,0},{9,1},... | collective-permute-start | bytes 393224 | tf_op jit(solution)/shard_map/ppermute | solution.py:24
  34.3 1.7 %collective-permute-start.10 = (bf16[4,128,128]{2,1,0:T(8,128)(2,1)S(1)}, bf16[4,128,128]{2,1,0:T(8,128)(2,1)S(1)}, u32[]{:S(2)}, u32[]{:S(2)}) collective-permute-start(bf16[4,128,128]{2,1,0:T(8,128)(2,1)S(1)} %get-tuple-element.72), channel_id=1, source_target_pairs={{0,4},{1,5},{2,6},{3,7},{4,0},{5,1},{6,2},{7,3},{8,12},{9,13},{10,... | collective-permute-start | bytes 393224 | tf_op jit(solution)/shard_map/ppermute | solution.py:24
  36.1 0.5 collective-permute-start.11
  36.6 1.5 %shard_map.203 = (bf16[8,128,128]{2,1,0:T(8,128)(2,1)}, f32[8,128,128]{2,1,0:T(8,128)S(1)}, f32[8,128,256]{2,1,0:T(8,128)S(1)}, f32[256,128]{1,0:T(8,128)S(1)}, f32[1,128]{1,0:T(1,128)S(1)}) custom-call(s32[68]{0:T(128)S(4)} %get-tuple-element.51.table, bf16[8,4,128,128]{3,2,1,0:T(8,128)(2,1)S(1)} %get-tuple-element.52.values_t, ...), custom_call_target="tpu_custom_call" | custom-call | flops 268435456 | bytes 4194304 | tf_op jit(solution)/shard_map/pallas_call | solution.py:36
  38.1 2.3 %collective-permute-done.9.refs_0_ = bf16[4,128,128]{2,1,0:T(8,128)(2,1)S(1)} collective-permute-done((bf16[4,128,128]{2,1,0:T(8,128)(2,1)S(1)}, bf16[4,128,128]{2,1,0:T(8,128)(2,1)S(1)}, u32[]{:S(2)}, u32[]{:S(2)}) %collective-permute-start.9) | collective-permute-done | bytes 131104 | tf_op jit(solution)/shard_map/ppermute | solution.py:24
  40.4 0.2 collective-permute-done.10.refs_1_
  40.6 0.4 collective-permute-done.11.refs_2_
  41.0 1.1 %shard_map.204 = (bf16[8,128,256]{2,1,0:T(8,128)(2,1)S(1)}, bf16[832,128]{1,0:T(8,128)(2,1)S(1)}, f32[832,128]{1,0:T(8,128)S(1)}) custom-call(s32[68]{0:T(128)S(4)} %get-tuple-element.51.table, bf16[4,128,128]{2,1,0:T(8,128)(2,1)S(1)} %collective-permute-done.9.refs_0_, bf16[4,128,128]{2,1,0:T(8,128)(2,1)S(1)} %collective-permute-done.10.refs_1_, ...), custom_call_target="tpu_custom_call" | custom-call | flops 402653184 | bytes 6291456 | tf_op jit(solution)/shard_map/pallas_call | solution.py:36
  42.1 0.1 collective-permute-start.12
  42.2 1.5 %collective-permute-done.12.arrived = bf16[832,128]{1,0:T(8,128)(2,1)S(1)} collective-permute-done((bf16[832,128]{1,0:T(8,128)(2,1)S(1)}, bf16[832,128]{1,0:T(8,128)(2,1)S(1)}, u32[]{:S(2)}, u32[]{:S(2)}) %collective-permute-start.12) | collective-permute-done | bytes 213024 | tf_op jit(solution)/shard_map/ppermute | solution.py:24
  43.7 0.4 collective-permute-start.13
  44.1 1.8 %collective-permute-start.14 = (bf16[208,128]{1,0:T(8,128)(2,1)S(1)}, bf16[208,128]{1,0:T(8,128)(2,1)S(1)}, u32[]{:S(2)}, u32[]{:S(2)}) collective-permute-start(bf16[208,128]{1,0:T(8,128)(2,1)S(1)} %get-tuple-element.86), channel_id=1, source_target_pairs={{0,8},{1,9},{2,10},{3,11},{4,12},{5,13},{6,14},{7,15},{8,0},{9,1},... | collective-permute-start | bytes 159752 | tf_op jit(solution)/shard_map/ppermute | solution.py:24
  45.9 2.2 %collective-permute-start.15 = (bf16[208,128]{1,0:T(8,128)(2,1)S(1)}, bf16[208,128]{1,0:T(8,128)(2,1)S(1)}, u32[]{:S(2)}, u32[]{:S(2)}) collective-permute-start(bf16[208,128]{1,0:T(8,128)(2,1)S(1)} %get-tuple-element.87), channel_id=1, source_target_pairs={{0,12},{1,13},{2,14},{3,15},{4,8},{5,9},{6,10},{7,11},{8,4},{9,5},... | collective-permute-start | bytes 159752 | tf_op jit(solution)/shard_map/ppermute | solution.py:24
  48.2 0.3 collective-permute-done.13.refs_0_
  48.5 2.4 %collective-permute-done.14.refs_1_ = bf16[208,128]{1,0:T(8,128)(2,1)S(1)} collective-permute-done((bf16[208,128]{1,0:T(8,128)(2,1)S(1)}, bf16[208,128]{1,0:T(8,128)(2,1)S(1)}, u32[]{:S(2)}, u32[]{:S(2)}) %collective-permute-start.14) | collective-permute-done | bytes 53280 | tf_op jit(solution)/shard_map/ppermute | solution.py:24
  50.9 1.1 %collective-permute-done.15.refs_2_ = bf16[208,128]{1,0:T(8,128)(2,1)S(1)} collective-permute-done((bf16[208,128]{1,0:T(8,128)(2,1)S(1)}, bf16[208,128]{1,0:T(8,128)(2,1)S(1)}, u32[]{:S(2)}, u32[]{:S(2)}) %collective-permute-start.15) | collective-permute-done | bytes 53280 | tf_op jit(solution)/shard_map/ppermute | solution.py:24
  52.0 0.6 collective-permute-start.16
  52.6 3.6 %collective-permute-done.16.refs_0_ = bf16[208,128]{1,0:T(8,128)(2,1)S(1)} collective-permute-done((bf16[208,128]{1,0:T(8,128)(2,1)S(1)}, bf16[208,128]{1,0:T(8,128)(2,1)S(1)}, u32[]{:S(2)}, u32[]{:S(2)}) %collective-permute-start.16) | collective-permute-done | bytes 53280 | tf_op jit(solution)/shard_map/ppermute | solution.py:24
  56.2 2.2 %collective-permute-start.19 = (bf16[208,128]{1,0:T(8,128)(2,1)S(1)}, bf16[208,128]{1,0:T(8,128)(2,1)S(1)}, u32[]{:S(2)}, u32[]{:S(2)}) collective-permute-start(bf16[208,128]{1,0:T(8,128)(2,1)S(1)} %shard_map.208.refs_0_), channel_id=1, source_target_pairs={{0,12},{1,13},{2,14},{3,15},{4,8},{5,9},{6,10},{7,11},{8,4},{9,5},... | collective-permute-start | bytes 159752 | tf_op jit(solution)/shard_map/ppermute | solution.py:24
  58.4 2.3 %collective-permute-start.17 = (bf16[208,128]{1,0:T(8,128)(2,1)S(1)}, bf16[208,128]{1,0:T(8,128)(2,1)S(1)}, u32[]{:S(2)}, u32[]{:S(2)}) collective-permute-start(bf16[208,128]{1,0:T(8,128)(2,1)S(1)} %shard_map.208.refs_0_), channel_id=1, source_target_pairs={{0,4},{1,5},{2,6},{3,7},{4,0},{5,1},{6,2},{7,3},{8,12},{9,13},{10,... | collective-permute-start | bytes 159752 | tf_op jit(solution)/shard_map/ppermute | solution.py:24
  60.7 1.5 %collective-permute-done.19.refs_3_ = bf16[208,128]{1,0:T(8,128)(2,1)S(1)} collective-permute-done((bf16[208,128]{1,0:T(8,128)(2,1)S(1)}, bf16[208,128]{1,0:T(8,128)(2,1)S(1)}, u32[]{:S(2)}, u32[]{:S(2)}) %collective-permute-start.19) | collective-permute-done | bytes 53280 | tf_op jit(solution)/shard_map/ppermute | solution.py:24
  62.2 1.2 %collective-permute-done.18.refs_2_ = bf16[208,128]{1,0:T(8,128)(2,1)S(1)} collective-permute-done((bf16[208,128]{1,0:T(8,128)(2,1)S(1)}, bf16[208,128]{1,0:T(8,128)(2,1)S(1)}, u32[]{:S(2)}, u32[]{:S(2)}) %collective-permute-start.18) | collective-permute-done | bytes 53280 | tf_op jit(solution)/shard_map/ppermute | solution.py:24
  63.5 0.1 collective-permute-start.20
  63.6 0.8 %shard_map.205 = bf16[8,128,256]{2,1,0:T(8,128)(2,1)} custom-call(bf16[8,128,256]{2,1,0:T(8,128)(2,1)S(1)} %get-tuple-element.81.value), custom_call_target="tpu_custom_call" | custom-call | bytes 1048576 | tf_op jit(solution)/shard_map/pallas_call | solution.py:36
  64.4 0.6 collective-permute-done.20.other
  65.0 1.0 %shard_map.210 = (f32[256,256]{1,0:T(8,128)}, f32[256,256]{1,0:T(8,128)}, f32[1,256]{1,0:T(1,128)}, f32[256,128]{1,0:T(8,128)}, f32[256,128]{1,0:T(8,128)}, /*index=5*/f32[1,128]{1,0:T(1,128)}) custom-call(bf16[832,128]{1,0:T(8,128)(2,1)S(1)} %shard_map.209.mine, bf16[832,128]{1,0:T(8,128)(2,1)S(1)} %collective-permute-done.20.other), custom_call_target="tpu_custom_call" | custom-call | bytes 1277952 | tf_op jit(solution)/shard_map/pallas_call | solution.py:36
  (34 shorter events, 0.2 us)
Async XLA Ops:
  0.6 13.1 %copy-start = (bf16[8,4,128,128]{3,2,1,0:T(8,128)(2,1)S(1)}, bf16[8,4,128,128]{3,2,1,0:T(8,128)(2,1)}, u32[]{:S(2)}) copy-start(bf16[8,4,128,128]{3,2,1,0:T(8,128)(2,1)} %values.1) | copy-start | bytes 3145732
  0.6 8.3 %collective-permute-start.2 = (s32[3,1,4]{2,1,0:T(1,128)}, s32[3,1,4]{2,1,0:T(1,128)S(1)}, u32[]{:S(2)}, u32[]{:S(2)}) collective-permute-start(s32[3,1,4]{2,1,0:T(1,128)} %bitcast.23), channel_id=1, source_target_pairs={{0,2},{1,3},{2,0},{3,1},{4,6},{5,7},{6,4},{7,5},{8,10},{9,11},{10,... | collective-permute-start | bytes 152 | tf_op jit(solution)/shard_map/ppermute | solution.py:24
  3.6 5.3 %collective-permute-start.1 = (s32[3,1,4]{2,1,0:T(1,128)}, s32[3,1,4]{2,1,0:T(1,128)S(1)}, u32[]{:S(2)}, u32[]{:S(2)}) collective-permute-start(s32[3,1,4]{2,1,0:T(1,128)} %bitcast.24), channel_id=1, source_target_pairs={{0,4},{1,5},{2,6},{3,7},{4,0},{5,1},{6,2},{7,3},{8,12},{9,13},{10,... | collective-permute-start | bytes 152 | tf_op jit(solution)/shard_map/ppermute | solution.py:24
  5.2 4.7 %collective-permute-start = (s32[3,1,4]{2,1,0:T(1,128)}, s32[3,1,4]{2,1,0:T(1,128)S(1)}, u32[]{:S(2)}, u32[]{:S(2)}) collective-permute-start(s32[3,1,4]{2,1,0:T(1,128)} %bitcast.25), channel_id=1, source_target_pairs={{0,8},{1,9},{2,10},{3,11},{4,12},{5,13},{6,14},{7,15},{8,0},{9,1},... | collective-permute-start | bytes 152 | tf_op jit(solution)/shard_map/ppermute | solution.py:24
  7.8 1.0 %copy-start.3 = (bf16[1024,256]{1,0:T(8,128)(2,1)S(1)}, bf16[1024,256]{1,0:T(8,128)(2,1)}, u32[]{:S(2)}) copy-start(bf16[1024,256]{1,0:T(8,128)(2,1)} %param.14) | copy-start | bytes 1572868
  8.9 4.8 %copy-start.1 = (bf16[1,3,4,128,128]{4,3,2,1,0:T(8,128)(2,1)S(1)}, bf16[1,3,4,128,128]{4,3,2,1,0:T(8,128)(2,1)}, u32[]{:S(2)}) copy-start(bf16[1,3,4,128,128]{4,3,2,1,0:T(8,128)(2,1)} %param.21) | copy-start | bytes 1179652
  8.9 4.8 %copy-start.6 = (bf16[256,256]{1,0:T(8,128)(2,1)S(1)}, bf16[256,256]{1,0:T(8,128)(2,1)}, u32[]{:S(2)}) copy-start(bf16[256,256]{1,0:T(8,128)(2,1)} %refs_6_.3) | copy-start | bytes 393220
  9.9 3.8 %copy-start.10 = (f32[256]{0:T(256)S(1)}, f32[256]{0:T(256)}, u32[]{:S(2)}) copy-start(f32[256]{0:T(256)} %param.24) | copy-start | bytes 3076
  9.9 3.8 %copy-start.11 = (s32[1,3]{1,0:T(1,128)S(1)}, s32[1,3]{1,0:T(1,128)}, u32[]{:S(2)}) copy-start(s32[1,3]{1,0:T(1,128)} %count.1) | copy-start | bytes 40
  10.1 12.9 %collective-permute-start.3 = (bf16[4,128,256]{2,1,0:T(8,128)(2,1)S(1)}, bf16[4,128,256]{2,1,0:T(8,128)(2,1)S(1)}, u32[]{:S(2)}, u32[]{:S(2)}) collective-permute-start(bf16[4,128,256]{2,1,0:T(8,128)(2,1)S(1)} %get-tuple-element.53), channel_id=1, source_target_pairs={{0,8},{1,9},{2,10},{3,11},{4,12},{5,13},{6,14},{7,15},{8,0},{9,1},... | collective-permute-start | bytes 786440 | tf_op jit(solution)/shard_map/ppermute | solution.py:24
  12.7 11.6 %collective-permute-start.4 = (bf16[4,128,256]{2,1,0:T(8,128)(2,1)S(1)}, bf16[4,128,256]{2,1,0:T(8,128)(2,1)S(1)}, u32[]{:S(2)}, u32[]{:S(2)}) collective-permute-start(bf16[4,128,256]{2,1,0:T(8,128)(2,1)S(1)} %get-tuple-element.54), channel_id=1, source_target_pairs={{0,4},{1,5},{2,6},{3,7},{4,0},{5,1},{6,2},{7,3},{8,12},{9,13},{10,... | collective-permute-start | bytes 786440 | tf_op jit(solution)/shard_map/ppermute | solution.py:24
  13.2 11.1 %collective-permute-start.5 = (bf16[4,128,256]{2,1,0:T(8,128)(2,1)S(1)}, bf16[4,128,256]{2,1,0:T(8,128)(2,1)S(1)}, u32[]{:S(2)}, u32[]{:S(2)}) collective-permute-start(bf16[4,128,256]{2,1,0:T(8,128)(2,1)S(1)} %get-tuple-element.55), channel_id=1, source_target_pairs={{0,2},{1,3},{2,0},{3,1},{4,6},{5,7},{6,4},{7,5},{8,10},{9,11},{10,... | collective-permute-start | bytes 786440 | tf_op jit(solution)/shard_map/ppermute | solution.py:24
  13.7 0.7 %copy-start.8 = (s32[8,4]{0,1:T(4,128)S(1)}, s32[8,4]{0,1:T(4,128)}, u32[]{:S(2)}) copy-start(s32[8,4]{0,1:T(4,128)} %param.16) | copy-start | bytes 388
  13.7 0.7 %copy-start.9 = (s32[1,3,4]{2,0,1:T(1,128)S(1)}, s32[1,3,4]{2,0,1:T(1,128)}, u32[]{:S(2)}) copy-start(s32[1,3,4]{2,0,1:T(1,128)} %param.19) | copy-start | bytes 148
  14.4 9.9 %copy-start.2 = (bf16[256,256]{1,0:T(8,128)(2,1)S(1)}, bf16[256,256]{1,0:T(8,128)(2,1)}, u32[]{:S(2)}) copy-start(bf16[256,256]{1,0:T(8,128)(2,1)} %w1_near.1) | copy-start | bytes 393220
  14.4 9.9 %copy-start.5 = (bf16[256,128]{1,0:T(8,128)(2,1)S(1)}, bf16[256,128]{1,0:T(8,128)(2,1)}, u32[]{:S(2)}) copy-start(bf16[256,128]{1,0:T(8,128)(2,1)} %refs_6_.5) | copy-start | bytes 196612
  24.3 3.4 %copy-start.4 = (bf16[256,128]{1,0:T(8,128)(2,1)S(1)}, bf16[256,128]{1,0:T(8,128)(2,1)}, u32[]{:S(2)}) copy-start(bf16[256,128]{1,0:T(8,128)(2,1)} %w2_self.3) | copy-start | bytes 196612
  25.3 7.3 %collective-permute-start.6 = (bf16[4,128,128]{2,1,0:T(8,128)(2,1)S(1)}, bf16[4,128,128]{2,1,0:T(8,128)(2,1)S(1)}, u32[]{:S(2)}, u32[]{:S(2)}) collective-permute-start(bf16[4,128,128]{2,1,0:T(8,128)(2,1)S(1)} %get-tuple-element.58), channel_id=1, source_target_pairs={{0,8},{1,9},{2,10},{3,11},{4,12},{5,13},{6,14},{7,15},{8,0},{9,1},... | collective-permute-start | bytes 393224 | tf_op jit(solution)/shard_map/ppermute | solution.py:24
  25.4 7.2 %collective-permute-start.7 = (bf16[4,128,128]{2,1,0:T(8,128)(2,1)S(1)}, bf16[4,128,128]{2,1,0:T(8,128)(2,1)S(1)}, u32[]{:S(2)}, u32[]{:S(2)}) collective-permute-start(bf16[4,128,128]{2,1,0:T(8,128)(2,1)S(1)} %get-tuple-element.59), channel_id=1, source_target_pairs={{0,4},{1,5},{2,6},{3,7},{4,0},{5,1},{6,2},{7,3},{8,12},{9,13},{10,... | collective-permute-start | bytes 393224 | tf_op jit(solution)/shard_map/ppermute | solution.py:24
  27.1 5.4 %collective-permute-start.8 = (bf16[4,128,128]{2,1,0:T(8,128)(2,1)S(1)}, bf16[4,128,128]{2,1,0:T(8,128)(2,1)S(1)}, u32[]{:S(2)}, u32[]{:S(2)}) collective-permute-start(bf16[4,128,128]{2,1,0:T(8,128)(2,1)S(1)} %get-tuple-element.60), channel_id=1, source_target_pairs={{0,2},{1,3},{2,0},{3,1},{4,6},{5,7},{6,4},{7,5},{8,10},{9,11},{10,... | collective-permute-start | bytes 393224 | tf_op jit(solution)/shard_map/ppermute | solution.py:24
  27.7 0.7 %copy-start.7 = (s32[1024]{0:T(1024)S(1)}, s32[1024]{0:T(1024)}, u32[]{:S(2)}) copy-start(s32[1024]{0:T(1024)} %param.15) | copy-start | bytes 12292
  27.7 0.7 %copy-start.12 = (f32[128]{0:T(128)S(1)}, f32[128]{0:T(128)}, u32[]{:S(2)}) copy-start(f32[128]{0:T(128)} %param.27) | copy-start | bytes 1540
  33.2 7.2 %collective-permute-start.9 = (bf16[4,128,128]{2,1,0:T(8,128)(2,1)S(1)}, bf16[4,128,128]{2,1,0:T(8,128)(2,1)S(1)}, u32[]{:S(2)}, u32[]{:S(2)}) collective-permute-start(bf16[4,128,128]{2,1,0:T(8,128)(2,1)S(1)} %get-tuple-element.71), channel_id=1, source_target_pairs={{0,8},{1,9},{2,10},{3,11},{4,12},{5,13},{6,14},{7,15},{8,0},{9,1},... | collective-permute-start | bytes 393224 | tf_op jit(solution)/shard_map/ppermute | solution.py:24
  34.3 6.3 %collective-permute-start.10 = (bf16[4,128,128]{2,1,0:T(8,128)(2,1)S(1)}, bf16[4,128,128]{2,1,0:T(8,128)(2,1)S(1)}, u32[]{:S(2)}, u32[]{:S(2)}) collective-permute-start(bf16[4,128,128]{2,1,0:T(8,128)(2,1)S(1)} %get-tuple-element.72), channel_id=1, source_target_pairs={{0,4},{1,5},{2,6},{3,7},{4,0},{5,1},{6,2},{7,3},{8,12},{9,13},{10,... | collective-permute-start | bytes 393224 | tf_op jit(solution)/shard_map/ppermute | solution.py:24
  36.1 5.0 %collective-permute-start.11 = (bf16[4,128,128]{2,1,0:T(8,128)(2,1)S(1)}, bf16[4,128,128]{2,1,0:T(8,128)(2,1)S(1)}, u32[]{:S(2)}, u32[]{:S(2)}) collective-permute-start(bf16[4,128,128]{2,1,0:T(8,128)(2,1)S(1)} %get-tuple-element.73), channel_id=1, source_target_pairs={{0,2},{1,3},{2,0},{3,1},{4,6},{5,7},{6,4},{7,5},{8,10},{9,11},{10,... | collective-permute-start | bytes 393224 | tf_op jit(solution)/shard_map/ppermute | solution.py:24
  42.1 1.5 %collective-permute-start.12 = (bf16[832,128]{1,0:T(8,128)(2,1)S(1)}, bf16[832,128]{1,0:T(8,128)(2,1)S(1)}, u32[]{:S(2)}, u32[]{:S(2)}) collective-permute-start(bf16[832,128]{1,0:T(8,128)(2,1)S(1)} %get-tuple-element.83), channel_id=1, source_target_pairs={{0,1},{1,0},{2,3},{3,2},{4,5},{5,4},{6,7},{7,6},{8,9},{9,8},{10,11... | collective-permute-start | bytes 638984 | tf_op jit(solution)/shard_map/ppermute | solution.py:24
  43.7 4.8 %collective-permute-start.13 = (bf16[208,128]{1,0:T(8,128)(2,1)S(1)}, bf16[208,128]{1,0:T(8,128)(2,1)S(1)}, u32[]{:S(2)}, u32[]{:S(2)}) collective-permute-start(bf16[208,128]{1,0:T(8,128)(2,1)S(1)} %get-tuple-element.85), channel_id=1, source_target_pairs={{0,4},{1,5},{2,6},{3,7},{4,0},{5,1},{6,2},{7,3},{8,12},{9,13},{10,... | collective-permute-start | bytes 159752 | tf_op jit(solution)/shard_map/ppermute | solution.py:24
  44.1 6.8 %collective-permute-start.14 = (bf16[208,128]{1,0:T(8,128)(2,1)S(1)}, bf16[208,128]{1,0:T(8,128)(2,1)S(1)}, u32[]{:S(2)}, u32[]{:S(2)}) collective-permute-start(bf16[208,128]{1,0:T(8,128)(2,1)S(1)} %get-tuple-element.86), channel_id=1, source_target_pairs={{0,8},{1,9},{2,10},{3,11},{4,12},{5,13},{6,14},{7,15},{8,0},{9,1},... | collective-permute-start | bytes 159752 | tf_op jit(solution)/shard_map/ppermute | solution.py:24
  45.9 6.0 %collective-permute-start.15 = (bf16[208,128]{1,0:T(8,128)(2,1)S(1)}, bf16[208,128]{1,0:T(8,128)(2,1)S(1)}, u32[]{:S(2)}, u32[]{:S(2)}) collective-permute-start(bf16[208,128]{1,0:T(8,128)(2,1)S(1)} %get-tuple-element.87), channel_id=1, source_target_pairs={{0,12},{1,13},{2,14},{3,15},{4,8},{5,9},{6,10},{7,11},{8,4},{9,5},... | collective-permute-start | bytes 159752 | tf_op jit(solution)/shard_map/ppermute | solution.py:24
  52.0 4.2 %collective-permute-start.16 = (bf16[208,128]{1,0:T(8,128)(2,1)S(1)}, bf16[208,128]{1,0:T(8,128)(2,1)S(1)}, u32[]{:S(2)}, u32[]{:S(2)}) collective-permute-start(bf16[208,128]{1,0:T(8,128)(2,1)S(1)} %shard_map.207.own), channel_id=1, source_target_pairs={{0,2},{1,3},{2,0},{3,1},{4,6},{5,7},{6,4},{7,5},{8,10},{9,11},{10,... | collective-permute-start | bytes 159752 | tf_op jit(solution)/shard_map/ppermute | solution.py:24
  56.2 6.0 %collective-permute-start.19 = (bf16[208,128]{1,0:T(8,128)(2,1)S(1)}, bf16[208,128]{1,0:T(8,128)(2,1)S(1)}, u32[]{:S(2)}, u32[]{:S(2)}) collective-permute-start(bf16[208,128]{1,0:T(8,128)(2,1)S(1)} %shard_map.208.refs_0_), channel_id=1, source_target_pairs={{0,12},{1,13},{2,14},{3,15},{4,8},{5,9},{6,10},{7,11},{8,4},{9,5},... | collective-permute-start | bytes 159752 | tf_op jit(solution)/shard_map/ppermute | solution.py:24
  58.4 5.0 %collective-permute-start.18 = (bf16[208,128]{1,0:T(8,128)(2,1)S(1)}, bf16[208,128]{1,0:T(8,128)(2,1)S(1)}, u32[]{:S(2)}, u32[]{:S(2)}) collective-permute-start(bf16[208,128]{1,0:T(8,128)(2,1)S(1)} %shard_map.208.refs_0_), channel_id=1, source_target_pairs={{0,8},{1,9},{2,10},{3,11},{4,12},{5,13},{6,14},{7,15},{8,0},{9,1},... | collective-permute-start | bytes 159752 | tf_op jit(solution)/shard_map/ppermute | solution.py:24
  58.4 5.0 %collective-permute-start.17 = (bf16[208,128]{1,0:T(8,128)(2,1)S(1)}, bf16[208,128]{1,0:T(8,128)(2,1)S(1)}, u32[]{:S(2)}, u32[]{:S(2)}) collective-permute-start(bf16[208,128]{1,0:T(8,128)(2,1)S(1)} %shard_map.208.refs_0_), channel_id=1, source_target_pairs={{0,4},{1,5},{2,6},{3,7},{4,0},{5,1},{6,2},{7,3},{8,12},{9,13},{10,... | collective-permute-start | bytes 159752 | tf_op jit(solution)/shard_map/ppermute | solution.py:24
  63.5 1.5 %collective-permute-start.20 = (bf16[832,128]{1,0:T(8,128)(2,1)S(1)}, bf16[832,128]{1,0:T(8,128)(2,1)S(1)}, u32[]{:S(2)}, u32[]{:S(2)}) collective-permute-start(bf16[832,128]{1,0:T(8,128)(2,1)S(1)} %shard_map.209.mine), channel_id=1, source_target_pairs={{0,1},{1,0},{2,3},{3,2},{4,5},{5,4},{6,7},{7,6},{8,9},{9,8},{10,11... | collective-permute-start | bytes 638984 | tf_op jit(solution)/shard_map/ppermute | solution.py:24

commit v6 on v5

--- a/solution.py
+++ b/solution.py
@@ -10,6 +10,7 @@
 AXES = ("dom", "sub", "feat")
 SMEM = pl.BlockSpec(memory_space=pltpu.SMEM)
 VMEM = pl.BlockSpec(memory_space=pltpu.VMEM)
+HBM = pl.BlockSpec(memory_space=pltpu.HBM)
 VMEM_LIMIT = 8 * 2**20
 F32 = jnp.float32
 BF16 = jnp.bfloat16
@@ -32,13 +33,14 @@
     return lax.dot_general(a, b, (((1,), (1,)), ((), ())), preferred_element_type=F32)
 
 
-def run(body, in_specs, out_specs, out_shape, scratch, args, flops=0, moved=0):
+def run(body, in_specs, out_specs, out_shape, scratch, args, flops=0, moved=0, aliases=()):
     return pl.pallas_call(
         body,
         in_specs=in_specs,
         out_specs=out_specs,
         out_shape=out_shape,
         scratch_shapes=scratch,
+        input_output_aliases=dict(aliases),
         compiler_params=pltpu.CompilerParams(vmem_limit_bytes=VMEM_LIMIT),
         cost_estimate=pl.CostEstimate(flops=flops, bytes_accessed=moved, transcendentals=0),
     )(*args)
@@ -217,26 +219,28 @@
         grad = (full * slope[t]).astype(BF16)
         first_grad[here, :] = grad
         bias = bias + jnp.sum(grad.astype(F32), axis=0, keepdims=True)
-    deep = features_t.shape[0]
-    row = 0
+    blocks = []
     for left in (features_t, first_agg_t):
         product = dot(left[...], first_grad[...])
-        for c in range(width // 128):
-            packed[row : row + deep, :] = product[:, c * 128 : (c + 1) * 128]
-            row += deep
-    packed[row : row + width, :] = grad_w2_self[...]
-    row += width
-    packed[row : row + width, :] = dot(hidden_t[...], back_16[...])
-    row += width
-    packed[row:, :] = jnp.zeros_like(packed[row:, :])
+        blocks += [product[:, c * 128 : (c + 1) * 128] for c in range(width // 128)]
+    blocks += [grad_w2_self[...], dot(hidden_t[...], back_16[...])]
+    row = 0
+    for block in blocks:
+        deep = block.shape[0] // 2
+        for h in range(2):
+            packed[h, row : row + deep, :] = block[h * deep : (h + 1) * deep, :]
+        row += deep
+    packed[:, row:, :] = jnp.zeros_like(packed[:, row:, :])
     for c in range(width // 128):
-        packed[row + c : row + c + 1, :] = bias[:, c * 128 : (c + 1) * 128]
+        packed[0, row + c : row + c + 1, :] = bias[:, c * 128 : (c + 1) * 128]
     row += width // 128
-    packed[row : row + 1, :] = grad_bias_two[...]
-    half = keep.shape[0]
+    packed[0, row : row + 1, :] = grad_bias_two[...]
     mine = lax.axis_index("feat")
-    keep[...] = packed[pl.ds(pl.multiple_of(mine * half, 16), half), :]
-    send[...] = packed[pl.ds(pl.multiple_of((1 - mine) * half, 16), half), :].astype(BF16)
+    lines, piece = keep.shape[:2]
+    for line in range(lines):
+        here = slice(line * piece, (line + 1) * piece)
+        keep[line] = packed[mine, here, :]
+        send[line] = packed[1 - mine, here, :].astype(BF16)
 
 
 def leave_body(value, out):
@@ -244,11 +248,9 @@
 
 
 def spread_body(keep, arrived, own, *sends):
-    rows = own.shape[0]
     for distance, out in enumerate((own, *sends)):
         owner = jnp.bitwise_xor(lax.axis_index("dom"), distance)
-        here = pl.ds(pl.multiple_of(owner * rows, 16), rows)
-        out[...] = (keep[here, :] + arrived[here, :].astype(F32)).astype(out.dtype)
+        out[...] = (keep[owner] + arrived[owner].astype(F32)).astype(out.dtype)
 
 
 def gather_body(own, *refs):
@@ -259,31 +261,48 @@
 
 
 def join_body(*refs):
-    out = refs[-1]
-    rows = refs[0].shape[0]
     for distance, piece in enumerate(refs[:-1]):
-        owner = jnp.bitwise_xor(lax.axis_index("dom"), distance)
-        out[pl.ds(pl.multiple_of(owner * rows, 16), rows), :] = piece[...]
-
-
-def unpack_body(mine, other, g1_self, g1_near, g1_bias, g2_self, g2_near, g2_bias, packed):
-    half = mine.shape[0]
-    feat = lax.axis_index("feat")
-    packed[pl.ds(pl.multiple_of(feat * half, 16), half), :] = mine[...].astype(F32)
-    packed[pl.ds(pl.multiple_of((1 - feat) * half, 16), half), :] = other[...].astype(F32)
-    deep, width = g1_self.shape
-    row = 0
-    for out in (g1_self, g1_near):
+        refs[-1][jnp.bitwise_xor(lax.axis_index("dom"), distance)] = piece[...]
+
+
+def place_half(h, value, outs, stages, sems):
+    copies, row = [], 0
+    for out, stage in zip(outs, stages):
+        deep, width = stage.shape
         for c in range(width // 128):
-            out[:, c * 128 : (c + 1) * 128] = packed[row : row + deep, :]
+            stage[:, c * 128 : (c + 1) * 128] = value[row : row + deep, :]
             row += deep
-    for out in (g2_self, g2_near):
-        out[...] = packed[row : row + width, :]
-        row += width
-    for c in range(width // 128):
-        g1_bias[:, c * 128 : (c + 1) * 128] = packed[row : row + 1, :]
-        row += 1
-    g2_bias[...] = packed[row : row + 1, :]
+        there = out.at[pl.ds(pl.multiple_of(h * deep, 8), deep), :]
+        copies.append(pltpu.make_async_copy(stage, there, sems.at[len(copies)]))
+        copies[-1].start()
+    return copies
+
+
+def unpack_mine_body(turned, mine, *refs):
+    count = (len(refs) - 1) // 2
+    value = mine[...].astype(F32).reshape(-1, 128)
+    half = jnp.bitwise_xor(lax.axis_index("feat"), turned)
+    for copy in place_half(half, value, refs[:count], refs[count:-1], refs[-1]):
+        copy.wait()
+
+
+def unpack_other_body(turned, mine, other, *refs):
+    count = (len(refs) - 5) // 3
+    outs, biases = refs[count : 2 * count], refs[2 * count : 2 * count + 2]
+    stages, bias_stages = refs[2 * count + 2 : 3 * count + 2], refs[3 * count + 2 : 3 * count + 4]
+    half = jnp.bitwise_xor(lax.axis_index("feat"), turned)
+    value = other[...].astype(F32).reshape(-1, 128)
+    copies = place_half(1 - half, value, outs, stages, refs[-1])
+    rest = jnp.where(half == 0, mine[...].astype(F32).reshape(-1, 128), value)
+    row = sum(stage.shape[0] * (stage.shape[1] // 128) for stage in stages)
+    for out, stage in zip(biases, bias_stages):
+        for c in range(stage.shape[1] // 128):
+            stage[:, c * 128 : (c + 1) * 128] = rest[row : row + 1, :]
+            row += 1
+        copies.append(pltpu.make_async_copy(stage, out, refs[-1].at[len(copies)]))
+        copies[-1].start()
+    for copy in copies:
+        copy.wait()
 
 
 def shards(
@@ -322,7 +341,7 @@
     partner_src = [swapped(reads, mask) for mask in masks]
     blocks = run(
         stage_body,
-        [pl.BlockSpec(memory_space=pltpu.HBM)],
+        [HBM],
         VMEM,
         struct(blocks.shape, BF16),
         [pltpu.SemaphoreType.DMA],
@@ -426,23 +445,25 @@
     )
 
     lines, columns = lax.axis_size("dom"), lax.axis_size("sub")
-    rows = (2 * width_in * hidden_width + 2 * hidden_width * classes + hidden_width + classes) // 128
-    piece = -(-rows // (2 * lines * 16)) * 16
-    half = piece * lines
+    lines, columns = lax.axis_size("dom"), lax.axis_size("sub")
+    matrices = [(width_in, hidden_width)] * 2 + [(hidden_width, classes)] * 2
+    rows = sum(deep * width // 256 for deep, width in matrices) + (hidden_width + classes) // 128
+    piece = -(-rows // (lines * 8)) * 8
+    half = (lines, piece, 128)
     hidden_grad, send, keep = run(
         functools.partial(back_body, at, rounds),
         [SMEM] + [VMEM] * (rounds + 9),
         [VMEM] * 3,
         [
             struct((tiles, size, hidden_width), BF16),
-            struct((half, 128), BF16),
-            struct((half, 128), F32),
+            struct(half, BF16),
+            struct(half, F32),
         ],
         [
             pltpu.VMEM((tiles, size, classes), F32),
             pltpu.VMEM((nodes, classes), BF16),
             pltpu.VMEM((nodes, hidden_width), BF16),
-            pltpu.VMEM((2 * half, 128), F32),
+            pltpu.VMEM((2, lines * piece, 128), F32),
         ],
         [
             table, *arrived, back, self_grad, slope, w2_near, features_t, first_agg_t,
@@ -457,44 +478,48 @@
         leave_body, [VMEM], VMEM, struct(hidden_grad.shape, BF16), [],
         [hidden_grad], moved=4 * nodes * hidden_width,
     )
+    arrived, hidden_grad = lax.optimization_barrier((arrived, hidden_grad))
 
     along = [distance * 2 * columns for distance in range(1, lines)]
     piece_struct = struct((piece, 128), BF16)
     own, *sends = run(
         spread_body, [VMEM] * 2, [VMEM] * lines,
         [struct((piece, 128), F32)] + [piece_struct] * (lines - 1), [],
-        [keep, arrived], flops=half * 128, moved=half * 128 * 8,
+        [keep, arrived], flops=lines * piece * 128, moved=lines * piece * 128 * 8,
     )
     arrived = [swapped(value, mask) for value, mask in zip(sends, along)]
     total = run(
         gather_body, [VMEM] * lines, VMEM, piece_struct, [],
-        [own, *arrived], flops=half * 128, moved=half * 128 * 2,
-    )
+        [own, *arrived], flops=lines * piece * 128, moved=lines * piece * 128 * 2,
+    )
+    turned = (columns.bit_length() - 1) % 2
     for bit in range(columns.bit_length() - 1):
         total = run(
             gather_body, [VMEM] * 2, VMEM, piece_struct, [],
-            [total, swapped(total, 2 << bit)], flops=piece * 128, moved=piece * 128 * 6,
+            [swapped(total, 1), swapped(total, (2 << bit) | 1)], flops=piece * 128, moved=piece * 128 * 6,
         )
     mine = run(
-        join_body, [VMEM] * lines, VMEM, struct((half, 128), BF16), [],
-        [total, *(swapped(total, mask) for mask in along)], moved=half * 128 * 4,
+        join_body, [VMEM] * lines, VMEM, struct(half, BF16), [],
+        [total, *(swapped(total, mask) for mask in along)], moved=lines * piece * 128 * 4,
     )
     other = swapped(mine, 1)
-    g1_self, g1_near, g1_bias, g2_self, g2_near, g2_bias = run(
-        unpack_body,
-        [VMEM] * 2,
-        [VMEM] * 6,
-        [
-            struct((width_in, hidden_width), F32),
-            struct((width_in, hidden_width), F32),
-            struct((1, hidden_width), F32),
-            struct((hidden_width, classes), F32),
-            struct((hidden_width, classes), F32),
-            struct((1, classes), F32),
-        ],
-        [pltpu.VMEM((2 * half, 128), F32)],
-        [mine, other],
-        moved=half * 128 * 12,
+    stages = [pltpu.VMEM((deep // 2, width), F32) for deep, width in matrices]
+    sems = pltpu.SemaphoreType.DMA((len(matrices) + 2,))
+    biases = [(1, hidden_width), (1, classes)]
+    outs = [struct(shape, F32) for shape in matrices]
+    halves = run(
+        functools.partial(unpack_mine_body, turned), [VMEM], [HBM] * len(outs), outs, [*stages, sems],
+        [mine], moved=lines * piece * 128 * 6,
+    )
+    g1_self, g1_near, g2_self, g2_near, g1_bias, g2_bias = run(
+        functools.partial(unpack_other_body, turned),
+        [VMEM] * 2 + [HBM] * len(outs),
+        [HBM] * (len(outs) + 2),
+        outs + [struct(shape, F32) for shape in biases],
+        [*stages, *[pltpu.VMEM(shape, F32) for shape in biases], sems],
+        [mine, other, *halves],
+        moved=lines * piece * 128 * 6,
+        aliases={2 + n: n for n in range(len(outs))},
     )
     return (
         logits.reshape(nodes, classes),

time: 66.2 us -> 65.7 us (level)
  waiting for transfers between devices: 27.8 us -> 26.6 us
    ppermute x21 -> x22, waiting for transfers between devices: 27.8 us -> 26.6 us  [swapped(): return lax.ppermute(value, AXES, pairs)]
    pallas_call x14 -> x15, Pallas kernels: 8.65 us -> 9.27 us  [run(): pl.pallas_call(body, in_specs=in_specs, out_specs=out_specs, out_shape=ou...]
    ppermute x21 -> x22, starting transfers between devices: 26.2 us -> 26.3 us  [swapped(): return lax.ppermute(value, AXES, pairs)]
  transfers between devices with their start and end apart: 21 -> 22, of which waited for: 15 -> 15; matrix products, arithmetic and copies ran while one was open for 0% -> 0% of each run, Pallas kernels for 7% -> 9%
where the time goes in v6:
time: 65.7 us; the launch traced here: 65.5 us
  waiting for transfers between devices  26.6 us (40%)
  starting transfers between devices  26.3 us (40%)
  Pallas kernels  9.27 us (14%)
  local copies, waits for them, and re-layouts  2.42 us (4%)
  between operations  0.84 us (1%)
    ppermute x22, waiting for transfers between devices, swapped(): return lax.ppermute(value, AXES, pairs)  26.6 us
    ppermute x22, starting transfers between devices, swapped(): return lax.ppermute(value, AXES, pairs)  26.3 us
    pallas_call x15, Pallas kernels, run(): pl.pallas_call(body, in_specs=in_specs, out_specs=out_specs, out_shape=ou...  9.27 us
    unnamed x26, local copies, waits for them, and re-layouts  2.42 us
  transfers between devices with their start and end apart: 22, of which 15 were waited for; matrix products, arithmetic and copies ran while one was open for 0% of the time, Pallas kernels for 9%

profile of v6, /device:TPU:0, one launch (start us, length us, event | category | flops | bytes accessed | tf_op | source)
XLA Modules:
  0.0 65.5 jit_solution(15978063411744269830)
XLA Ops:
  0.6 3.0 %collective-permute-start.2 = (s32[3,1,4]{2,1,0:T(1,128)}, s32[3,1,4]{2,1,0:T(1,128)S(1)}, u32[]{:S(2)}, u32[]{:S(2)}) collective-permute-start(s32[3,1,4]{2,1,0:T(1,128)} %bitcast.23), channel_id=1, source_target_pairs={{0,2},{1,3},{2,0},{3,1},{4,6},{5,7},{6,4},{7,5},{8,10},{9,11},{10,... | collective-permute-start | bytes 152 | tf_op jit(solution)/shard_map/ppermute | solution.py:25
  3.6 1.6 %collective-permute-start.1 = (s32[3,1,4]{2,1,0:T(1,128)}, s32[3,1,4]{2,1,0:T(1,128)S(1)}, u32[]{:S(2)}, u32[]{:S(2)}) collective-permute-start(s32[3,1,4]{2,1,0:T(1,128)} %bitcast.24), channel_id=1, source_target_pairs={{0,4},{1,5},{2,6},{3,7},{4,0},{5,1},{6,2},{7,3},{8,12},{9,13},{10,... | collective-permute-start | bytes 152 | tf_op jit(solution)/shard_map/ppermute | solution.py:25
  5.2 2.6 %collective-permute-start = (s32[3,1,4]{2,1,0:T(1,128)}, s32[3,1,4]{2,1,0:T(1,128)S(1)}, u32[]{:S(2)}, u32[]{:S(2)}) collective-permute-start(s32[3,1,4]{2,1,0:T(1,128)} %bitcast.25), channel_id=1, source_target_pairs={{0,8},{1,9},{2,10},{3,11},{4,12},{5,13},{6,14},{7,15},{8,0},{9,1},... | collective-permute-start | bytes 152 | tf_op jit(solution)/shard_map/ppermute | solution.py:25
  7.8 1.0 %copy-done.3 = bf16[1024,256]{1,0:T(8,128)(2,1)S(1)} copy-done((bf16[1024,256]{1,0:T(8,128)(2,1)S(1)}, bf16[1024,256]{1,0:T(8,128)(2,1)}, u32[]{:S(2)}) %copy-start.3) | copy-done | bytes 524312
  9.0 1.0 %collective-permute-done.refs_0_ = s32[3,1,4]{2,1,0:T(1,128)S(1)} collective-permute-done((s32[3,1,4]{2,1,0:T(1,128)}, s32[3,1,4]{2,1,0:T(1,128)S(1)}, u32[]{:S(2)}, u32[]{:S(2)}) %collective-permute-start) | collective-permute-done | bytes 80 | tf_op jit(solution)/shard_map/ppermute | solution.py:25
  9.9 0.1 shard_map.199
  10.1 2.7 %collective-permute-start.3 = (bf16[4,128,256]{2,1,0:T(8,128)(2,1)S(1)}, bf16[4,128,256]{2,1,0:T(8,128)(2,1)S(1)}, u32[]{:S(2)}, u32[]{:S(2)}) collective-permute-start(bf16[4,128,256]{2,1,0:T(8,128)(2,1)S(1)} %get-tuple-element.59), channel_id=1, source_target_pairs={{0,8},{1,9},{2,10},{3,11},{4,12},{5,13},{6,14},{7,15},{8,0},{9,1},... | collective-permute-start | bytes 786440 | tf_op jit(solution)/shard_map/ppermute | solution.py:25
  12.7 0.4 collective-permute-start.4
  13.2 0.5 collective-permute-start.5
  13.8 0.6 copy-done.8
  14.4 1.5 %shard_map.198 = (s32[68]{0:T(128)S(4)}, f32[8,128,256]{2,1,0:T(8,128)S(1)}, f32[8,128,256]{2,1,0:T(8,128)S(1)}, bf16[256,1024]{1,0:T(8,128)(2,1)S(1)}, bf16[8,4...) custom-call(s32[4,8]{1,0:T(4,128)S(1)} %bitcast.17, s32[3,1,4]{2,1,0:T(1,128)S(1)} %bitcast.18, ...), custom_call_target="tpu_custom_call" | custom-call | flops 402653184 | bytes 8388608 | tf_op jit(solution)/shard_map/pallas_call | solution.py:37
  15.9 7.1 %collective-permute-done.3.refs_0_ = bf16[4,128,256]{2,1,0:T(8,128)(2,1)S(1)} collective-permute-done((bf16[4,128,256]{2,1,0:T(8,128)(2,1)S(1)}, bf16[4,128,256]{2,1,0:T(8,128)(2,1)S(1)}, u32[]{:S(2)}, u32[]{:S(2)}) %collective-permute-start.3) | collective-permute-done | bytes 262176 | tf_op jit(solution)/shard_map/ppermute | solution.py:25
  23.0 1.3 %collective-permute-done.4.refs_1_ = bf16[4,128,256]{2,1,0:T(8,128)(2,1)S(1)} collective-permute-done((bf16[4,128,256]{2,1,0:T(8,128)(2,1)S(1)}, bf16[4,128,256]{2,1,0:T(8,128)(2,1)S(1)}, u32[]{:S(2)}, u32[]{:S(2)}) %collective-permute-start.4) | collective-permute-done | bytes 262176 | tf_op jit(solution)/shard_map/ppermute | solution.py:25
  24.3 1.0 %shard_map.200 = (bf16[8,128,256]{2,1,0:T(8,128)(2,1)S(1)}, bf16[8,128,256]{2,1,0:T(8,128)(2,1)S(1)}, bf16[8,128,128]{2,1,0:T(8,128)(2,1)S(1)}, bf16[4,128,128]{...) custom-call(s32[68]{0:T(128)S(4)} %get-tuple-element.57.table, ...), custom_call_target="tpu_custom_call" | custom-call | flops 301989888 | bytes 8388608 | tf_op jit(solution)/shard_map/pallas_call | solution.py:37
  25.3 0.1 collective-permute-start.6
  25.4 1.8 %collective-permute-start.7 = (bf16[4,128,128]{2,1,0:T(8,128)(2,1)S(1)}, bf16[4,128,128]{2,1,0:T(8,128)(2,1)S(1)}, u32[]{:S(2)}, u32[]{:S(2)}) collective-permute-start(bf16[4,128,128]{2,1,0:T(8,128)(2,1)S(1)} %get-tuple-element.65), channel_id=1, source_target_pairs={{0,4},{1,5},{2,6},{3,7},{4,0},{5,1},{6,2},{7,3},{8,12},{9,13},{10,... | collective-permute-start | bytes 393224 | tf_op jit(solution)/shard_map/ppermute | solution.py:25
  27.1 0.5 collective-permute-start.8
  27.7 0.7 %copy-done.7 = s32[1024]{0:T(1024)S(1)} copy-done((s32[1024]{0:T(1024)S(1)}, s32[1024]{0:T(1024)}, u32[]{:S(2)}) %copy-start.7) | copy-done | bytes 4120
  28.4 0.9 %shard_map.201 = (f32[8,128,256]{2,1,0:T(8,128)S(1)}, f32[8,128,128]{2,1,0:T(8,128)S(1)}, f32[8,128,128]{2,1,0:T(8,128)S(1)}, bf16[256,1024]{1,0:T(8,128)(2,1)S(1)}, bf16[256,1024]{1,0:T(8,128)(2,1)S(1)}) custom-call(s32[68]{0:T(128)S(4)} %get-tuple-element.57.table, s32[8,128]{1,0:T(8,128)S(1)} %bitcast.16, bf16[8,4,128,128]{3,2,1,0:T(8,128)(2,1)S(1)} %copy-done, ...), custom_call_target="tpu_custom_call" | custom-call | flops 335544320 | bytes 6291456 | tf_op jit(solution)/shard_map/pallas_call | solution.py:37
  29.3 3.2 %collective-permute-done.6.refs_0_ = bf16[4,128,128]{2,1,0:T(8,128)(2,1)S(1)} collective-permute-done((bf16[4,128,128]{2,1,0:T(8,128)(2,1)S(1)}, bf16[4,128,128]{2,1,0:T(8,128)(2,1)S(1)}, u32[]{:S(2)}, u32[]{:S(2)}) %collective-permute-start.6) | collective-permute-done | bytes 131104 | tf_op jit(solution)/shard_map/ppermute | solution.py:25
  32.6 0.6 shard_map.202
  33.2 1.2 %collective-permute-start.9 = (bf16[4,128,128]{2,1,0:T(8,128)(2,1)S(1)}, bf16[4,128,128]{2,1,0:T(8,128)(2,1)S(1)}, u32[]{:S(2)}, u32[]{:S(2)}) collective-permute-start(bf16[4,128,128]{2,1,0:T(8,128)(2,1)S(1)} %get-tuple-element.77), channel_id=1, source_target_pairs={{0,8},{1,9},{2,10},{3,11},{4,12},{5,13},{6,14},{7,15},{8,0},{9,1},... | collective-permute-start | bytes 393224 | tf_op jit(solution)/shard_map/ppermute | solution.py:25
  34.3 1.7 %collective-permute-start.10 = (bf16[4,128,128]{2,1,0:T(8,128)(2,1)S(1)}, bf16[4,128,128]{2,1,0:T(8,128)(2,1)S(1)}, u32[]{:S(2)}, u32[]{:S(2)}) collective-permute-start(bf16[4,128,128]{2,1,0:T(8,128)(2,1)S(1)} %get-tuple-element.78), channel_id=1, source_target_pairs={{0,4},{1,5},{2,6},{3,7},{4,0},{5,1},{6,2},{7,3},{8,12},{9,13},{10,... | collective-permute-start | bytes 393224 | tf_op jit(solution)/shard_map/ppermute | solution.py:25
  36.1 0.5 collective-permute-start.11
  36.6 1.5 %shard_map.203 = (bf16[8,128,128]{2,1,0:T(8,128)(2,1)}, f32[8,128,128]{2,1,0:T(8,128)S(1)}, f32[8,128,256]{2,1,0:T(8,128)S(1)}, f32[256,128]{1,0:T(8,128)S(1)}, f32[1,128]{1,0:T(1,128)S(1)}) custom-call(s32[68]{0:T(128)S(4)} %get-tuple-element.57.table, bf16[8,4,128,128]{3,2,1,0:T(8,128)(2,1)S(1)} %get-tuple-element.58.values_t, ...), custom_call_target="tpu_custom_call" | custom-call | flops 268435456 | bytes 4194304 | tf_op jit(solution)/shard_map/pallas_call | solution.py:37
  38.1 2.3 %collective-permute-done.9.refs_0_ = bf16[4,128,128]{2,1,0:T(8,128)(2,1)S(1)} collective-permute-done((bf16[4,128,128]{2,1,0:T(8,128)(2,1)S(1)}, bf16[4,128,128]{2,1,0:T(8,128)(2,1)S(1)}, u32[]{:S(2)}, u32[]{:S(2)}) %collective-permute-start.9) | collective-permute-done | bytes 131104 | tf_op jit(solution)/shard_map/ppermute | solution.py:25
  40.4 0.2 collective-permute-done.10.refs_1_
  40.6 0.4 collective-permute-done.11.refs_2_
  41.0 1.0 %shard_map.204 = (bf16[8,128,256]{2,1,0:T(8,128)(2,1)S(1)}, bf16[4,200,128]{2,1,0:T(8,128)(2,1)S(1)}, f32[4,200,128]{2,1,0:T(8,128)S(1)}) custom-call(s32[68]{0:T(128)S(4)} %get-tuple-element.57.table, bf16[4,128,128]{2,1,0:T(8,128)(2,1)S(1)} %collective-permute-done.9.refs_0_, bf16[4,128,128]{2,1,0:T(8,128)(2,1)S(1)} %collective-permute-done.10.refs_1_, ...), custom_call_target="tpu_custom_call" | custom-call | flops 402653184 | bytes 6291456 | tf_op jit(solution)/shard_map/pallas_call | solution.py:37
  42.2 0.8 %shard_map.205 = bf16[8,128,256]{2,1,0:T(8,128)(2,1)} custom-call(bf16[8,128,256]{2,1,0:T(8,128)(2,1)S(1)} %get-tuple-element.88.value), custom_call_target="tpu_custom_call" | custom-call | bytes 1048576 | tf_op jit(solution)/shard_map/pallas_call | solution.py:37
  43.0 0.6 collective-permute-done.12.arrived
  43.7 0.4 collective-permute-start.13
  44.1 1.8 %collective-permute-start.14 = (bf16[200,128]{1,0:T(8,128)(2,1)S(1)}, bf16[200,128]{1,0:T(8,128)(2,1)S(1)}, u32[]{:S(2)}, u32[]{:S(2)}) collective-permute-start(bf16[200,128]{1,0:T(8,128)(2,1)S(1)} %get-tuple-element.94), channel_id=1, source_target_pairs={{0,8},{1,9},{2,10},{3,11},{4,12},{5,13},{6,14},{7,15},{8,0},{9,1},... | collective-permute-start | bytes 153608 | tf_op jit(solution)/shard_map/ppermute | solution.py:25
  45.9 2.2 %collective-permute-start.15 = (bf16[200,128]{1,0:T(8,128)(2,1)S(1)}, bf16[200,128]{1,0:T(8,128)(2,1)S(1)}, u32[]{:S(2)}, u32[]{:S(2)}) collective-permute-start(bf16[200,128]{1,0:T(8,128)(2,1)S(1)} %get-tuple-element.95), channel_id=1, source_target_pairs={{0,12},{1,13},{2,14},{3,15},{4,8},{5,9},{6,10},{7,11},{8,4},{9,5},... | collective-permute-start | bytes 153608 | tf_op jit(solution)/shard_map/ppermute | solution.py:25
  48.1 0.3 collective-permute-done.13.refs_0_
  48.4 1.2 %collective-permute-done.14.refs_1_ = bf16[200,128]{1,0:T(8,128)(2,1)S(1)} collective-permute-done((bf16[200,128]{1,0:T(8,128)(2,1)S(1)}, bf16[200,128]{1,0:T(8,128)(2,1)S(1)}, u32[]{:S(2)}, u32[]{:S(2)}) %collective-permute-start.14) | collective-permute-done | bytes 51232 | tf_op jit(solution)/shard_map/ppermute | solution.py:25
  49.6 2.2 %collective-permute-done.15.refs_2_ = bf16[200,128]{1,0:T(8,128)(2,1)S(1)} collective-permute-done((bf16[200,128]{1,0:T(8,128)(2,1)S(1)}, bf16[200,128]{1,0:T(8,128)(2,1)S(1)}, u32[]{:S(2)}, u32[]{:S(2)}) %collective-permute-start.15) | collective-permute-done | bytes 51232 | tf_op jit(solution)/shard_map/ppermute | solution.py:25
  51.9 0.1 collective-permute-start.17
  51.9 0.6 collective-permute-start.16
  52.5 2.9 %collective-permute-done.17.refs_0_ = bf16[200,128]{1,0:T(8,128)(2,1)S(1)} collective-permute-done((bf16[200,128]{1,0:T(8,128)(2,1)S(1)}, bf16[200,128]{1,0:T(8,128)(2,1)S(1)}, u32[]{:S(2)}, u32[]{:S(2)}) %collective-permute-start.17) | collective-permute-done | bytes 51232 | tf_op jit(solution)/shard_map/ppermute | solution.py:25
  55.5 2.3 %collective-permute-start.20 = (bf16[200,128]{1,0:T(8,128)(2,1)S(1)}, bf16[200,128]{1,0:T(8,128)(2,1)S(1)}, u32[]{:S(2)}, u32[]{:S(2)}) collective-permute-start(bf16[200,128]{1,0:T(8,128)(2,1)S(1)} %shard_map.208.refs_0_), channel_id=1, source_target_pairs={{0,12},{1,13},{2,14},{3,15},{4,8},{5,9},{6,10},{7,11},{8,4},{9,5},... | collective-permute-start | bytes 153608 | tf_op jit(solution)/shard_map/ppermute | solution.py:25
  57.7 2.2 %collective-permute-start.18 = (bf16[200,128]{1,0:T(8,128)(2,1)S(1)}, bf16[200,128]{1,0:T(8,128)(2,1)S(1)}, u32[]{:S(2)}, u32[]{:S(2)}) collective-permute-start(bf16[200,128]{1,0:T(8,128)(2,1)S(1)} %shard_map.208.refs_0_), channel_id=1, source_target_pairs={{0,4},{1,5},{2,6},{3,7},{4,0},{5,1},{6,2},{7,3},{8,12},{9,13},{10,... | collective-permute-start | bytes 153608 | tf_op jit(solution)/shard_map/ppermute | solution.py:25
  59.9 1.9 %collective-permute-done.20.refs_3_ = bf16[200,128]{1,0:T(8,128)(2,1)S(1)} collective-permute-done((bf16[200,128]{1,0:T(8,128)(2,1)S(1)}, bf16[200,128]{1,0:T(8,128)(2,1)S(1)}, u32[]{:S(2)}, u32[]{:S(2)}) %collective-permute-start.20) | collective-permute-done | bytes 51232 | tf_op jit(solution)/shard_map/ppermute | solution.py:25
  61.9 1.2 %collective-permute-done.19.refs_2_ = bf16[200,128]{1,0:T(8,128)(2,1)S(1)} collective-permute-done((bf16[200,128]{1,0:T(8,128)(2,1)S(1)}, bf16[200,128]{1,0:T(8,128)(2,1)S(1)}, u32[]{:S(2)}, u32[]{:S(2)}) %collective-permute-start.19) | collective-permute-done | bytes 51232 | tf_op jit(solution)/shard_map/ppermute | solution.py:25
  63.1 0.1 collective-permute-start.21
  63.2 0.8 %shard_map.210 = (f32[256,256]{1,0:T(8,128)}, f32[256,256]{1,0:T(8,128)}, f32[256,128]{1,0:T(8,128)}, f32[256,128]{1,0:T(8,128)}) custom-call(bf16[4,200,128]{2,1,0:T(8,128)(2,1)S(1)} %shard_map.209.mine), custom_call_target="tpu_custom_call" | custom-call | bytes 614400 | tf_op jit(solution)/shard_map/pallas_call | solution.py:37
  64.0 0.6 collective-permute-done.21.other
  64.7 0.8 %shard_map.211 = (f32[256,256]{1,0:T(8,128)}, f32[256,256]{1,0:T(8,128)}, f32[256,128]{1,0:T(8,128)}, f32[256,128]{1,0:T(8,128)}, f32[1,256]{1,0:T(1,128)}, /*index=5*/f32[1,128]{1,0:T(1,128)}) custom-call(bf16[4,200,128]{2,1,0:T(8,128)(2,1)S(1)} %shard_map.209.mine, ...), custom_call_target="tpu_custom_call", output_to_operand_aliasing={{0}: (2, {}), {1}: (3, {}), {2}: (4, {}), {3}: (5, {})} | custom-call | bytes 614400 | tf_op jit(solution)/shard_map/pallas_call | solution.py:37
  (37 shorter events, 0.3 us)
Async XLA Ops:
  0.6 13.1 %copy-start = (bf16[8,4,128,128]{3,2,1,0:T(8,128)(2,1)S(1)}, bf16[8,4,128,128]{3,2,1,0:T(8,128)(2,1)}, u32[]{:S(2)}) copy-start(bf16[8,4,128,128]{3,2,1,0:T(8,128)(2,1)} %values.1) | copy-start | bytes 3145732
  0.6 8.3 %collective-permute-start.2 = (s32[3,1,4]{2,1,0:T(1,128)}, s32[3,1,4]{2,1,0:T(1,128)S(1)}, u32[]{:S(2)}, u32[]{:S(2)}) collective-permute-start(s32[3,1,4]{2,1,0:T(1,128)} %bitcast.23), channel_id=1, source_target_pairs={{0,2},{1,3},{2,0},{3,1},{4,6},{5,7},{6,4},{7,5},{8,10},{9,11},{10,... | collective-permute-start | bytes 152 | tf_op jit(solution)/shard_map/ppermute | solution.py:25
  3.6 5.3 %collective-permute-start.1 = (s32[3,1,4]{2,1,0:T(1,128)}, s32[3,1,4]{2,1,0:T(1,128)S(1)}, u32[]{:S(2)}, u32[]{:S(2)}) collective-permute-start(s32[3,1,4]{2,1,0:T(1,128)} %bitcast.24), channel_id=1, source_target_pairs={{0,4},{1,5},{2,6},{3,7},{4,0},{5,1},{6,2},{7,3},{8,12},{9,13},{10,... | collective-permute-start | bytes 152 | tf_op jit(solution)/shard_map/ppermute | solution.py:25
  5.2 4.7 %collective-permute-start = (s32[3,1,4]{2,1,0:T(1,128)}, s32[3,1,4]{2,1,0:T(1,128)S(1)}, u32[]{:S(2)}, u32[]{:S(2)}) collective-permute-start(s32[3,1,4]{2,1,0:T(1,128)} %bitcast.25), channel_id=1, source_target_pairs={{0,8},{1,9},{2,10},{3,11},{4,12},{5,13},{6,14},{7,15},{8,0},{9,1},... | collective-permute-start | bytes 152 | tf_op jit(solution)/shard_map/ppermute | solution.py:25
  7.8 1.0 %copy-start.3 = (bf16[1024,256]{1,0:T(8,128)(2,1)S(1)}, bf16[1024,256]{1,0:T(8,128)(2,1)}, u32[]{:S(2)}) copy-start(bf16[1024,256]{1,0:T(8,128)(2,1)} %param.14) | copy-start | bytes 1572868
  8.9 4.8 %copy-start.1 = (bf16[1,3,4,128,128]{4,3,2,1,0:T(8,128)(2,1)S(1)}, bf16[1,3,4,128,128]{4,3,2,1,0:T(8,128)(2,1)}, u32[]{:S(2)}) copy-start(bf16[1,3,4,128,128]{4,3,2,1,0:T(8,128)(2,1)} %param.21) | copy-start | bytes 1179652
  8.9 4.8 %copy-start.6 = (bf16[256,256]{1,0:T(8,128)(2,1)S(1)}, bf16[256,256]{1,0:T(8,128)(2,1)}, u32[]{:S(2)}) copy-start(bf16[256,256]{1,0:T(8,128)(2,1)} %refs_6_.3) | copy-start | bytes 393220
  9.9 3.8 %copy-start.10 = (f32[256]{0:T(256)S(1)}, f32[256]{0:T(256)}, u32[]{:S(2)}) copy-start(f32[256]{0:T(256)} %param.24) | copy-start | bytes 3076
  9.9 3.8 %copy-start.11 = (s32[1,3]{1,0:T(1,128)S(1)}, s32[1,3]{1,0:T(1,128)}, u32[]{:S(2)}) copy-start(s32[1,3]{1,0:T(1,128)} %count.1) | copy-start | bytes 40
  10.1 12.9 %collective-permute-start.3 = (bf16[4,128,256]{2,1,0:T(8,128)(2,1)S(1)}, bf16[4,128,256]{2,1,0:T(8,128)(2,1)S(1)}, u32[]{:S(2)}, u32[]{:S(2)}) collective-permute-start(bf16[4,128,256]{2,1,0:T(8,128)(2,1)S(1)} %get-tuple-element.59), channel_id=1, source_target_pairs={{0,8},{1,9},{2,10},{3,11},{4,12},{5,13},{6,14},{7,15},{8,0},{9,1},... | collective-permute-start | bytes 786440 | tf_op jit(solution)/shard_map/ppermute | solution.py:25
  12.7 11.6 %collective-permute-start.4 = (bf16[4,128,256]{2,1,0:T(8,128)(2,1)S(1)}, bf16[4,128,256]{2,1,0:T(8,128)(2,1)S(1)}, u32[]{:S(2)}, u32[]{:S(2)}) collective-permute-start(bf16[4,128,256]{2,1,0:T(8,128)(2,1)S(1)} %get-tuple-element.60), channel_id=1, source_target_pairs={{0,4},{1,5},{2,6},{3,7},{4,0},{5,1},{6,2},{7,3},{8,12},{9,13},{10,... | collective-permute-start | bytes 786440 | tf_op jit(solution)/shard_map/ppermute | solution.py:25
  13.2 11.1 %collective-permute-start.5 = (bf16[4,128,256]{2,1,0:T(8,128)(2,1)S(1)}, bf16[4,128,256]{2,1,0:T(8,128)(2,1)S(1)}, u32[]{:S(2)}, u32[]{:S(2)}) collective-permute-start(bf16[4,128,256]{2,1,0:T(8,128)(2,1)S(1)} %get-tuple-element.61), channel_id=1, source_target_pairs={{0,2},{1,3},{2,0},{3,1},{4,6},{5,7},{6,4},{7,5},{8,10},{9,11},{10,... | collective-permute-start | bytes 786440 | tf_op jit(solution)/shard_map/ppermute | solution.py:25
  13.7 0.7 %copy-start.8 = (s32[8,4]{0,1:T(4,128)S(1)}, s32[8,4]{0,1:T(4,128)}, u32[]{:S(2)}) copy-start(s32[8,4]{0,1:T(4,128)} %param.16) | copy-start | bytes 388
  13.7 0.7 %copy-start.9 = (s32[1,3,4]{2,0,1:T(1,128)S(1)}, s32[1,3,4]{2,0,1:T(1,128)}, u32[]{:S(2)}) copy-start(s32[1,3,4]{2,0,1:T(1,128)} %param.19) | copy-start | bytes 148
  14.4 9.9 %copy-start.2 = (bf16[256,256]{1,0:T(8,128)(2,1)S(1)}, bf16[256,256]{1,0:T(8,128)(2,1)}, u32[]{:S(2)}) copy-start(bf16[256,256]{1,0:T(8,128)(2,1)} %w1_near.1) | copy-start | bytes 393220
  14.4 9.9 %copy-start.5 = (bf16[256,128]{1,0:T(8,128)(2,1)S(1)}, bf16[256,128]{1,0:T(8,128)(2,1)}, u32[]{:S(2)}) copy-start(bf16[256,128]{1,0:T(8,128)(2,1)} %refs_6_.5) | copy-start | bytes 196612
  24.3 3.4 %copy-start.4 = (bf16[256,128]{1,0:T(8,128)(2,1)S(1)}, bf16[256,128]{1,0:T(8,128)(2,1)}, u32[]{:S(2)}) copy-start(bf16[256,128]{1,0:T(8,128)(2,1)} %w2_self.3) | copy-start | bytes 196612
  25.3 7.3 %collective-permute-start.6 = (bf16[4,128,128]{2,1,0:T(8,128)(2,1)S(1)}, bf16[4,128,128]{2,1,0:T(8,128)(2,1)S(1)}, u32[]{:S(2)}, u32[]{:S(2)}) collective-permute-start(bf16[4,128,128]{2,1,0:T(8,128)(2,1)S(1)} %get-tuple-element.64), channel_id=1, source_target_pairs={{0,8},{1,9},{2,10},{3,11},{4,12},{5,13},{6,14},{7,15},{8,0},{9,1},... | collective-permute-start | bytes 393224 | tf_op jit(solution)/shard_map/ppermute | solution.py:25
  25.4 7.2 %collective-permute-start.7 = (bf16[4,128,128]{2,1,0:T(8,128)(2,1)S(1)}, bf16[4,128,128]{2,1,0:T(8,128)(2,1)S(1)}, u32[]{:S(2)}, u32[]{:S(2)}) collective-permute-start(bf16[4,128,128]{2,1,0:T(8,128)(2,1)S(1)} %get-tuple-element.65), channel_id=1, source_target_pairs={{0,4},{1,5},{2,6},{3,7},{4,0},{5,1},{6,2},{7,3},{8,12},{9,13},{10,... | collective-permute-start | bytes 393224 | tf_op jit(solution)/shard_map/ppermute | solution.py:25
  27.1 5.4 %collective-permute-start.8 = (bf16[4,128,128]{2,1,0:T(8,128)(2,1)S(1)}, bf16[4,128,128]{2,1,0:T(8,128)(2,1)S(1)}, u32[]{:S(2)}, u32[]{:S(2)}) collective-permute-start(bf16[4,128,128]{2,1,0:T(8,128)(2,1)S(1)} %get-tuple-element.66), channel_id=1, source_target_pairs={{0,2},{1,3},{2,0},{3,1},{4,6},{5,7},{6,4},{7,5},{8,10},{9,11},{10,... | collective-permute-start | bytes 393224 | tf_op jit(solution)/shard_map/ppermute | solution.py:25
  27.7 0.7 %copy-start.7 = (s32[1024]{0:T(1024)S(1)}, s32[1024]{0:T(1024)}, u32[]{:S(2)}) copy-start(s32[1024]{0:T(1024)} %param.15) | copy-start | bytes 12292
  27.7 0.7 %copy-start.12 = (f32[128]{0:T(128)S(1)}, f32[128]{0:T(128)}, u32[]{:S(2)}) copy-start(f32[128]{0:T(128)} %param.27) | copy-start | bytes 1540
  33.2 7.2 %collective-permute-start.9 = (bf16[4,128,128]{2,1,0:T(8,128)(2,1)S(1)}, bf16[4,128,128]{2,1,0:T(8,128)(2,1)S(1)}, u32[]{:S(2)}, u32[]{:S(2)}) collective-permute-start(bf16[4,128,128]{2,1,0:T(8,128)(2,1)S(1)} %get-tuple-element.77), channel_id=1, source_target_pairs={{0,8},{1,9},{2,10},{3,11},{4,12},{5,13},{6,14},{7,15},{8,0},{9,1},... | collective-permute-start | bytes 393224 | tf_op jit(solution)/shard_map/ppermute | solution.py:25
  34.3 6.3 %collective-permute-start.10 = (bf16[4,128,128]{2,1,0:T(8,128)(2,1)S(1)}, bf16[4,128,128]{2,1,0:T(8,128)(2,1)S(1)}, u32[]{:S(2)}, u32[]{:S(2)}) collective-permute-start(bf16[4,128,128]{2,1,0:T(8,128)(2,1)S(1)} %get-tuple-element.78), channel_id=1, source_target_pairs={{0,4},{1,5},{2,6},{3,7},{4,0},{5,1},{6,2},{7,3},{8,12},{9,13},{10,... | collective-permute-start | bytes 393224 | tf_op jit(solution)/shard_map/ppermute | solution.py:25
  36.1 5.0 %collective-permute-start.11 = (bf16[4,128,128]{2,1,0:T(8,128)(2,1)S(1)}, bf16[4,128,128]{2,1,0:T(8,128)(2,1)S(1)}, u32[]{:S(2)}, u32[]{:S(2)}) collective-permute-start(bf16[4,128,128]{2,1,0:T(8,128)(2,1)S(1)} %get-tuple-element.79), channel_id=1, source_target_pairs={{0,2},{1,3},{2,0},{3,1},{4,6},{5,7},{6,4},{7,5},{8,10},{9,11},{10,... | collective-permute-start | bytes 393224 | tf_op jit(solution)/shard_map/ppermute | solution.py:25
  42.1 1.5 %collective-permute-start.12 = (bf16[4,200,128]{2,1,0:T(8,128)(2,1)S(1)}, bf16[4,200,128]{2,1,0:T(8,128)(2,1)S(1)}, u32[]{:S(2)}, u32[]{:S(2)}) collective-permute-start(bf16[4,200,128]{2,1,0:T(8,128)(2,1)S(1)} %get-tuple-element.87), channel_id=1, source_target_pairs={{0,1},{1,0},{2,3},{3,2},{4,5},{5,4},{6,7},{7,6},{8,9},{9,8},{10,11... | collective-permute-start | bytes 614408 | tf_op jit(solution)/shard_map/ppermute | solution.py:25
  43.7 4.7 %collective-permute-start.13 = (bf16[200,128]{1,0:T(8,128)(2,1)S(1)}, bf16[200,128]{1,0:T(8,128)(2,1)S(1)}, u32[]{:S(2)}, u32[]{:S(2)}) collective-permute-start(bf16[200,128]{1,0:T(8,128)(2,1)S(1)} %get-tuple-element.93), channel_id=1, source_target_pairs={{0,4},{1,5},{2,6},{3,7},{4,0},{5,1},{6,2},{7,3},{8,12},{9,13},{10,... | collective-permute-start | bytes 153608 | tf_op jit(solution)/shard_map/ppermute | solution.py:25
  44.1 5.6 %collective-permute-start.14 = (bf16[200,128]{1,0:T(8,128)(2,1)S(1)}, bf16[200,128]{1,0:T(8,128)(2,1)S(1)}, u32[]{:S(2)}, u32[]{:S(2)}) collective-permute-start(bf16[200,128]{1,0:T(8,128)(2,1)S(1)} %get-tuple-element.94), channel_id=1, source_target_pairs={{0,8},{1,9},{2,10},{3,11},{4,12},{5,13},{6,14},{7,15},{8,0},{9,1},... | collective-permute-start | bytes 153608 | tf_op jit(solution)/shard_map/ppermute | solution.py:25
  45.9 5.9 %collective-permute-start.15 = (bf16[200,128]{1,0:T(8,128)(2,1)S(1)}, bf16[200,128]{1,0:T(8,128)(2,1)S(1)}, u32[]{:S(2)}, u32[]{:S(2)}) collective-permute-start(bf16[200,128]{1,0:T(8,128)(2,1)S(1)} %get-tuple-element.95), channel_id=1, source_target_pairs={{0,12},{1,13},{2,14},{3,15},{4,8},{5,9},{6,10},{7,11},{8,4},{9,5},... | collective-permute-start | bytes 153608 | tf_op jit(solution)/shard_map/ppermute | solution.py:25
  51.9 3.6 %collective-permute-start.17 = (bf16[200,128]{1,0:T(8,128)(2,1)S(1)}, bf16[200,128]{1,0:T(8,128)(2,1)S(1)}, u32[]{:S(2)}, u32[]{:S(2)}) collective-permute-start(bf16[200,128]{1,0:T(8,128)(2,1)S(1)} %shard_map.207), channel_id=1, source_target_pairs={{0,3},{1,2},{2,1},{3,0},{4,7},{5,6},{6,5},{7,4},{8,11},{9,10},{10,... | collective-permute-start | bytes 153608 | tf_op jit(solution)/shard_map/ppermute | solution.py:25
  51.9 3.5 %collective-permute-start.16 = (bf16[200,128]{1,0:T(8,128)(2,1)S(1)}, bf16[200,128]{1,0:T(8,128)(2,1)S(1)}, u32[]{:S(2)}, u32[]{:S(2)}) collective-permute-start(bf16[200,128]{1,0:T(8,128)(2,1)S(1)} %shard_map.207), channel_id=1, source_target_pairs={{0,1},{1,0},{2,3},{3,2},{4,5},{5,4},{6,7},{7,6},{8,9},{9,8},{10,11... | collective-permute-start | bytes 153608 | tf_op jit(solution)/shard_map/ppermute | solution.py:25
  55.5 6.4 %collective-permute-start.20 = (bf16[200,128]{1,0:T(8,128)(2,1)S(1)}, bf16[200,128]{1,0:T(8,128)(2,1)S(1)}, u32[]{:S(2)}, u32[]{:S(2)}) collective-permute-start(bf16[200,128]{1,0:T(8,128)(2,1)S(1)} %shard_map.208.refs_0_), channel_id=1, source_target_pairs={{0,12},{1,13},{2,14},{3,15},{4,8},{5,9},{6,10},{7,11},{8,4},{9,5},... | collective-permute-start | bytes 153608 | tf_op jit(solution)/shard_map/ppermute | solution.py:25
  57.7 5.4 %collective-permute-start.19 = (bf16[200,128]{1,0:T(8,128)(2,1)S(1)}, bf16[200,128]{1,0:T(8,128)(2,1)S(1)}, u32[]{:S(2)}, u32[]{:S(2)}) collective-permute-start(bf16[200,128]{1,0:T(8,128)(2,1)S(1)} %shard_map.208.refs_0_), channel_id=1, source_target_pairs={{0,8},{1,9},{2,10},{3,11},{4,12},{5,13},{6,14},{7,15},{8,0},{9,1},... | collective-permute-start | bytes 153608 | tf_op jit(solution)/shard_map/ppermute | solution.py:25
  57.7 5.4 %collective-permute-start.18 = (bf16[200,128]{1,0:T(8,128)(2,1)S(1)}, bf16[200,128]{1,0:T(8,128)(2,1)S(1)}, u32[]{:S(2)}, u32[]{:S(2)}) collective-permute-start(bf16[200,128]{1,0:T(8,128)(2,1)S(1)} %shard_map.208.refs_0_), channel_id=1, source_target_pairs={{0,4},{1,5},{2,6},{3,7},{4,0},{5,1},{6,2},{7,3},{8,12},{9,13},{10,... | collective-permute-start | bytes 153608 | tf_op jit(solution)/shard_map/ppermute | solution.py:25
  63.1 1.5 %collective-permute-start.21 = (bf16[4,200,128]{2,1,0:T(8,128)(2,1)S(1)}, bf16[4,200,128]{2,1,0:T(8,128)(2,1)S(1)}, u32[]{:S(2)}, u32[]{:S(2)}) collective-permute-start(bf16[4,200,128]{2,1,0:T(8,128)(2,1)S(1)} %shard_map.209.mine), channel_id=1, source_target_pairs={{0,1},{1,0},{2,3},{3,2},{4,5},{5,4},{6,7},{7,6},{8,9},{9,8},{10,11... | collective-permute-start | bytes 614408 | tf_op jit(solution)/shard_map/ppermute | solution.py:25

commit v7 on v6

--- a/solution.py
+++ b/solution.py
@@ -104,9 +104,10 @@
         right = jnp.concatenate([features[index[k, t]] for k in range(fan)], axis=0)
         near[t] = dot(left, right)
         own[t] = dot(features[t], w1_self[...]) + bias[...]
-        features_t[:, t * size : (t + 1) * size] = features[t].T
+        features_t[:-16, t * size : (t + 1) * size] = features[t].T
         for k in range(fan):
             values_t[t, k] = values[t, k].T
+    features_t[-16:, :] = jnp.ones_like(features_t[-16:, :])
     for r in range(rounds):
         for s in range(slots):
             live = s < count[0, r]
@@ -209,7 +210,6 @@
         for s in range(arrived[r].shape[0]):
             where = table[at.give_at(r, s)]
             total[where] = total[where] + arrived[r][s].astype(F32)
-    bias = jnp.zeros((1, width), F32)
     for t in range(tiles):
         here = slice(t * size, (t + 1) * size)
         rows = total[t].astype(BF16)
@@ -218,11 +218,13 @@
         hidden_grad[t] = full.astype(BF16)
         grad = (full * slope[t]).astype(BF16)
         first_grad[here, :] = grad
-        bias = bias + jnp.sum(grad.astype(F32), axis=0, keepdims=True)
     blocks = []
+    width_in = first_agg_t.shape[0]
     for left in (features_t, first_agg_t):
         product = dot(left[...], first_grad[...])
-        blocks += [product[:, c * 128 : (c + 1) * 128] for c in range(width // 128)]
+        if left is features_t:
+            bias = product[width_in : width_in + 1, :]
+        blocks += [product[:width_in, c * 128 : (c + 1) * 128] for c in range(width // 128)]
     blocks += [grad_w2_self[...], dot(hidden_t[...], back_16[...])]
     row = 0
     for block in blocks:
@@ -260,9 +262,10 @@
     refs[-1][...] = total.astype(BF16)
 
 
-def join_body(*refs):
-    for distance, piece in enumerate(refs[:-1]):
-        refs[-1][jnp.bitwise_xor(lax.axis_index("dom"), distance)] = piece[...]
+def in_order(distances, pieces, held):
+    for distance, piece in zip(distances, pieces):
+        held[jnp.bitwise_xor(lax.axis_index("dom"), distance)] = piece[...].astype(F32)
+    return held[...].reshape(-1, 128)
 
 
 def place_half(h, value, outs, stages, sems):
@@ -278,31 +281,35 @@
     return copies
 
 
-def unpack_mine_body(turned, mine, *refs):
-    count = (len(refs) - 1) // 2
-    value = mine[...].astype(F32).reshape(-1, 128)
-    half = jnp.bitwise_xor(lax.axis_index("feat"), turned)
-    for copy in place_half(half, value, refs[:count], refs[count:-1], refs[-1]):
-        copy.wait()
-
-
-def unpack_other_body(turned, mine, other, *refs):
-    count = (len(refs) - 5) // 3
-    outs, biases = refs[count : 2 * count], refs[2 * count : 2 * count + 2]
-    stages, bias_stages = refs[2 * count + 2 : 3 * count + 2], refs[3 * count + 2 : 3 * count + 4]
-    half = jnp.bitwise_xor(lax.axis_index("feat"), turned)
-    value = other[...].astype(F32).reshape(-1, 128)
-    copies = place_half(1 - half, value, outs, stages, refs[-1])
-    rest = jnp.where(half == 0, mine[...].astype(F32).reshape(-1, 128), value)
-    row = sum(stage.shape[0] * (stage.shape[1] // 128) for stage in stages)
-    for out, stage in zip(biases, bias_stages):
+def unpack_body(distances, other, *refs):
+    lines, count = len(distances), 6
+    pieces, outs = refs[:lines], refs[lines : lines + count]
+    stages, held, sems = refs[lines + count : -2], refs[-2], refs[-1]
+    value = in_order(distances, pieces, held)
+    half = jnp.bitwise_xor(lax.axis_index("feat"), other)
+    copies = place_half(half, value, outs[:4], stages[:4], sems)
+    row = sum(stage.shape[0] * (stage.shape[1] // 128) for stage in stages[:4])
+    biases = []
+    for out, stage in zip(outs[4:], stages[4:]):
         for c in range(stage.shape[1] // 128):
-            stage[:, c * 128 : (c + 1) * 128] = rest[row : row + 1, :]
+            stage[:, c * 128 : (c + 1) * 128] = value[row : row + 1, :]
             row += 1
-        copies.append(pltpu.make_async_copy(stage, out, refs[-1].at[len(copies)]))
-        copies[-1].start()
+        biases.append(pltpu.make_async_copy(stage, out, sems.at[len(copies) + len(biases)]))
+
+    @pl.when(half == 0)
+    def _():
+        for copy in biases:
+            copy.start()
+        for copy in biases:
+            copy.wait()
+
     for copy in copies:
         copy.wait()
+
+
+def unpack_rest_body(distances, other, *refs):
+    lines, count = len(distances), 6
+    unpack_body(distances, other, *refs[:lines], *refs[lines + count :])
 
 
 def shards(
@@ -367,7 +374,7 @@
             pltpu.SMEM((at.size,), jnp.int32),
             struct((tiles, size, width_in), F32),
             struct((tiles, size, hidden_width), F32),
-            struct((width_in, nodes), BF16),
+            struct((width_in + 16, nodes), BF16),
             struct(local_values.shape, BF16),
             struct(edges.shape, BF16),
         ],
@@ -498,28 +505,32 @@
             gather_body, [VMEM] * 2, VMEM, piece_struct, [],
             [swapped(total, 1), swapped(total, (2 << bit) | 1)], flops=piece * 128, moved=piece * 128 * 6,
         )
-    mine = run(
-        join_body, [VMEM] * lines, VMEM, struct(half, BF16), [],
-        [total, *(swapped(total, mask) for mask in along)], moved=lines * piece * 128 * 4,
-    )
-    other = swapped(mine, 1)
-    stages = [pltpu.VMEM((deep // 2, width), F32) for deep, width in matrices]
-    sems = pltpu.SemaphoreType.DMA((len(matrices) + 2,))
-    biases = [(1, hidden_width), (1, classes)]
-    outs = [struct(shape, F32) for shape in matrices]
+    distances = [0, *range(2, 0, -1), *range(3, lines)]
+    pieces = [total, *(swapped(total, along[distance - 1]) for distance in distances[1:])]
+    copies = [swapped(value, 1) for value in pieces]
+    shapes = matrices + [(1, hidden_width), (1, classes)]
+    outs = [struct(shape, F32) for shape in shapes]
+    scratch = [pltpu.VMEM((deep // 2, width), F32) for deep, width in matrices]
+    scratch += [pltpu.VMEM(shape, F32) for shape in shapes[len(matrices) :]]
+    scratch += [pltpu.VMEM(half, F32), pltpu.SemaphoreType.DMA((len(shapes),))]
     halves = run(
-        functools.partial(unpack_mine_body, turned), [VMEM], [HBM] * len(outs), outs, [*stages, sems],
-        [mine], moved=lines * piece * 128 * 6,
+        functools.partial(unpack_body, distances, turned),
+        [VMEM] * lines,
+        [HBM] * len(outs),
+        outs,
+        scratch,
+        pieces,
+        moved=lines * piece * 128 * 6,
     )
     g1_self, g1_near, g2_self, g2_near, g1_bias, g2_bias = run(
-        functools.partial(unpack_other_body, turned),
-        [VMEM] * 2 + [HBM] * len(outs),
-        [HBM] * (len(outs) + 2),
-        outs + [struct(shape, F32) for shape in biases],
-        [*stages, *[pltpu.VMEM(shape, F32) for shape in biases], sems],
-        [mine, other, *halves],
+        functools.partial(unpack_rest_body, distances, 1 - turned),
+        [VMEM] * lines + [HBM] * len(outs),
+        [HBM] * len(outs),
+        outs,
+        scratch,
+        [*copies, *halves],
         moved=lines * piece * 128 * 6,
-        aliases={2 + n: n for n in range(len(outs))},
+        aliases={lines + n: n for n in range(len(outs))},
     )
     return (
         logits.reshape(nodes, classes),

time: 65.7 us -> 65 us (0.989)
  waiting for transfers between devices: 26.6 us -> 25.7 us
    ppermute x22 -> x25, waiting for transfers between devices: 26.6 us -> 25.7 us  [swapped(): return lax.ppermute(value, AXES, pairs)]
    ppermute x22 -> x25, starting transfers between devices: 26.3 us -> 26.5 us  [swapped(): return lax.ppermute(value, AXES, pairs)]
    pallas_call x15 -> x14, Pallas kernels: 9.27 us -> 9.26 us  [run(): pl.pallas_call(body, in_specs=in_specs, out_specs=out_specs, out_shape=ou...]
  transfers between devices with their start and end apart: 22 -> 25, of which waited for: 15 -> 16; matrix products, arithmetic and copies ran while one was open for 0% -> 0% of each run, Pallas kernels for 9% -> 9%
where the time goes in v7:
time: 65 us; the launch traced here: 64.8 us
  starting transfers between devices  26.5 us (41%)
  waiting for transfers between devices  25.7 us (40%)
  Pallas kernels  9.26 us (14%)
  local copies, waits for them, and re-layouts  2.42 us (4%)
  between operations  0.86 us (1%)
    ppermute x25, starting transfers between devices, swapped(): return lax.ppermute(value, AXES, pairs)  26.5 us
    ppermute x25, waiting for transfers between devices, swapped(): return lax.ppermute(value, AXES, pairs)  25.7 us
    pallas_call x14, Pallas kernels, run(): pl.pallas_call(body, in_specs=in_specs, out_specs=out_specs, out_shape=ou...  9.26 us
    unnamed x26, local copies, waits for them, and re-layouts  2.42 us
  transfers between devices with their start and end apart: 25, of which 16 were waited for; matrix products, arithmetic and copies ran while one was open for 0% of the time, Pallas kernels for 9%

profile of v7, /device:TPU:0, one launch (start us, length us, event | category | flops | bytes accessed | tf_op | source)
XLA Modules:
  0.0 64.8 jit_solution(8510453256958757981)
XLA Ops:
  0.6 3.0 %collective-permute-start.2 = (s32[3,1,4]{2,1,0:T(1,128)}, s32[3,1,4]{2,1,0:T(1,128)S(1)}, u32[]{:S(2)}, u32[]{:S(2)}) collective-permute-start(s32[3,1,4]{2,1,0:T(1,128)} %bitcast.25), channel_id=1, source_target_pairs={{0,2},{1,3},{2,0},{3,1},{4,6},{5,7},{6,4},{7,5},{8,10},{9,11},{10,... | collective-permute-start | bytes 152 | tf_op jit(solution)/shard_map/ppermute | solution.py:25
  3.6 1.6 %collective-permute-start.1 = (s32[3,1,4]{2,1,0:T(1,128)}, s32[3,1,4]{2,1,0:T(1,128)S(1)}, u32[]{:S(2)}, u32[]{:S(2)}) collective-permute-start(s32[3,1,4]{2,1,0:T(1,128)} %bitcast.26), channel_id=1, source_target_pairs={{0,4},{1,5},{2,6},{3,7},{4,0},{5,1},{6,2},{7,3},{8,12},{9,13},{10,... | collective-permute-start | bytes 152 | tf_op jit(solution)/shard_map/ppermute | solution.py:25
  5.2 2.6 %collective-permute-start = (s32[3,1,4]{2,1,0:T(1,128)}, s32[3,1,4]{2,1,0:T(1,128)S(1)}, u32[]{:S(2)}, u32[]{:S(2)}) collective-permute-start(s32[3,1,4]{2,1,0:T(1,128)} %bitcast.27), channel_id=1, source_target_pairs={{0,8},{1,9},{2,10},{3,11},{4,12},{5,13},{6,14},{7,15},{8,0},{9,1},... | collective-permute-start | bytes 152 | tf_op jit(solution)/shard_map/ppermute | solution.py:25
  7.8 1.0 %copy-done.3 = bf16[1024,256]{1,0:T(8,128)(2,1)S(1)} copy-done((bf16[1024,256]{1,0:T(8,128)(2,1)S(1)}, bf16[1024,256]{1,0:T(8,128)(2,1)}, u32[]{:S(2)}) %copy-start.3) | copy-done | bytes 524312
  9.0 1.0 %collective-permute-done.refs_0_ = s32[3,1,4]{2,1,0:T(1,128)S(1)} collective-permute-done((s32[3,1,4]{2,1,0:T(1,128)}, s32[3,1,4]{2,1,0:T(1,128)S(1)}, u32[]{:S(2)}, u32[]{:S(2)}) %collective-permute-start) | collective-permute-done | bytes 80 | tf_op jit(solution)/shard_map/ppermute | solution.py:25
  9.9 0.1 shard_map.199
  10.1 2.7 %collective-permute-start.3 = (bf16[4,128,256]{2,1,0:T(8,128)(2,1)S(1)}, bf16[4,128,256]{2,1,0:T(8,128)(2,1)S(1)}, u32[]{:S(2)}, u32[]{:S(2)}) collective-permute-start(bf16[4,128,256]{2,1,0:T(8,128)(2,1)S(1)} %get-tuple-element.61), channel_id=1, source_target_pairs={{0,8},{1,9},{2,10},{3,11},{4,12},{5,13},{6,14},{7,15},{8,0},{9,1},... | collective-permute-start | bytes 786440 | tf_op jit(solution)/shard_map/ppermute | solution.py:25
  12.7 0.4 collective-permute-start.4
  13.2 0.5 collective-permute-start.5
  13.8 0.6 copy-done.8
  14.4 1.5 %shard_map.198 = (s32[68]{0:T(128)S(4)}, f32[8,128,256]{2,1,0:T(8,128)S(1)}, f32[8,128,256]{2,1,0:T(8,128)S(1)}, bf16[272,1024]{1,0:T(8,128)(2,1)S(1)}, bf16[8,4...) custom-call(s32[4,8]{1,0:T(4,128)S(1)} %bitcast.17, s32[3,1,4]{2,1,0:T(1,128)S(1)} %bitcast.18, ...), custom_call_target="tpu_custom_call" | custom-call | flops 402653184 | bytes 8388608 | tf_op jit(solution)/shard_map/pallas_call | solution.py:37
  15.9 7.1 %collective-permute-done.3.refs_0_ = bf16[4,128,256]{2,1,0:T(8,128)(2,1)S(1)} collective-permute-done((bf16[4,128,256]{2,1,0:T(8,128)(2,1)S(1)}, bf16[4,128,256]{2,1,0:T(8,128)(2,1)S(1)}, u32[]{:S(2)}, u32[]{:S(2)}) %collective-permute-start.3) | collective-permute-done | bytes 262176 | tf_op jit(solution)/shard_map/ppermute | solution.py:25
  23.0 1.3 %collective-permute-done.4.refs_1_ = bf16[4,128,256]{2,1,0:T(8,128)(2,1)S(1)} collective-permute-done((bf16[4,128,256]{2,1,0:T(8,128)(2,1)S(1)}, bf16[4,128,256]{2,1,0:T(8,128)(2,1)S(1)}, u32[]{:S(2)}, u32[]{:S(2)}) %collective-permute-start.4) | collective-permute-done | bytes 262176 | tf_op jit(solution)/shard_map/ppermute | solution.py:25
  24.3 1.0 %shard_map.200 = (bf16[8,128,256]{2,1,0:T(8,128)(2,1)S(1)}, bf16[8,128,256]{2,1,0:T(8,128)(2,1)S(1)}, bf16[8,128,128]{2,1,0:T(8,128)(2,1)S(1)}, bf16[4,128,128]{...) custom-call(s32[68]{0:T(128)S(4)} %get-tuple-element.59.table, ...), custom_call_target="tpu_custom_call" | custom-call | flops 301989888 | bytes 8388608 | tf_op jit(solution)/shard_map/pallas_call | solution.py:37
  25.3 0.1 collective-permute-start.6
  25.4 1.8 %collective-permute-start.7 = (bf16[4,128,128]{2,1,0:T(8,128)(2,1)S(1)}, bf16[4,128,128]{2,1,0:T(8,128)(2,1)S(1)}, u32[]{:S(2)}, u32[]{:S(2)}) collective-permute-start(bf16[4,128,128]{2,1,0:T(8,128)(2,1)S(1)} %get-tuple-element.67), channel_id=1, source_target_pairs={{0,4},{1,5},{2,6},{3,7},{4,0},{5,1},{6,2},{7,3},{8,12},{9,13},{10,... | collective-permute-start | bytes 393224 | tf_op jit(solution)/shard_map/ppermute | solution.py:25
  27.2 0.5 collective-permute-start.8
  27.7 0.7 %copy-done.7 = s32[1024]{0:T(1024)S(1)} copy-done((s32[1024]{0:T(1024)S(1)}, s32[1024]{0:T(1024)}, u32[]{:S(2)}) %copy-start.7) | copy-done | bytes 4120
  28.4 1.0 %shard_map.201 = (f32[8,128,256]{2,1,0:T(8,128)S(1)}, f32[8,128,128]{2,1,0:T(8,128)S(1)}, f32[8,128,128]{2,1,0:T(8,128)S(1)}, bf16[256,1024]{1,0:T(8,128)(2,1)S(1)}, bf16[256,1024]{1,0:T(8,128)(2,1)S(1)}) custom-call(s32[68]{0:T(128)S(4)} %get-tuple-element.59.table, s32[8,128]{1,0:T(8,128)S(1)} %bitcast.16, bf16[8,4,128,128]{3,2,1,0:T(8,128)(2,1)S(1)} %copy-done, ...), custom_call_target="tpu_custom_call" | custom-call | flops 335544320 | bytes 6291456 | tf_op jit(solution)/shard_map/pallas_call | solution.py:37
  29.3 3.2 %collective-permute-done.6.refs_0_ = bf16[4,128,128]{2,1,0:T(8,128)(2,1)S(1)} collective-permute-done((bf16[4,128,128]{2,1,0:T(8,128)(2,1)S(1)}, bf16[4,128,128]{2,1,0:T(8,128)(2,1)S(1)}, u32[]{:S(2)}, u32[]{:S(2)}) %collective-permute-start.6) | collective-permute-done | bytes 131104 | tf_op jit(solution)/shard_map/ppermute | solution.py:25
  32.6 0.6 shard_map.202
  33.2 1.2 %collective-permute-start.9 = (bf16[4,128,128]{2,1,0:T(8,128)(2,1)S(1)}, bf16[4,128,128]{2,1,0:T(8,128)(2,1)S(1)}, u32[]{:S(2)}, u32[]{:S(2)}) collective-permute-start(bf16[4,128,128]{2,1,0:T(8,128)(2,1)S(1)} %get-tuple-element.79), channel_id=1, source_target_pairs={{0,8},{1,9},{2,10},{3,11},{4,12},{5,13},{6,14},{7,15},{8,0},{9,1},... | collective-permute-start | bytes 393224 | tf_op jit(solution)/shard_map/ppermute | solution.py:25
  34.4 1.7 %collective-permute-start.10 = (bf16[4,128,128]{2,1,0:T(8,128)(2,1)S(1)}, bf16[4,128,128]{2,1,0:T(8,128)(2,1)S(1)}, u32[]{:S(2)}, u32[]{:S(2)}) collective-permute-start(bf16[4,128,128]{2,1,0:T(8,128)(2,1)S(1)} %get-tuple-element.80), channel_id=1, source_target_pairs={{0,4},{1,5},{2,6},{3,7},{4,0},{5,1},{6,2},{7,3},{8,12},{9,13},{10,... | collective-permute-start | bytes 393224 | tf_op jit(solution)/shard_map/ppermute | solution.py:25
  36.1 0.5 collective-permute-start.11
  36.6 1.5 %shard_map.203 = (bf16[8,128,128]{2,1,0:T(8,128)(2,1)}, f32[8,128,128]{2,1,0:T(8,128)S(1)}, f32[8,128,256]{2,1,0:T(8,128)S(1)}, f32[256,128]{1,0:T(8,128)S(1)}, f32[1,128]{1,0:T(1,128)S(1)}) custom-call(s32[68]{0:T(128)S(4)} %get-tuple-element.59.table, bf16[8,4,128,128]{3,2,1,0:T(8,128)(2,1)S(1)} %get-tuple-element.60.values_t, ...), custom_call_target="tpu_custom_call" | custom-call | flops 268435456 | bytes 4194304 | tf_op jit(solution)/shard_map/pallas_call | solution.py:37
  38.1 2.3 %collective-permute-done.9.refs_0_ = bf16[4,128,128]{2,1,0:T(8,128)(2,1)S(1)} collective-permute-done((bf16[4,128,128]{2,1,0:T(8,128)(2,1)S(1)}, bf16[4,128,128]{2,1,0:T(8,128)(2,1)S(1)}, u32[]{:S(2)}, u32[]{:S(2)}) %collective-permute-start.9) | collective-permute-done | bytes 131104 | tf_op jit(solution)/shard_map/ppermute | solution.py:25
  40.4 0.2 collective-permute-done.10.refs_1_
  40.6 0.4 collective-permute-done.11.refs_2_
  41.0 1.0 %shard_map.204 = (bf16[8,128,256]{2,1,0:T(8,128)(2,1)S(1)}, bf16[4,200,128]{2,1,0:T(8,128)(2,1)S(1)}, f32[4,200,128]{2,1,0:T(8,128)S(1)}) custom-call(s32[68]{0:T(128)S(4)} %get-tuple-element.59.table, bf16[4,128,128]{2,1,0:T(8,128)(2,1)S(1)} %collective-permute-done.9.refs_0_, bf16[4,128,128]{2,1,0:T(8,128)(2,1)S(1)} %collective-permute-done.10.refs_1_, ...), custom_call_target="tpu_custom_call" | custom-call | flops 402653184 | bytes 6291456 | tf_op jit(solution)/shard_map/pallas_call | solution.py:37
  42.1 0.8 %shard_map.205 = bf16[8,128,256]{2,1,0:T(8,128)(2,1)} custom-call(bf16[8,128,256]{2,1,0:T(8,128)(2,1)S(1)} %get-tuple-element.90.value), custom_call_target="tpu_custom_call" | custom-call | bytes 1048576 | tf_op jit(solution)/shard_map/pallas_call | solution.py:37
  42.9 0.6 collective-permute-done.12.arrived
  43.6 0.4 collective-permute-start.13
  44.0 1.8 %collective-permute-start.14 = (bf16[200,128]{1,0:T(8,128)(2,1)S(1)}, bf16[200,128]{1,0:T(8,128)(2,1)S(1)}, u32[]{:S(2)}, u32[]{:S(2)}) collective-permute-start(bf16[200,128]{1,0:T(8,128)(2,1)S(1)} %get-tuple-element.96), channel_id=1, source_target_pairs={{0,8},{1,9},{2,10},{3,11},{4,12},{5,13},{6,14},{7,15},{8,0},{9,1},... | collective-permute-start | bytes 153608 | tf_op jit(solution)/shard_map/ppermute | solution.py:25
  45.8 2.2 %collective-permute-start.15 = (bf16[200,128]{1,0:T(8,128)(2,1)S(1)}, bf16[200,128]{1,0:T(8,128)(2,1)S(1)}, u32[]{:S(2)}, u32[]{:S(2)}) collective-permute-start(bf16[200,128]{1,0:T(8,128)(2,1)S(1)} %get-tuple-element.97), channel_id=1, source_target_pairs={{0,12},{1,13},{2,14},{3,15},{4,8},{5,9},{6,10},{7,11},{8,4},{9,5},... | collective-permute-start | bytes 153608 | tf_op jit(solution)/shard_map/ppermute | solution.py:25
  48.1 0.3 collective-permute-done.13.refs_0_
  48.3 1.2 %collective-permute-done.14.refs_1_ = bf16[200,128]{1,0:T(8,128)(2,1)S(1)} collective-permute-done((bf16[200,128]{1,0:T(8,128)(2,1)S(1)}, bf16[200,128]{1,0:T(8,128)(2,1)S(1)}, u32[]{:S(2)}, u32[]{:S(2)}) %collective-permute-start.14) | collective-permute-done | bytes 51232 | tf_op jit(solution)/shard_map/ppermute | solution.py:25
  49.6 2.2 %collective-permute-done.15.refs_2_ = bf16[200,128]{1,0:T(8,128)(2,1)S(1)} collective-permute-done((bf16[200,128]{1,0:T(8,128)(2,1)S(1)}, bf16[200,128]{1,0:T(8,128)(2,1)S(1)}, u32[]{:S(2)}, u32[]{:S(2)}) %collective-permute-start.15) | collective-permute-done | bytes 51232 | tf_op jit(solution)/shard_map/ppermute | solution.py:25
  51.9 0.6 collective-permute-start.16
  52.5 2.9 %collective-permute-done.17.refs_0_ = bf16[200,128]{1,0:T(8,128)(2,1)S(1)} collective-permute-done((bf16[200,128]{1,0:T(8,128)(2,1)S(1)}, bf16[200,128]{1,0:T(8,128)(2,1)S(1)}, u32[]{:S(2)}, u32[]{:S(2)}) %collective-permute-start.17) | collective-permute-done | bytes 51232 | tf_op jit(solution)/shard_map/ppermute | solution.py:25
  55.4 2.3 %collective-permute-start.23 = (bf16[200,128]{1,0:T(8,128)(2,1)S(1)}, bf16[200,128]{1,0:T(8,128)(2,1)S(1)}, u32[]{:S(2)}, u32[]{:S(2)}) collective-permute-start(bf16[200,128]{1,0:T(8,128)(2,1)S(1)} %shard_map.208.refs_0_), channel_id=1, source_target_pairs={{0,12},{1,13},{2,14},{3,15},{4,8},{5,9},{6,10},{7,11},{8,4},{9,5},... | collective-permute-start | bytes 153608 | tf_op jit(solution)/shard_map/ppermute | solution.py:25
  57.7 2.2 %collective-permute-start.19 = (bf16[200,128]{1,0:T(8,128)(2,1)S(1)}, bf16[200,128]{1,0:T(8,128)(2,1)S(1)}, u32[]{:S(2)}, u32[]{:S(2)}) collective-permute-start(bf16[200,128]{1,0:T(8,128)(2,1)S(1)} %shard_map.208.refs_0_), channel_id=1, source_target_pairs={{0,8},{1,9},{2,10},{3,11},{4,12},{5,13},{6,14},{7,15},{8,0},{9,1},... | collective-permute-start | bytes 153608 | tf_op jit(solution)/shard_map/ppermute | solution.py:25
  59.9 1.9 %collective-permute-done.23.refs_3_ = bf16[200,128]{1,0:T(8,128)(2,1)S(1)} collective-permute-done((bf16[200,128]{1,0:T(8,128)(2,1)S(1)}, bf16[200,128]{1,0:T(8,128)(2,1)S(1)}, u32[]{:S(2)}, u32[]{:S(2)}) %collective-permute-start.23) | collective-permute-done | bytes 51232 | tf_op jit(solution)/shard_map/ppermute | solution.py:25
  61.8 0.3 collective-permute-done.21.refs_2_
  62.1 0.3 collective-permute-start.22
  62.3 0.4 collective-permute-done.19.refs_1_
  62.7 0.8 %shard_map.209 = (f32[256,256]{1,0:T(8,128)}, f32[256,256]{1,0:T(8,128)}, f32[256,128]{1,0:T(8,128)}, f32[256,128]{1,0:T(8,128)}, f32[1,256]{1,0:T(1,128)}, /*index=5*/f32[1,128]{1,0:T(1,128)}) custom-call(bf16[200,128]{1,0:T(8,128)(2,1)S(1)} %shard_map.208.refs_0_, bf16[200,128]{1,0:T(8,128)(2,1)S(1)} %collective-permute-done.19.refs_1_, ...), custom_call_target="tpu_custom_call" | custom-call | bytes 614400 | tf_op jit(solution)/shard_map/pallas_call | solution.py:37
  63.6 0.4 collective-permute-done.20.refs_1_
  63.9 0.8 %shard_map.210 = (f32[256,256]{1,0:T(8,128)}, f32[256,256]{1,0:T(8,128)}, f32[256,128]{1,0:T(8,128)}, f32[256,128]{1,0:T(8,128)}, f32[1,256]{1,0:T(1,128)}, /*index=5*/f32[1,128]{1,0:T(1,128)}) custom-call(bf16[200,128]{1,0:T(8,128)(2,1)S(1)} %collective-permute-done.18.refs_0_, ...), custom_call_target="tpu_custom_call", output_to_operand_aliasing={{0}: (4, {}), {1}: (5, {}), {2}: (6, {}), {3}: (7, {}), {4}... | custom-call | bytes 614400 | tf_op jit(solution)/shard_map/pallas_call | solution.py:37
  (42 shorter events, 0.4 us)
Async XLA Ops:
  0.6 13.1 %copy-start = (bf16[8,4,128,128]{3,2,1,0:T(8,128)(2,1)S(1)}, bf16[8,4,128,128]{3,2,1,0:T(8,128)(2,1)}, u32[]{:S(2)}) copy-start(bf16[8,4,128,128]{3,2,1,0:T(8,128)(2,1)} %values.1) | copy-start | bytes 3145732
  0.6 8.3 %collective-permute-start.2 = (s32[3,1,4]{2,1,0:T(1,128)}, s32[3,1,4]{2,1,0:T(1,128)S(1)}, u32[]{:S(2)}, u32[]{:S(2)}) collective-permute-start(s32[3,1,4]{2,1,0:T(1,128)} %bitcast.25), channel_id=1, source_target_pairs={{0,2},{1,3},{2,0},{3,1},{4,6},{5,7},{6,4},{7,5},{8,10},{9,11},{10,... | collective-permute-start | bytes 152 | tf_op jit(solution)/shard_map/ppermute | solution.py:25
  3.6 5.3 %collective-permute-start.1 = (s32[3,1,4]{2,1,0:T(1,128)}, s32[3,1,4]{2,1,0:T(1,128)S(1)}, u32[]{:S(2)}, u32[]{:S(2)}) collective-permute-start(s32[3,1,4]{2,1,0:T(1,128)} %bitcast.26), channel_id=1, source_target_pairs={{0,4},{1,5},{2,6},{3,7},{4,0},{5,1},{6,2},{7,3},{8,12},{9,13},{10,... | collective-permute-start | bytes 152 | tf_op jit(solution)/shard_map/ppermute | solution.py:25
  5.2 4.7 %collective-permute-start = (s32[3,1,4]{2,1,0:T(1,128)}, s32[3,1,4]{2,1,0:T(1,128)S(1)}, u32[]{:S(2)}, u32[]{:S(2)}) collective-permute-start(s32[3,1,4]{2,1,0:T(1,128)} %bitcast.27), channel_id=1, source_target_pairs={{0,8},{1,9},{2,10},{3,11},{4,12},{5,13},{6,14},{7,15},{8,0},{9,1},... | collective-permute-start | bytes 152 | tf_op jit(solution)/shard_map/ppermute | solution.py:25
  7.8 1.0 %copy-start.3 = (bf16[1024,256]{1,0:T(8,128)(2,1)S(1)}, bf16[1024,256]{1,0:T(8,128)(2,1)}, u32[]{:S(2)}) copy-start(bf16[1024,256]{1,0:T(8,128)(2,1)} %param.14) | copy-start | bytes 1572868
  8.9 4.8 %copy-start.1 = (bf16[1,3,4,128,128]{4,3,2,1,0:T(8,128)(2,1)S(1)}, bf16[1,3,4,128,128]{4,3,2,1,0:T(8,128)(2,1)}, u32[]{:S(2)}) copy-start(bf16[1,3,4,128,128]{4,3,2,1,0:T(8,128)(2,1)} %param.21) | copy-start | bytes 1179652
  8.9 4.8 %copy-start.6 = (bf16[256,256]{1,0:T(8,128)(2,1)S(1)}, bf16[256,256]{1,0:T(8,128)(2,1)}, u32[]{:S(2)}) copy-start(bf16[256,256]{1,0:T(8,128)(2,1)} %refs_6_.3) | copy-start | bytes 393220
  9.9 3.8 %copy-start.10 = (f32[256]{0:T(256)S(1)}, f32[256]{0:T(256)}, u32[]{:S(2)}) copy-start(f32[256]{0:T(256)} %param.24) | copy-start | bytes 3076
  9.9 3.8 %copy-start.11 = (s32[1,3]{1,0:T(1,128)S(1)}, s32[1,3]{1,0:T(1,128)}, u32[]{:S(2)}) copy-start(s32[1,3]{1,0:T(1,128)} %count.1) | copy-start | bytes 40
  10.1 12.9 %collective-permute-start.3 = (bf16[4,128,256]{2,1,0:T(8,128)(2,1)S(1)}, bf16[4,128,256]{2,1,0:T(8,128)(2,1)S(1)}, u32[]{:S(2)}, u32[]{:S(2)}) collective-permute-start(bf16[4,128,256]{2,1,0:T(8,128)(2,1)S(1)} %get-tuple-element.61), channel_id=1, source_target_pairs={{0,8},{1,9},{2,10},{3,11},{4,12},{5,13},{6,14},{7,15},{8,0},{9,1},... | collective-permute-start | bytes 786440 | tf_op jit(solution)/shard_map/ppermute | solution.py:25
  12.7 11.6 %collective-permute-start.4 = (bf16[4,128,256]{2,1,0:T(8,128)(2,1)S(1)}, bf16[4,128,256]{2,1,0:T(8,128)(2,1)S(1)}, u32[]{:S(2)}, u32[]{:S(2)}) collective-permute-start(bf16[4,128,256]{2,1,0:T(8,128)(2,1)S(1)} %get-tuple-element.62), channel_id=1, source_target_pairs={{0,4},{1,5},{2,6},{3,7},{4,0},{5,1},{6,2},{7,3},{8,12},{9,13},{10,... | collective-permute-start | bytes 786440 | tf_op jit(solution)/shard_map/ppermute | solution.py:25
  13.2 11.1 %collective-permute-start.5 = (bf16[4,128,256]{2,1,0:T(8,128)(2,1)S(1)}, bf16[4,128,256]{2,1,0:T(8,128)(2,1)S(1)}, u32[]{:S(2)}, u32[]{:S(2)}) collective-permute-start(bf16[4,128,256]{2,1,0:T(8,128)(2,1)S(1)} %get-tuple-element.63), channel_id=1, source_target_pairs={{0,2},{1,3},{2,0},{3,1},{4,6},{5,7},{6,4},{7,5},{8,10},{9,11},{10,... | collective-permute-start | bytes 786440 | tf_op jit(solution)/shard_map/ppermute | solution.py:25
  13.7 0.7 %copy-start.8 = (s32[8,4]{0,1:T(4,128)S(1)}, s32[8,4]{0,1:T(4,128)}, u32[]{:S(2)}) copy-start(s32[8,4]{0,1:T(4,128)} %param.16) | copy-start | bytes 388
  13.7 0.7 %copy-start.9 = (s32[1,3,4]{2,0,1:T(1,128)S(1)}, s32[1,3,4]{2,0,1:T(1,128)}, u32[]{:S(2)}) copy-start(s32[1,3,4]{2,0,1:T(1,128)} %param.19) | copy-start | bytes 148
  14.4 9.9 %copy-start.2 = (bf16[256,256]{1,0:T(8,128)(2,1)S(1)}, bf16[256,256]{1,0:T(8,128)(2,1)}, u32[]{:S(2)}) copy-start(bf16[256,256]{1,0:T(8,128)(2,1)} %w1_near.1) | copy-start | bytes 393220
  14.4 9.9 %copy-start.5 = (bf16[256,128]{1,0:T(8,128)(2,1)S(1)}, bf16[256,128]{1,0:T(8,128)(2,1)}, u32[]{:S(2)}) copy-start(bf16[256,128]{1,0:T(8,128)(2,1)} %refs_6_.5) | copy-start | bytes 196612
  24.3 3.4 %copy-start.4 = (bf16[256,128]{1,0:T(8,128)(2,1)S(1)}, bf16[256,128]{1,0:T(8,128)(2,1)}, u32[]{:S(2)}) copy-start(bf16[256,128]{1,0:T(8,128)(2,1)} %w2_self.3) | copy-start | bytes 196612
  25.3 7.3 %collective-permute-start.6 = (bf16[4,128,128]{2,1,0:T(8,128)(2,1)S(1)}, bf16[4,128,128]{2,1,0:T(8,128)(2,1)S(1)}, u32[]{:S(2)}, u32[]{:S(2)}) collective-permute-start(bf16[4,128,128]{2,1,0:T(8,128)(2,1)S(1)} %get-tuple-element.66), channel_id=1, source_target_pairs={{0,8},{1,9},{2,10},{3,11},{4,12},{5,13},{6,14},{7,15},{8,0},{9,1},... | collective-permute-start | bytes 393224 | tf_op jit(solution)/shard_map/ppermute | solution.py:25
  25.4 7.2 %collective-permute-start.7 = (bf16[4,128,128]{2,1,0:T(8,128)(2,1)S(1)}, bf16[4,128,128]{2,1,0:T(8,128)(2,1)S(1)}, u32[]{:S(2)}, u32[]{:S(2)}) collective-permute-start(bf16[4,128,128]{2,1,0:T(8,128)(2,1)S(1)} %get-tuple-element.67), channel_id=1, source_target_pairs={{0,4},{1,5},{2,6},{3,7},{4,0},{5,1},{6,2},{7,3},{8,12},{9,13},{10,... | collective-permute-start | bytes 393224 | tf_op jit(solution)/shard_map/ppermute | solution.py:25
  27.2 5.4 %collective-permute-start.8 = (bf16[4,128,128]{2,1,0:T(8,128)(2,1)S(1)}, bf16[4,128,128]{2,1,0:T(8,128)(2,1)S(1)}, u32[]{:S(2)}, u32[]{:S(2)}) collective-permute-start(bf16[4,128,128]{2,1,0:T(8,128)(2,1)S(1)} %get-tuple-element.68), channel_id=1, source_target_pairs={{0,2},{1,3},{2,0},{3,1},{4,6},{5,7},{6,4},{7,5},{8,10},{9,11},{10,... | collective-permute-start | bytes 393224 | tf_op jit(solution)/shard_map/ppermute | solution.py:25
  27.7 0.7 %copy-start.7 = (s32[1024]{0:T(1024)S(1)}, s32[1024]{0:T(1024)}, u32[]{:S(2)}) copy-start(s32[1024]{0:T(1024)} %param.15) | copy-start | bytes 12292
  27.7 0.7 %copy-start.12 = (f32[128]{0:T(128)S(1)}, f32[128]{0:T(128)}, u32[]{:S(2)}) copy-start(f32[128]{0:T(128)} %param.27) | copy-start | bytes 1540
  33.2 7.2 %collective-permute-start.9 = (bf16[4,128,128]{2,1,0:T(8,128)(2,1)S(1)}, bf16[4,128,128]{2,1,0:T(8,128)(2,1)S(1)}, u32[]{:S(2)}, u32[]{:S(2)}) collective-permute-start(bf16[4,128,128]{2,1,0:T(8,128)(2,1)S(1)} %get-tuple-element.79), channel_id=1, source_target_pairs={{0,8},{1,9},{2,10},{3,11},{4,12},{5,13},{6,14},{7,15},{8,0},{9,1},... | collective-permute-start | bytes 393224 | tf_op jit(solution)/shard_map/ppermute | solution.py:25
  34.4 6.3 %collective-permute-start.10 = (bf16[4,128,128]{2,1,0:T(8,128)(2,1)S(1)}, bf16[4,128,128]{2,1,0:T(8,128)(2,1)S(1)}, u32[]{:S(2)}, u32[]{:S(2)}) collective-permute-start(bf16[4,128,128]{2,1,0:T(8,128)(2,1)S(1)} %get-tuple-element.80), channel_id=1, source_target_pairs={{0,4},{1,5},{2,6},{3,7},{4,0},{5,1},{6,2},{7,3},{8,12},{9,13},{10,... | collective-permute-start | bytes 393224 | tf_op jit(solution)/shard_map/ppermute | solution.py:25
  36.1 5.0 %collective-permute-start.11 = (bf16[4,128,128]{2,1,0:T(8,128)(2,1)S(1)}, bf16[4,128,128]{2,1,0:T(8,128)(2,1)S(1)}, u32[]{:S(2)}, u32[]{:S(2)}) collective-permute-start(bf16[4,128,128]{2,1,0:T(8,128)(2,1)S(1)} %get-tuple-element.81), channel_id=1, source_target_pairs={{0,2},{1,3},{2,0},{3,1},{4,6},{5,7},{6,4},{7,5},{8,10},{9,11},{10,... | collective-permute-start | bytes 393224 | tf_op jit(solution)/shard_map/ppermute | solution.py:25
  42.0 1.5 %collective-permute-start.12 = (bf16[4,200,128]{2,1,0:T(8,128)(2,1)S(1)}, bf16[4,200,128]{2,1,0:T(8,128)(2,1)S(1)}, u32[]{:S(2)}, u32[]{:S(2)}) collective-permute-start(bf16[4,200,128]{2,1,0:T(8,128)(2,1)S(1)} %get-tuple-element.89), channel_id=1, source_target_pairs={{0,1},{1,0},{2,3},{3,2},{4,5},{5,4},{6,7},{7,6},{8,9},{9,8},{10,11... | collective-permute-start | bytes 614408 | tf_op jit(solution)/shard_map/ppermute | solution.py:25
  43.6 4.7 %collective-permute-start.13 = (bf16[200,128]{1,0:T(8,128)(2,1)S(1)}, bf16[200,128]{1,0:T(8,128)(2,1)S(1)}, u32[]{:S(2)}, u32[]{:S(2)}) collective-permute-start(bf16[200,128]{1,0:T(8,128)(2,1)S(1)} %get-tuple-element.95), channel_id=1, source_target_pairs={{0,4},{1,5},{2,6},{3,7},{4,0},{5,1},{6,2},{7,3},{8,12},{9,13},{10,... | collective-permute-start | bytes 153608 | tf_op jit(solution)/shard_map/ppermute | solution.py:25
  44.0 5.6 %collective-permute-start.14 = (bf16[200,128]{1,0:T(8,128)(2,1)S(1)}, bf16[200,128]{1,0:T(8,128)(2,1)S(1)}, u32[]{:S(2)}, u32[]{:S(2)}) collective-permute-start(bf16[200,128]{1,0:T(8,128)(2,1)S(1)} %get-tuple-element.96), channel_id=1, source_target_pairs={{0,8},{1,9},{2,10},{3,11},{4,12},{5,13},{6,14},{7,15},{8,0},{9,1},... | collective-permute-start | bytes 153608 | tf_op jit(solution)/shard_map/ppermute | solution.py:25
  45.8 5.9 %collective-permute-start.15 = (bf16[200,128]{1,0:T(8,128)(2,1)S(1)}, bf16[200,128]{1,0:T(8,128)(2,1)S(1)}, u32[]{:S(2)}, u32[]{:S(2)}) collective-permute-start(bf16[200,128]{1,0:T(8,128)(2,1)S(1)} %get-tuple-element.97), channel_id=1, source_target_pairs={{0,12},{1,13},{2,14},{3,15},{4,8},{5,9},{6,10},{7,11},{8,4},{9,5},... | collective-permute-start | bytes 153608 | tf_op jit(solution)/shard_map/ppermute | solution.py:25
  51.8 3.6 %collective-permute-start.17 = (bf16[200,128]{1,0:T(8,128)(2,1)S(1)}, bf16[200,128]{1,0:T(8,128)(2,1)S(1)}, u32[]{:S(2)}, u32[]{:S(2)}) collective-permute-start(bf16[200,128]{1,0:T(8,128)(2,1)S(1)} %shard_map.207), channel_id=1, source_target_pairs={{0,3},{1,2},{2,1},{3,0},{4,7},{5,6},{6,5},{7,4},{8,11},{9,10},{10,... | collective-permute-start | bytes 153608 | tf_op jit(solution)/shard_map/ppermute | solution.py:25
  51.9 3.5 %collective-permute-start.16 = (bf16[200,128]{1,0:T(8,128)(2,1)S(1)}, bf16[200,128]{1,0:T(8,128)(2,1)S(1)}, u32[]{:S(2)}, u32[]{:S(2)}) collective-permute-start(bf16[200,128]{1,0:T(8,128)(2,1)S(1)} %shard_map.207), channel_id=1, source_target_pairs={{0,1},{1,0},{2,3},{3,2},{4,5},{5,4},{6,7},{7,6},{8,9},{9,8},{10,11... | collective-permute-start | bytes 153608 | tf_op jit(solution)/shard_map/ppermute | solution.py:25
  55.4 6.4 %collective-permute-start.23 = (bf16[200,128]{1,0:T(8,128)(2,1)S(1)}, bf16[200,128]{1,0:T(8,128)(2,1)S(1)}, u32[]{:S(2)}, u32[]{:S(2)}) collective-permute-start(bf16[200,128]{1,0:T(8,128)(2,1)S(1)} %shard_map.208.refs_0_), channel_id=1, source_target_pairs={{0,12},{1,13},{2,14},{3,15},{4,8},{5,9},{6,10},{7,11},{8,4},{9,5},... | collective-permute-start | bytes 153608 | tf_op jit(solution)/shard_map/ppermute | solution.py:25
  57.7 4.4 %collective-permute-start.21 = (bf16[200,128]{1,0:T(8,128)(2,1)S(1)}, bf16[200,128]{1,0:T(8,128)(2,1)S(1)}, u32[]{:S(2)}, u32[]{:S(2)}) collective-permute-start(bf16[200,128]{1,0:T(8,128)(2,1)S(1)} %shard_map.208.refs_0_), channel_id=1, source_target_pairs={{0,4},{1,5},{2,6},{3,7},{4,0},{5,1},{6,2},{7,3},{8,12},{9,13},{10,... | collective-permute-start | bytes 153608 | tf_op jit(solution)/shard_map/ppermute | solution.py:25
  57.7 5.0 %collective-permute-start.19 = (bf16[200,128]{1,0:T(8,128)(2,1)S(1)}, bf16[200,128]{1,0:T(8,128)(2,1)S(1)}, u32[]{:S(2)}, u32[]{:S(2)}) collective-permute-start(bf16[200,128]{1,0:T(8,128)(2,1)S(1)} %shard_map.208.refs_0_), channel_id=1, source_target_pairs={{0,8},{1,9},{2,10},{3,11},{4,12},{5,13},{6,14},{7,15},{8,0},{9,1},... | collective-permute-start | bytes 153608 | tf_op jit(solution)/shard_map/ppermute | solution.py:25
  59.9 3.7 %collective-permute-start.18 = (bf16[200,128]{1,0:T(8,128)(2,1)S(1)}, bf16[200,128]{1,0:T(8,128)(2,1)S(1)}, u32[]{:S(2)}, u32[]{:S(2)}) collective-permute-start(bf16[200,128]{1,0:T(8,128)(2,1)S(1)} %shard_map.208.refs_0_), channel_id=1, source_target_pairs={{0,1},{1,0},{2,3},{3,2},{4,5},{5,4},{6,7},{7,6},{8,9},{9,8},{10,11... | collective-permute-start | bytes 153608 | tf_op jit(solution)/shard_map/ppermute | solution.py:25
  61.8 1.7 %collective-permute-start.24 = (bf16[200,128]{1,0:T(8,128)(2,1)S(1)}, bf16[200,128]{1,0:T(8,128)(2,1)S(1)}, u32[]{:S(2)}, u32[]{:S(2)}) collective-permute-start(bf16[200,128]{1,0:T(8,128)(2,1)S(1)} %collective-permute-done.23.refs_3_), channel_id=1, source_target_pairs={{0,1},{1,0},{2,3},{3,2},{4,5},{5,4},{6,7},{7,6},{8,9},{9,8},{10,11... | collective-permute-start | bytes 153608 | tf_op jit(solution)/shard_map/ppermute | solution.py:25
  62.1 1.5 %collective-permute-start.22 = (bf16[200,128]{1,0:T(8,128)(2,1)S(1)}, bf16[200,128]{1,0:T(8,128)(2,1)S(1)}, u32[]{:S(2)}, u32[]{:S(2)}) collective-permute-start(bf16[200,128]{1,0:T(8,128)(2,1)S(1)} %collective-permute-done.21.refs_2_), channel_id=1, source_target_pairs={{0,1},{1,0},{2,3},{3,2},{4,5},{5,4},{6,7},{7,6},{8,9},{9,8},{10,11... | collective-permute-start | bytes 153608 | tf_op jit(solution)/shard_map/ppermute | solution.py:25
  62.7 1.2 %collective-permute-start.20 = (bf16[200,128]{1,0:T(8,128)(2,1)S(1)}, bf16[200,128]{1,0:T(8,128)(2,1)S(1)}, u32[]{:S(2)}, u32[]{:S(2)}) collective-permute-start(bf16[200,128]{1,0:T(8,128)(2,1)S(1)} %collective-permute-done.19.refs_1_), channel_id=1, source_target_pairs={{0,1},{1,0},{2,3},{3,2},{4,5},{5,4},{6,7},{7,6},{8,9},{9,8},{10,11... | collective-permute-start | bytes 153608 | tf_op jit(solution)/shard_map/ppermute | solution.py:25
